TPU v7x, 32 devices: a whole 2x2x4 slice. The times are simulated.
32 devices in a mesh: row: 8 (over y, x, core), col: 4 (over z).
Axes of the slice: x: 2, y: 2, z: 4, core: 2. Of those that a mesh axis runs over, the one named last changes fastest.
Arguments:
- field: bfloat16 [8, 1536, 2, 2, 512], P(None, 'row', None, None, 'col'), may hold values from -6 to 6
- coef: float32 [1536, 512], P('row', 'col'), may hold values from 0.3 to 3
- table: bfloat16 [8, 1024, 1536], P('row'), may hold values from -0.15625 to 0.15625
- order_ids: int32 [8], P('row'), may hold values from 0 to 1023, as said below
- inverses: bfloat16 [1024, 512, 512], P(('row', 'col')), may hold values from -0.25 to 0.25
- degree_owner: int32 [1024], replicated, may hold values from 0 to 1023, each once
Outputs:
- synthesized: bfloat16 [8, 1536, 2, 2, 512], P(None, 'row', None, None, 'col')
Inputs may be any that keep to these rules, and one draw needn't show every extreme that they name: `order_ids`: distinct orders; 0 and 1023 are always among them. `degree_owner`: every degree appears exactly once.
All inputs are finite; a program needn't handle non-finite values.
Results may differ from a plain program's by a relative error of at most 0.0064.
Values may be sent and summed in bfloat16 or wider, within the bound.
No kernel may reach another device: no remote copies, remote signals or barrier semaphores. Data moves between devices by JAX's collectives and lax.ppermute only.
A program may use at most 64 MiB of HBM per device.

v0:
```python
import jax
import jax.numpy as jnp
from jax import lax
from jax.sharding import PartitionSpec as P


def analyze(degree_table, order_id, columns, block_rows):
    degrees_all = degree_table.shape[0]

    def analyze_add_block(block_no, spectra):
        first_row = block_no * block_rows
        table_part = lax.dynamic_slice_in_dim(degree_table, first_row, block_rows, 0)
        product = jnp.dot(table_part, columns, preferred_element_type=jnp.float32)
        degree = first_row + lax.iota(jnp.int32, block_rows)
        product = jnp.where((degree >= order_id)[:, None], product, 0.0)
        return lax.dynamic_update_slice_in_dim(spectra, product.astype(jnp.bfloat16), first_row, 0)

    blank_rows = jnp.zeros((degrees_all, columns.shape[1]), jnp.bfloat16)
    return lax.fori_loop(
        order_id // block_rows, degrees_all // block_rows, analyze_add_block, blank_rows
    )


def synthesize(degree_table, order_id, coeffs, block_rows):
    degrees_all = degree_table.shape[0]

    def synthesize_add_block(block_no, running):
        first_row = block_no * block_rows
        table_part = lax.dynamic_slice_in_dim(degree_table, first_row, block_rows, 0)
        coeff_part = lax.dynamic_slice_in_dim(coeffs, first_row, block_rows, 0)
        return running + lax.dot_general(
            table_part, coeff_part, (((0,), (0,)), ((), ())), preferred_element_type=jnp.float32
        )

    zero_sum = jnp.zeros((degree_table.shape[1], coeffs.shape[1]), jnp.float32)
    return lax.fori_loop(
        order_id // block_rows, degrees_all // block_rows, synthesize_add_block, zero_sum
    ).astype(jnp.bfloat16)


def per_device(field, coef, table, order_ids, inverses, degree_owner):
    n_row = lax.axis_size("row")
    n_col = lax.axis_size("col")
    ord_dev = table.shape[0]
    degrees_all = table.shape[1]
    latitudes = table.shape[2]
    deg_dev = inverses.shape[0]
    members = field.shape[2]
    radii_dev = field.shape[4]
    block_rows = 128
    weighted = (field.astype(jnp.float32) * coef[None, :, None, None, :]).astype(jnp.bfloat16)
    arrived_all = lax.all_to_all(weighted, "row", split_axis=0, concat_axis=1, tiled=True)
    spectral = jnp.stack(
        [analyze(table[0], order_ids[0], arrived_all[0].reshape(latitudes, -1), block_rows)]
    )
    spectral = spectral.reshape(ord_dev, degrees_all, members, 2, radii_dev)
    positions = lax.iota(jnp.int32, degrees_all)
    listing = degree_owner.reshape(n_row, n_col, deg_dev).transpose(1, 0, 2).reshape(degrees_all)
    placed = jnp.take(spectral, listing, axis=1)
    owned_rows = lax.all_to_all(
        lax.all_to_all(placed, "col", split_axis=1, concat_axis=4, tiled=True),
        "row",
        split_axis=1,
        concat_axis=0,
        tiled=True,
    )
    solved = jnp.einsum(
        "kdfcs,drs->kdfcr", owned_rows, inverses, preferred_element_type=jnp.float32
    ).astype(jnp.bfloat16)
    returned = lax.all_to_all(
        lax.all_to_all(solved, "row", split_axis=0, concat_axis=1, tiled=True),
        "col",
        split_axis=4,
        concat_axis=1,
        tiled=True,
    )
    inverse_order = jnp.zeros((degrees_all,), jnp.int32).at[listing].set(positions)
    coeffs = jnp.take(returned, inverse_order, axis=1)
    outputs = jnp.stack(
        [synthesize(table[0], order_ids[0], coeffs[0].reshape(degrees_all, -1), block_rows)]
    )
    outputs = outputs.reshape(ord_dev, latitudes, members, 2, radii_dev)
    return lax.all_to_all(outputs, "row", split_axis=1, concat_axis=0, tiled=True)


def solution(mesh):
    in_specs = (
        P(None, "row", None, None, "col"),
        P("row", "col"),
        P("row", None, None),
        P("row"),
        P(("row", "col"), None, None),
        P(),
    )
    out_specs = P(None, "row", None, None, "col")
    return jax.shard_map(
        per_device, mesh=mesh, in_specs=in_specs, out_specs=out_specs, check_vma=False
    )
```

profile of v0, /device:TPU:0, one launch (start us, length us, event | category | flops | bytes accessed | tf_op | source)
XLA Modules:
  0.0 215.6 jit_solution(13871816395428627042)
XLA Ops:
  0.0 4.0 %multiply_convert_fusion = bf16[8,192,2,2,128]{4,3,2,1,0:T(2,128)(2,1)} fusion(bf16[8,192,2,2,128]{4,3,2,1,0:T(2,128)(2,1)} %param.12, f32[192,128]{1,0:T(8,128)} %param.13), kind=kLoop, calls=%fused_computation.15 | loop fusion | flops 2359296 | bytes 3244032 | tf_op jit(solution)/shard_map/convert_element_type | solution.py:51
  4.0 5.2 %all-to-all-start = ((bf16[8,192,2,2,128]{4,3,2,1,0:T(2,128)(2,1)}), bf16[8,192,2,2,128]{4,3,2,1,0:T(2,128)(2,1)S(1)}, u32[]{:S(2)}, u32[]{:S(2)}) async-start(bf16[8,192,2,2,128]{4,3,2,1,0:T(2,128)(2,1)} %multiply_convert_fusion), calls=%async_computation | async-start | bytes 3145728 | tf_op jit(solution)/shard_map/all_to_all | solution.py:52
  10.0 20.2 %all-to-all-done = bf16[8,192,2,2,128]{4,3,2,1,0:T(2,128)(2,1)S(1)} async-done(((bf16[8,192,2,2,128]{4,3,2,1,0:T(2,128)(2,1)}), bf16[8,192,2,2,128]{4,3,2,1,0:T(2,128)(2,1)S(1)}, u32[]{:S(2)}, u32[]{:S(2)}) %all-to-all-start) | async-done | bytes 1572896 | tf_op jit(solution)/shard_map/all_to_all | solution.py:52
  30.2 0.6 reshape_squeeze.6
  30.9 2.1 while.20
  30.9 0.7 add_compare_fusion.2
  31.6 1.4 fusion.29
  33.3 4.8 %gather_fusion = bf16[1024,2,2,128]{3,2,1,0:T(2,128)(2,1)S(1)} fusion(bf16[1024,2,2,128]{3,2,1,0:T(2,128)(2,1)S(1)} %reshape.101, s32[1024]{0:T(1024)S(1)} %fusion.17), kind=kCustom, calls=%fused_computation.clone | custom fusion | bytes 2101248 | tf_op jit(solution)/shard_map/jit(_take)/gather | solution.py:59
  38.1 3.8 %fusion.16 = bf16[1,1024,2,2,128]{4,3,2,0,1:T(2,128)(2,1)S(1)} fusion(bf16[1024,2,2,128]{3,2,1,0:T(2,128)(2,1)S(1)} %gather_fusion, pred[1024]{0:T(1024)(128)(4,1)S(1)} %compare_and_fusion.1), kind=kLoop, calls=%fused_computation.22 | loop fusion | flops 524288 | bytes 2098176 | tf_op jit(solution)/shard_map/jit(_take)/select_n | solution.py:59
  41.9 27.7 %all_to_all.81 = bf16[1,1024,2,2,128]{4,3,2,0,1:T(2,128)(2,1)S(1)} all-to-all(bf16[1,1024,2,2,128]{4,3,2,0,1:T(2,128)(2,1)S(1)} %fusion.16), channel_id=1, replica_groups=mesh['row'=8,'col'=4] {'col'}, dimensions={1} | all-to-all | bytes 2097152 | tf_op jit(solution)/shard_map/all_to_all | solution.py:61
  69.7 0.5 copy.50
  70.3 1.1 copy.51
  71.4 28.1 %all_to_all.82 = bf16[1,256,2,2,512]{4,3,2,0,1:T(2,128)(2,1)S(1)} all-to-all(bf16[1,256,2,2,512]{4,3,2,0,1:T(2,128)(2,1)S(1)} %copy.51), channel_id=1, replica_groups=mesh['row'=8,'col'=4] {'row'}, dimensions={1} | all-to-all | bytes 2097152 | tf_op jit(solution)/shard_map/all_to_all | solution.py:60
  99.5 10.6 %fusion.12 = bf16[8,32,2,2,512]{4,0,3,2,1:T(8,128)(2,1)S(1)} fusion(bf16[32,512,512]{2,1,0:T(8,128)(2,1)} %param.16, bf16[8,32,2,2,512]{4,3,2,1,0:T(2,128)(2,1)S(1)} %bitcast.48), kind=kOutput, calls=%fused_computation.19 | convolution fusion | flops 537395200 | bytes 18874368 | tf_op jit(solution)/shard_map/kdfcs,drs->kdfcr/dot_general | solution.py:67
  110.1 0.8 copy.54
  110.9 17.8 %all_to_all.83 = bf16[8,32,2,2,512]{4,3,2,1,0:T(2,128)(2,1)S(1)} all-to-all(bf16[8,32,2,2,512]{4,3,2,1,0:T(2,128)(2,1)S(1)} %copy.54), channel_id=1, replica_groups=mesh['row'=8,'col'=4] {'row'}, dimensions={0} | all-to-all | bytes 2097152 | tf_op jit(solution)/shard_map/all_to_all | solution.py:71
  128.7 3.8 %copy.56 = bf16[1,256,2,2,512]{1,3,2,0,4:T(2,128)(2,1)} copy(bf16[1,256,2,2,512]{4,3,2,1,0:T(2,128)(2,1)S(1)} %bitcast.52) | data formatting | bytes 2097152 | tf_op jit(solution)/shard_map/all_to_all | solution.py:71
  132.5 3.5 %all-to-all-start.4 = ((bf16[1,256,2,2,512]{1,3,2,0,4:T(2,128)(2,1)}), bf16[1,256,2,2,512]{1,3,2,0,4:T(2,128)(2,1)S(1)}, u32[]{:S(2)}, u32[]{:S(2)}) async-start(bf16[1,256,2,2,512]{1,3,2,0,4:T(2,128)(2,1)} %copy.56), calls=%async_computation.4 | async-start | bytes 2097152 | tf_op jit(solution)/shard_map/all_to_all | solution.py:70
  136.1 4.5 %scatter_custom_fusion = s32[1024]{0:T(1024)S(1)} fusion(s32[1024]{0:T(1024)S(1)} %bitcast.57, s32[1024]{0:T(1024)S(1)} %iota.8, s32[]{:T(128)} %constant.50.clone.1), kind=kCustom, calls=%fused_computation.30 | custom fusion | bytes 4100 | tf_op jit(solution)/shard_map/scatter | solution.py:77
  140.6 20.7 %all-to-all-done.4 = bf16[1,256,2,2,512]{1,3,2,0,4:T(2,128)(2,1)S(1)} async-done(((bf16[1,256,2,2,512]{1,3,2,0,4:T(2,128)(2,1)}), bf16[1,256,2,2,512]{1,3,2,0,4:T(2,128)(2,1)S(1)}, u32[]{:S(2)}, u32[]{:S(2)}) %all-to-all-start.4) | async-done | bytes 1048608 | tf_op jit(solution)/shard_map/all_to_all | solution.py:70
  161.5 0.7 copy.58
  162.1 1.1 copy.71
  163.2 4.8 %gather_fusion.1 = bf16[1024,2,2,128]{3,2,1,0:T(2,128)(2,1)S(1)} fusion(bf16[1024,2,2,128]{3,2,1,0:T(2,128)(2,1)S(1)} %bitcast.49, s32[1024]{0:T(1024)S(1)} %fusion.18), kind=kCustom, calls=%fused_computation.1.clone | custom fusion | bytes 2101248 | tf_op jit(solution)/shard_map/jit(_take)/gather | solution.py:78
  168.1 3.8 %broadcast_select_fusion = bf16[1,1024,2,2,128]{4,3,2,1,0:T(2,128)(2,1)S(1)} fusion(pred[1024]{0:T(1024)(128)(4,1)S(1)} %compare_and_fusion, bf16[1024,2,2,128]{3,2,1,0:T(2,128)(2,1)S(1)} %gather_fusion.1), kind=kLoop, calls=%fused_computation.16 | loop fusion | flops 524288 | bytes 2098176 | tf_op jit(solution)/shard_map/jit(_take)/select_n | solution.py:78
  171.9 2.5 %copy.60 = bf16[1,1024,2,2,128]{1,4,3,2,0:T(8,128)(2,1)} copy(bf16[1,1024,2,2,128]{4,3,2,1,0:T(2,128)(2,1)S(1)} %broadcast_select_fusion) | data formatting | bytes 2097152 | tf_op jit(solution)/shard_map/jit(_take)/select_n | solution.py:78
  174.4 0.4 broadcast_in_dim.30
  174.8 1.7 while.21
  174.8 1.6 convolution_add_fusion.2
  176.5 1.3 convert_element_type.22
  177.8 2.4 %reshape_stack.7 = bf16[1,1536,2,2,128]{4,3,2,0,1:T(2,128)(2,1)S(1)} reshape(bf16[1536,512]{1,0:T(8,128)(2,1)} %convert_element_type.22) | data formatting | bytes 3145728 | tf_op jit(solution)/shard_map/reshape;stack | solution.py:82
  180.2 34.3 %all_to_all.84 = bf16[1,1536,2,2,128]{4,3,2,0,1:T(2,128)(2,1)S(1)} all-to-all(bf16[1,1536,2,2,128]{4,3,2,0,1:T(2,128)(2,1)S(1)} %reshape_stack.7), channel_id=1, replica_groups=mesh['row'=8,'col'=4] {'row'}, dimensions={1} | all-to-all | bytes 3145728 | tf_op jit(solution)/shard_map/all_to_all | solution.py:83
  214.4 1.1 copy.87
  (16 shorter events, 0.9 us)
Async XLA Ops:
  0.0 9.8 %copy-start = (s32[1024]{0:T(1024)S(1)}, s32[1024]{0:T(1024)}, u32[]{:S(2)}) copy-start(s32[1024]{0:T(1024)} %param.17) | copy-start | bytes 12292
  4.0 26.2 %all-to-all-start = ((bf16[8,192,2,2,128]{4,3,2,1,0:T(2,128)(2,1)}), bf16[8,192,2,2,128]{4,3,2,1,0:T(2,128)(2,1)S(1)}, u32[]{:S(2)}, u32[]{:S(2)}) async-start(bf16[8,192,2,2,128]{4,3,2,1,0:T(2,128)(2,1)} %multiply_convert_fusion), calls=%async_computation | async-start | bytes 3145728 | tf_op jit(solution)/shard_map/all_to_all | solution.py:52
  132.5 28.8 %all-to-all-start.4 = ((bf16[1,256,2,2,512]{1,3,2,0,4:T(2,128)(2,1)}), bf16[1,256,2,2,512]{1,3,2,0,4:T(2,128)(2,1)S(1)}, u32[]{:S(2)}, u32[]{:S(2)}) async-start(bf16[1,256,2,2,512]{1,3,2,0,4:T(2,128)(2,1)} %copy.56), calls=%async_computation.4 | async-start | bytes 2097152 | tf_op jit(solution)/shard_map/all_to_all | solution.py:70
where the time goes:
time: 215 us; the launch traced here: 216 us
  blocking collectives  108 us (50%)
  waiting for transfers between devices  40.9 us (19%)
  local copies, waits for them, and re-layouts  30 us (14%)
  other arithmetic  13.7 us (6%)
  matrix products  13.6 us (6%)
  starting transfers between devices  8.69 us (4%)
    all_to_all x1, blocking collectives, per_device(): lax.all_to_all(outputs, 'row', split_axis=1, concat_axis=0, tiled=True)  34.3 us
    all_to_all x1, blocking collectives, per_device(): lax.all_to_all(lax.all_to_all(placed, 'col', split_axis=1, concat_axis=4,...  28.1 us
    all_to_all x1, blocking collectives, per_device(): lax.all_to_all(placed, 'col', split_axis=1, concat_axis=4, tiled=True)  27.7 us
    all_to_all x1, waiting for transfers between devices, per_device(): lax.all_to_all(lax.all_to_all(solved, 'row', split_axis=0, concat_axis=1,...  20.7 us
    all_to_all x1, waiting for transfers between devices, per_device(): lax.all_to_all(weighted, 'row', split_axis=0, concat_axis=1, tiled=True)  20.2 us
    all_to_all x1, blocking collectives, per_device(): lax.all_to_all(solved, 'row', split_axis=0, concat_axis=1, tiled=True)  17.8 us
    dot_general x1, matrix products, per_device(): jnp.einsum('kdfcs,drs->kdfcr', owned_rows, inverses, preferred_element_ty...  10.6 us
    all_to_all x1, starting transfers between devices, per_device(): lax.all_to_all(weighted, 'row', split_axis=0, concat_axis=1, tiled=True)  5.17 us
  transfers between devices with their start and end apart: 2, of which 2 were waited for; matrix products, arithmetic and copies ran while one was open for 2% of the time, Pallas kernels for 0%

commit v1 on v0

v1 whole, which is shorter than its diff:
```python
import functools

import jax
import jax.numpy as jnp
from jax import lax
from jax.experimental import pallas as pl
from jax.experimental.pallas import tpu as pltpu
from jax.sharding import PartitionSpec as P

LANES = 128
SUBLANES = 8


def solve_kernel(orders, shards, members, x_ref, inv_ref, y_ref, x32, y32):
    step = pl.program_id(0)
    per_step = inv_ref.shape[0]
    degrees = x_ref.shape[0] // (orders * shards)

    @pl.when(step == 0)
    def _():
        for m in range(members):
            x32[m] = x_ref[:, m * LANES : (m + 1) * LANES].astype(jnp.float32)

    for local in range(per_step):
        degree = step * per_step + local

        def rows(shard):
            return pl.ds(shard * degrees + degree, orders, stride=shards * degrees)

        x = jnp.concatenate(
            [
                jnp.concatenate([x32[m, rows(r), :] for r in range(shards)], axis=1)
                for m in range(members)
            ],
            axis=0,
        ).astype(jnp.bfloat16)
        y = lax.dot_general(
            x, inv_ref[local], (((1,), (1,)), ((), ())), preferred_element_type=jnp.float32
        )
        for m in range(members):
            for r in range(shards):
                y32[m, rows(r), :] = y[
                    m * orders : (m + 1) * orders, r * LANES : (r + 1) * LANES
                ]

    @pl.when(step == pl.num_programs(0) - 1)
    def _():
        for m in range(members):
            y_ref[:, m * LANES : (m + 1) * LANES] = y32[m].astype(jnp.bfloat16)


def solve(owned, inverses, orders, shards, members):
    blocks, degrees, columns = owned.shape
    radii = inverses.shape[1]
    if columns != members * LANES or orders != SUBLANES or degrees % 4:
        split = owned.reshape(orders, shards, degrees, members, radii // shards)
        solved = jnp.einsum(
            "kadms,dtas->kdmt",
            split,
            inverses.reshape(degrees, radii, shards, radii // shards),
            preferred_element_type=jnp.float32,
        ).astype(jnp.bfloat16)
        solved = solved.reshape(orders, degrees, members, shards, radii // shards)
        return solved.transpose(0, 3, 1, 2, 4).reshape(owned.shape)
    per_step = 4
    rows = blocks * degrees
    out = pl.pallas_call(
        functools.partial(solve_kernel, orders, shards, members),
        grid=(degrees // per_step,),
        out_shape=jax.ShapeDtypeStruct((rows, columns), jnp.bfloat16),
        in_specs=[
            pl.BlockSpec((rows, columns), lambda i: (0, 0)),
            pl.BlockSpec((per_step, radii, radii), lambda i: (i, 0, 0)),
        ],
        out_specs=pl.BlockSpec((rows, columns), lambda i: (0, 0)),
        scratch_shapes=[
            pltpu.VMEM((members, rows, LANES), jnp.float32),
            pltpu.VMEM((members, rows, LANES), jnp.float32),
        ],
        compiler_params=pltpu.CompilerParams(vmem_limit_bytes=40 * 1024 * 1024),
        cost_estimate=pl.CostEstimate(
            flops=2 * degrees * radii * radii * orders * members,
            bytes_accessed=inverses.size * 2 + 4 * rows * columns,
            transcendentals=0,
        ),
    )(owned.reshape(rows, columns), inverses)
    return out.reshape(owned.shape)


def per_device(field, coef, table, order_ids, inverses, degree_owner):
    both = ("row", "col")
    n_row = lax.axis_size("row")
    n_col = lax.axis_size("col")
    orders, latitudes_dev = field.shape[:2]
    members = field.shape[2] * field.shape[3]
    columns = members * field.shape[4]
    ord_dev, degrees_all, latitudes = table.shape
    deg_dev = inverses.shape[0]
    devices = n_row * n_col

    weighted = (field.astype(jnp.float32) * coef[None, :, None, None, :]).astype(jnp.bfloat16)
    weighted = weighted.reshape(n_row, ord_dev, latitudes_dev, columns)
    arrived = lax.all_to_all(weighted, "row", split_axis=0, concat_axis=0, tiled=True)
    arrived = arrived.swapaxes(0, 1).reshape(ord_dev, latitudes, columns)

    degrees = lax.iota(jnp.int32, degrees_all)
    chosen = (degree_owner[:, None] == degrees[None, :])[None] & (
        degrees[None, None, :] >= order_ids[:, None, None]
    )
    chosen = chosen.astype(jnp.bfloat16)
    placed_table = jnp.einsum(
        "kpl,klt->kpt", chosen, table, preferred_element_type=jnp.float32
    ).astype(jnp.bfloat16)
    turned_table = jnp.einsum(
        "klt,kpl->ktp", table, chosen, preferred_element_type=jnp.float32
    ).astype(jnp.bfloat16)

    spectral = jnp.einsum(
        "kpt,ktn->kpn", placed_table, arrived, preferred_element_type=jnp.float32
    ).astype(jnp.bfloat16)
    spectral = spectral.reshape(ord_dev, devices, deg_dev, columns).swapaxes(0, 1)
    owned = lax.all_to_all(spectral, both, split_axis=0, concat_axis=0, tiled=True)
    owned = owned.reshape(n_row, n_col, ord_dev, deg_dev, columns).swapaxes(1, 2)
    solved = solve(
        owned.reshape(orders * n_col, deg_dev, columns), inverses, orders, n_col, members
    )
    solved = solved.reshape(n_row, ord_dev, n_col, deg_dev, columns).swapaxes(1, 2)
    solved = solved.reshape(devices, ord_dev, deg_dev, columns)
    coeffs = lax.all_to_all(solved, both, split_axis=0, concat_axis=0, tiled=True)
    coeffs = coeffs.swapaxes(0, 1).reshape(ord_dev, degrees_all, columns)
    outputs = jnp.einsum(
        "ktp,kpn->ktn", turned_table, coeffs, preferred_element_type=jnp.float32
    ).astype(jnp.bfloat16)
    outputs = outputs.reshape(ord_dev, n_row, latitudes_dev, columns).swapaxes(0, 1)
    outputs = lax.all_to_all(outputs, "row", split_axis=0, concat_axis=0, tiled=True)
    return outputs.reshape(field.shape)


def solution(mesh):
    in_specs = (
        P(None, "row", None, None, "col"),
        P("row", "col"),
        P("row", None, None),
        P("row"),
        P(("row", "col"), None, None),
        P(),
    )
    out_specs = P(None, "row", None, None, "col")
    return jax.shard_map(
        per_device, mesh=mesh, in_specs=in_specs, out_specs=out_specs, check_vma=False
    )
```

time: 215 us -> 139 us (0.65)
  waiting for transfers between devices: 40.9 us -> 15.4 us
  blocking collectives: 108 us -> 83.5 us
  local copies, waits for them, and re-layouts: 30 us -> 7.15 us
  Pallas kernels: 0 us -> 11.9 us
  other arithmetic: 13.7 us -> 4.12 us
  starting transfers between devices: 8.69 us -> 5.17 us
  matrix products: 13.6 us -> 11 us
    all_to_all x2 -> x1, waiting for transfers between devices: 40.9 us -> 15.4 us  [per_device(): lax.all_to_all(weighted, 'row', split_axis=0, concat_axis=0, tiled=True)]
    all_to_all x4 -> x3, blocking collectives: 108 us -> 83.5 us  [the longest x1 29.3 us: per_device(): lax.all_to_all(spectral, both, split_axis=0, concat_axis=0, tiled=True)]
    pallas_call x0 -> x1, Pallas kernels: none -> 11.9 us  [solve(): pl.pallas_call(functools.partial(solve_kernel, orders, shards, members),...]
    gather x2 -> x0, local copies, waits for them, and re-layouts: 9.64 us -> none  [the longest x1 4.82 us: per_device(): coeffs = jnp.take(returned, inverse_order, axis=1)]
    select_n x3 -> x0, other arithmetic: 7.67 us -> none  [the longest x1 3.83 us: per_device(): placed = jnp.take(spectral, listing, axis=1)]
    all_to_all x7 -> x0, local copies, waits for them, and re-layouts: 7.43 us -> none  [the longest x1 3.77 us: per_device(): lax.all_to_all(solved, 'row', split_axis=0, concat_axis=1, tiled=True)]
    reshape x3 -> x2, local copies, waits for them, and re-layouts: 0.23 us -> 7.14 us  [the longest x1 3.65 us: per_device(): weighted = weighted.reshape(n_row, ord_dev, latitudes_dev, columns)]
    scatter x1 -> x0, local copies, waits for them, and re-layouts: 4.49 us -> none  [per_device(): jnp.zeros((degrees_all,), jnp.int32).at[listing].set(positions)]
  transfers between devices with their start and end apart: 2 -> 1, of which waited for: 2 -> 1; matrix products, arithmetic and copies ran while one was open for 2% -> 4% of each run, Pallas kernels for 0% -> 0%
where the time goes in v1:
time: 139 us
  blocking collectives  83.5 us (60%)
  waiting for transfers between devices  15.4 us (11%)
  Pallas kernels  11.9 us (9%)
  matrix products  11 us (8%)
  local copies, waits for them, and re-layouts  7.15 us (5%)
  starting transfers between devices  5.17 us (4%)
  other arithmetic  4.12 us (3%)
    all_to_all x1, blocking collectives, per_device(): lax.all_to_all(spectral, both, split_axis=0, concat_axis=0, tiled=True)  29.3 us
    all_to_all x1, blocking collectives, per_device(): lax.all_to_all(solved, both, split_axis=0, concat_axis=0, tiled=True)  29.3 us
    all_to_all x1, blocking collectives, per_device(): lax.all_to_all(outputs, 'row', split_axis=0, concat_axis=0, tiled=True)  24.8 us
    all_to_all x1, waiting for transfers between devices, per_device(): lax.all_to_all(weighted, 'row', split_axis=0, concat_axis=0, tiled=True)  15.4 us
    pallas_call x1, Pallas kernels, solve(): pl.pallas_call(functools.partial(solve_kernel, orders, shards, members),...  11.9 us
    all_to_all x1, starting transfers between devices, per_device(): lax.all_to_all(weighted, 'row', split_axis=0, concat_axis=0, tiled=True)  5.17 us
    dot_general x1, matrix products, per_device(): jnp.einsum('klt,kpl->ktp', table, chosen, preferred_element_type=jnp.floa...  5.01 us
    dot_general x1, matrix products, per_device(): jnp.einsum('kpt,ktn->kpn', placed_table, arrived, preferred_element_type=...  4.13 us
  transfers between devices with their start and end apart: 1, of which 1 were waited for; matrix products, arithmetic and copies ran while one was open for 4% of the time, Pallas kernels for 0%

profile of v1, /device:TPU:0, one launch (start us, length us, event | category | flops | bytes accessed | tf_op | source)
XLA Modules:
  0.0 139.0 jit_solution(8404220885907166874)
XLA Ops:
  0.0 0.0 copy-start
  0.0 4.1 %multiply_convert_fusion = bf16[8,192,2,2,128]{4,3,2,1,0:T(2,128)(2,1)} fusion(bf16[8,192,2,2,128]{4,3,2,1,0:T(2,128)(2,1)} %param.6, f32[192,128]{1,0:T(8,128)} %param.7), kind=kLoop, calls=%fused_computation.5 | loop fusion | flops 2359296 | bytes 3244032 | tf_op jit(solution)/shard_map/convert_element_type | solution.py:101
  4.1 0.0 copy-start.1
  4.1 3.6 %reshape.83 = bf16[8,1,192,512]{3,2,1,0:T(8,128)(2,1)} reshape(bf16[8,192,2,2,128]{4,3,2,1,0:T(2,128)(2,1)} %multiply_convert_fusion) | data formatting | bytes 3145728 | tf_op jit(solution)/shard_map/reshape | solution.py:102
  7.8 5.2 %all-to-all-start = ((bf16[8,1,192,512]{3,2,1,0:T(8,128)(2,1)}), bf16[8,1,192,512]{3,2,1,0:T(8,128)(2,1)}, u32[]{:S(2)}, u32[]{:S(2)}) async-start(bf16[8,1,192,512]{3,2,1,0:T(8,128)(2,1)} %reshape.83), calls=%async_computation | async-start | bytes 3145728 | tf_op jit(solution)/shard_map/all_to_all | solution.py:103
  13.6 0.0 copy-done
  13.6 0.0 copy-done.1
  13.6 5.0 %fusion.3 = bf16[1024,1536]{1,0:T(8,128)(2,1)} fusion(bf16[1,1024,1536]{2,1,0:T(8,128)(2,1)S(1)} %copy-done, s32[1024]{0:T(1024)S(1)} %copy-done.1, pred[1024]{0:T(1024)(128)(4,1)S(1)} %iota_compare_fusion.1), kind=kOutput, calls=%fused_computation.3 | convolution fusion | flops 3224895488 | bytes 6296576 | tf_op jit(solution)/shard_map/klt,kpl->ktp/dot_general | solution.py:114
  18.6 15.4 %all-to-all-done = bf16[8,1,192,512]{3,2,1,0:T(8,128)(2,1)} async-done(((bf16[8,1,192,512]{3,2,1,0:T(8,128)(2,1)}), bf16[8,1,192,512]{3,2,1,0:T(8,128)(2,1)}, u32[]{:S(2)}, u32[]{:S(2)}) %all-to-all-start) | async-done | bytes 1572896 | tf_op jit(solution)/shard_map/all_to_all | solution.py:103
  34.1 4.1 %convolution_convert_fusion.1 = bf16[1024,512]{1,0:T(8,128)(2,1)S(1)} fusion(bf16[1024,1536]{1,0:T(8,128)(2,1)} %fusion.3, bf16[1536,512]{1,0:T(8,128)(2,1)} %bitcast.2), kind=kOutput, calls=%fused_computation.9 | convolution fusion | flops 1611137024 | bytes 5767168 | tf_op jit(solution)/shard_map/kpt,ktn->kpn/dot_general | solution.py:118
  38.2 29.3 %all_to_all.20 = bf16[32,1,32,512]{3,2,1,0:T(8,128)(2,1)S(1)} all-to-all(bf16[32,1,32,512]{3,2,1,0:T(8,128)(2,1)S(1)} %bitcast.27), channel_id=1, replica_groups=mesh['row'=8,'col'=4] {'row','col'}, dimensions={0} | all-to-all | bytes 2097152 | tf_op jit(solution)/shard_map/all_to_all | solution.py:122
  67.6 0.0 copy-start.2
  67.6 11.9 %shard_map.64 = bf16[1024,512]{1,0:T(8,128)(2,1)S(1)} custom-call(bf16[1024,512]{1,0:T(8,128)(2,1)S(1)} %bitcast.23, bf16[32,512,512]{2,1,0:T(8,128)(2,1)} %inv_ref.1), custom_call_target="tpu_custom_call" | custom-call | flops 536870912 | bytes 18874368 | tf_op jit(solution)/shard_map/pallas_call | solution.py:67
  79.5 29.3 %all_to_all.21 = bf16[32,1,32,512]{3,2,1,0:T(8,128)(2,1)S(1)} all-to-all(bf16[32,1,32,512]{3,2,1,0:T(8,128)(2,1)S(1)} %bitcast.24), channel_id=1, replica_groups=mesh['row'=8,'col'=4] {'row','col'}, dimensions={0} | all-to-all | bytes 2097152 | tf_op jit(solution)/shard_map/all_to_all | solution.py:129
  108.8 0.0 copy-done.2
  108.8 1.8 %convolution_convert_fusion = bf16[1536,512]{1,0:T(8,128)(2,1)S(1)} fusion(bf16[1024,1536]{1,0:T(8,128)(2,1)S(1)} %copy-done.2, bf16[1024,512]{1,0:T(8,128)(2,1)S(1)} %bitcast.26), kind=kOutput, calls=%fused_computation.6 | convolution fusion | flops 1611399168 | bytes 5767168 | tf_op jit(solution)/shard_map/ktp,kpn->ktn/dot_general | solution.py:131
  110.7 24.8 %all_to_all.22 = bf16[8,1,192,512]{3,2,1,0:T(8,128)(2,1)} all-to-all(bf16[8,1,192,512]{3,2,1,0:T(8,128)(2,1)S(1)} %bitcast.25), channel_id=1, replica_groups=mesh['row'=8,'col'=4] {'row'}, dimensions={0} | all-to-all | bytes 3145728 | tf_op jit(solution)/shard_map/all_to_all | solution.py:135
  135.5 3.5 %reshape.86 = bf16[8,192,2,2,128]{4,3,2,1,0:T(2,128)(2,1)} reshape(bf16[8,1,192,512]{3,2,1,0:T(8,128)(2,1)} %all_to_all.22) | data formatting | bytes 3145728 | tf_op jit(solution)/shard_map/reshape | solution.py:136
  (1 shorter events, 0.0 us)
Async XLA Ops:
  0.0 13.6 %copy-start = (bf16[1,1024,1536]{2,1,0:T(8,128)(2,1)S(1)}, bf16[1,1024,1536]{2,1,0:T(8,128)(2,1)}, u32[]{:S(2)}) copy-start(bf16[1,1024,1536]{2,1,0:T(8,128)(2,1)} %param.8) | copy-start | bytes 9437188
  4.1 9.5 %copy-start.1 = (s32[1024]{0:T(1024)S(1)}, s32[1024]{0:T(1024)}, u32[]{:S(2)}) copy-start(s32[1024]{0:T(1024)} %param.11) | copy-start | bytes 12292
  7.8 26.3 %all-to-all-start = ((bf16[8,1,192,512]{3,2,1,0:T(8,128)(2,1)}), bf16[8,1,192,512]{3,2,1,0:T(8,128)(2,1)}, u32[]{:S(2)}, u32[]{:S(2)}) async-start(bf16[8,1,192,512]{3,2,1,0:T(8,128)(2,1)} %reshape.83), calls=%async_computation | async-start | bytes 3145728 | tf_op jit(solution)/shard_map/all_to_all | solution.py:103
  67.6 41.3 %copy-start.2 = (bf16[1024,1536]{1,0:T(8,128)(2,1)S(1)}, bf16[1024,1536]{1,0:T(8,128)(2,1)}, u32[]{:S(2)}) copy-start(bf16[1024,1536]{1,0:T(8,128)(2,1)} %fusion.3) | copy-start | bytes 9437188

commit v2 on v1

v2 whole, which is shorter than its diff:
```python
import functools

import jax
import jax.numpy as jnp
from jax import lax
from jax.experimental import pallas as pl
from jax.experimental.pallas import tpu as pltpu
from jax.sharding import PartitionSpec as P

LANES = 128
SUBLANES = 8
UNROLL = 4
PREPARE_FLOPS = 5 * 10**9
MIB = 1024 * 1024
BF16 = jnp.bfloat16
F32 = jnp.float32
VMEM = pl.BlockSpec(memory_space=pltpu.VMEM)
SMEM = pl.BlockSpec(memory_space=pltpu.SMEM)
HBM = pl.BlockSpec(memory_space=pltpu.HBM)
ANY = pl.BlockSpec(memory_space=pl.ANY)


def dot(a, b):
    return jnp.dot(a, b, preferred_element_type=F32)


def params(mib):
    return pltpu.CompilerParams(vmem_limit_bytes=mib * MIB)


def in_hbm(array):
    return pltpu.with_memory_space_constraint(array, pltpu.HBM)


def cost(flops, moved):
    return pl.CostEstimate(flops=flops, bytes_accessed=moved, transcendentals=0)


def start(*copies):
    for copy in copies:
        copy.start()


def wait(*copies):
    for copy in copies:
        copy.wait()


def tiles(rows, count):
    return [pl.ds(i * (rows // count), rows // count) for i in range(count)]


def fetches(source, target, sems):
    parts = tiles(source.shape[0], sems.shape[0])
    copies = [
        pltpu.make_async_copy(source.at[part], target.at[part], sems.at[i])
        for i, part in enumerate(parts)
    ]
    return list(zip(parts, copies))


def weigh_kernel(members, x_hbm, coef_hbm, out_hbm, x16, x32, y16, coef, coef_sem, in_sems, out_sems):
    orders = in_sems.shape[0]
    lats = coef.shape[0]
    coef_copy = pltpu.make_async_copy(coef_hbm, coef, coef_sem)
    coef_copy.start()
    parts = fetches(x_hbm, x16, in_sems)
    start(*[copy for _, copy in parts])
    coef_copy.wait()
    stores = []
    for k, (rows, copy) in enumerate(parts):
        copy.wait()
        slot = k % 2
        x32[slot] = x16[rows, :].astype(F32)
        for m in range(members):
            part = x32[slot, pl.ds(m, lats, stride=members), :]
            y16[k, :, m * LANES : (m + 1) * LANES] = (part * coef[...]).astype(BF16)
        stores.append(pltpu.make_async_copy(y16.at[k], out_hbm.at[k], out_sems.at[k]))
        stores[-1].start()
    wait(*stores)


def weigh(field, coef):
    orders, lats, groups, parts, _ = field.shape
    members = groups * parts
    block = lats * members
    shape = (orders, lats, members * LANES)
    return pl.pallas_call(
        functools.partial(weigh_kernel, members),
        out_shape=pltpu.HBM(shape, BF16),
        in_specs=[HBM, HBM],
        out_specs=HBM,
        scratch_shapes=[
            pltpu.VMEM((orders * block, LANES), BF16),
            pltpu.VMEM((2, block, LANES), F32),
            pltpu.VMEM(shape, BF16),
            pltpu.VMEM(coef.shape, F32),
            pltpu.SemaphoreType.DMA,
            pltpu.SemaphoreType.DMA((orders,)),
            pltpu.SemaphoreType.DMA((orders,)),
        ],
        compiler_params=params(16),
        cost_estimate=cost(field.size, field.size * 4),
    )(in_hbm(field.reshape(orders * block, LANES)), in_hbm(coef))


def analyse_kernel(table_hbm, chosen_hbm, fields, out_ref, w, s, table, chosen, sems, table_sems, chosen_sems):
    field_parts = fetches(fields, w, sems)
    start(*[copy for _, copy in field_parts])
    table_parts = fetches(table_hbm, table, table_sems)
    start(*[copy for _, copy in table_parts])
    chosen_parts = fetches(chosen_hbm, chosen, chosen_sems)
    start(*[copy for _, copy in chosen_parts])
    wait(*[copy for _, copy in field_parts])
    for rows, copy in table_parts:
        copy.wait()
        s[rows, :] = dot(table[rows, :], w[...]).astype(BF16)
    for rows, copy in chosen_parts:
        copy.wait()
        out_ref[rows, :] = dot(chosen[rows, :], s[...]).astype(BF16)


def analyse(table, chosen, fields):
    rows, lats = table.shape
    columns = fields.shape[1]
    return pl.pallas_call(
        analyse_kernel,
        out_shape=jax.ShapeDtypeStruct((rows, columns), BF16),
        in_specs=[HBM, HBM, ANY],
        out_specs=VMEM,
        scratch_shapes=[
            pltpu.VMEM((lats, columns), BF16),
            pltpu.VMEM((rows, columns), BF16),
            pltpu.VMEM(table.shape, BF16),
            pltpu.VMEM(chosen.shape, BF16),
            pltpu.SemaphoreType.DMA((8,)),
            pltpu.SemaphoreType.DMA((4,)),
            pltpu.SemaphoreType.DMA((4,)),
        ],
        compiler_params=params(20),
        cost_estimate=cost(2 * rows * (lats + rows) * columns, 2 * rows * (lats + rows)),
    )(in_hbm(table), in_hbm(chosen), fields)


def prepare_kernel(order_ref, table_hbm, owner_ref, *rest):
    turned_hbm, chosen_hbm, back_hbm, table, turned, chosen, back, table_sem, sems = rest
    table_copy = pltpu.make_async_copy(table_hbm, table, table_sem)
    table_copy.start()
    degrees, lats = table.shape
    order = order_ref[0]
    owner = jnp.broadcast_to(owner_ref[...], (LANES, degrees))
    across = owner.T
    for block in range(degrees // LANES):
        part = slice(block * LANES, (block + 1) * LANES)
        degree = lax.broadcasted_iota(jnp.int32, (degrees, LANES), 1) + block * LANES
        chosen[:, part] = ((across == degree) & (degree >= order)).astype(F32).astype(BF16)
        degree = lax.broadcasted_iota(jnp.int32, (LANES, degrees), 0) + block * LANES
        back[part, :] = ((owner == degree) & (degree >= order)).astype(F32).astype(BF16)
    chosen_copy = pltpu.make_async_copy(chosen, chosen_hbm, sems.at[0])
    back_copy = pltpu.make_async_copy(back, back_hbm, sems.at[1])
    start(chosen_copy, back_copy)
    table_copy.wait()

    @pl.loop(0, lats // LANES)
    def _(i):
        part = pl.ds(pl.multiple_of(i * LANES, LANES), LANES)
        turned[part, :] = table[:, part].T

    turned_copy = pltpu.make_async_copy(turned, turned_hbm, sems.at[2])
    turned_copy.start()
    wait(chosen_copy, back_copy, turned_copy)


def prepare(order_ids, table, degree_owner):
    degrees, lats = table.shape
    shapes = [(lats, degrees), (degrees, degrees), (degrees, degrees)]
    return pl.pallas_call(
        prepare_kernel,
        out_shape=[pltpu.HBM(shape, BF16) for shape in shapes],
        in_specs=[SMEM, HBM, VMEM],
        out_specs=[HBM] * 3,
        scratch_shapes=[pltpu.VMEM(shape, BF16) for shape in [table.shape] + shapes]
        + [pltpu.SemaphoreType.DMA, pltpu.SemaphoreType.DMA((3,))],
        compiler_params=params(20),
        cost_estimate=cost(PREPARE_FLOPS, 4 * table.size),
    )(order_ids, in_hbm(table), degree_owner.reshape(1, degrees))


def solve_kernel(orders, shards, members, x_ref, inv_hbm, y_ref, x32, y32, inv, sems):
    degrees = inv.shape[0]
    chunks = sems.shape[0]
    parts = fetches(inv_hbm, inv, sems)
    start(*[copy for _, copy in parts])
    for m in range(members):
        x32[m] = x_ref[:, m * LANES : (m + 1) * LANES].astype(F32)

    @pl.loop(0, chunks)
    def _(i):
        each = degrees // chunks
        rows = pl.ds(i * each, each)
        pltpu.make_async_copy(inv_hbm.at[rows], inv.at[rows], sems.at[i]).wait()
        for local in range(each):
            degree = i * each + local

            def rows(shard):
                return pl.ds(shard * degrees + degree, orders, stride=shards * degrees)

            x = jnp.concatenate(
                [
                    jnp.concatenate([x32[m, rows(r), :] for r in range(shards)], axis=1)
                    for m in range(members)
                ],
                axis=0,
            ).astype(BF16)
            y = lax.dot_general(
                x, inv[degree], (((1,), (1,)), ((), ())), preferred_element_type=F32
            )
            for m in range(members):
                for r in range(shards):
                    y32[m, rows(r), :] = y[
                        m * orders : (m + 1) * orders, r * LANES : (r + 1) * LANES
                    ]

    for m in range(members):
        y_ref[:, m * LANES : (m + 1) * LANES] = y32[m].astype(BF16)


def solve(owned, inverses, orders, shards, members):
    rows, columns = owned.shape
    degrees, radii, _ = inverses.shape
    return pl.pallas_call(
        functools.partial(solve_kernel, orders, shards, members),
        out_shape=jax.ShapeDtypeStruct((rows, columns), BF16),
        in_specs=[VMEM, HBM],
        out_specs=VMEM,
        scratch_shapes=[pltpu.VMEM((members, rows, LANES), F32)] * 2
        + [pltpu.VMEM(inverses.shape, BF16), pltpu.SemaphoreType.DMA((degrees // UNROLL,))],
        compiler_params=params(30),
        cost_estimate=cost(2 * degrees * radii * radii * orders * members, 2 * inverses.size),
    )(owned, in_hbm(inverses))


def synthesise_kernel(turned_ref, back_ref, coeffs_ref, out_hbm, s, y, sems):
    for rows in tiles(back_ref.shape[0], 4):
        s[rows, :] = dot(back_ref[rows, :], coeffs_ref[...]).astype(BF16)
    copies = []
    for i, rows in enumerate(tiles(turned_ref.shape[0], sems.shape[0])):
        y[rows, :] = dot(turned_ref[rows, :], s[...]).astype(BF16)
        copies.append(pltpu.make_async_copy(y.at[rows], out_hbm.at[rows], sems.at[i]))
        copies[-1].start()
    wait(*copies)


def synthesise(turned, back, coeffs):
    lats, degrees = turned.shape
    columns = coeffs.shape[1]
    return pl.pallas_call(
        synthesise_kernel,
        out_shape=pltpu.HBM((lats, columns), BF16),
        in_specs=[VMEM] * 3,
        out_specs=HBM,
        scratch_shapes=[
            pltpu.VMEM((degrees, columns), BF16),
            pltpu.VMEM((lats, columns), BF16),
            pltpu.SemaphoreType.DMA((6,)),
        ],
        compiler_params=params(16),
        cost_estimate=cost(
            2 * degrees * (lats + degrees) * columns, 2 * degrees * (lats + degrees)
        ),
    )(turned, back, coeffs)


def assemble_kernel(members, x_any, out_hbm, x16, y32, y16, in_sems, out_sems):
    orders, lats = x16.shape[:2]
    block = lats * members
    parts = fetches(x_any, x16, in_sems)
    start(*[copy for _, copy in parts])
    copies = []
    for k, (_, copy) in enumerate(parts):
        copy.wait()
        slot = k % 2
        for m in range(members):
            part = x16[k, :, m * LANES : (m + 1) * LANES].astype(F32)
            y32[slot, pl.ds(m, lats, stride=members), :] = part
        rows = pl.ds(k * block, block)
        y16[rows, :] = y32[slot].astype(BF16)
        copies.append(pltpu.make_async_copy(y16.at[rows], out_hbm.at[rows], out_sems.at[k]))
        copies[-1].start()
    wait(*copies)


def assemble(received, shape):
    orders, lats, groups, parts, _ = shape
    members = groups * parts
    block = lats * members
    out = pl.pallas_call(
        functools.partial(assemble_kernel, members),
        out_shape=pltpu.HBM((orders * block, LANES), BF16),
        in_specs=[ANY],
        out_specs=HBM,
        scratch_shapes=[
            pltpu.VMEM(received.shape, BF16),
            pltpu.VMEM((2, block, LANES), F32),
            pltpu.VMEM((orders * block, LANES), BF16),
            pltpu.SemaphoreType.DMA((orders,)),
            pltpu.SemaphoreType.DMA((orders,)),
        ],
        compiler_params=params(16),
        cost_estimate=cost(orders * block * LANES, orders * block * LANES * 4),
    )(received)
    return out.reshape(shape)


def exchange_rows(blocks):
    return lax.all_to_all(blocks, "row", split_axis=0, concat_axis=0, tiled=True)


def exchange_degrees(blocks):
    return lax.all_to_all(blocks, ("row", "col"), split_axis=0, concat_axis=0, tiled=True)


def tiled(field, coef, table, order_ids, inverses, degree_owner):
    n_row = lax.axis_size("row")
    n_col = lax.axis_size("col")
    orders, lats_dev, groups, parts, radii_dev = field.shape
    degrees_all, lats = table.shape[1:]
    deg_dev = inverses.shape[0]
    members = groups * parts
    columns = members * radii_dev

    weighted = weigh(field, coef)
    turned, chosen, back = prepare(order_ids, table[0], degree_owner)
    arrived = exchange_rows(weighted).reshape(lats, columns)
    spectral = analyse(table[0], chosen, arrived)
    owned = exchange_degrees(spectral.reshape(n_row * n_col, deg_dev, columns))
    solved = solve(owned.reshape(degrees_all, columns), inverses, orders, n_col, members)
    coeffs = exchange_degrees(solved.reshape(n_row * n_col, deg_dev, columns))
    outputs = synthesise(turned, back, coeffs.reshape(degrees_all, columns))
    received = exchange_rows(outputs.reshape(n_row, lats_dev, columns))
    return assemble(received, field.shape)


def general(field, coef, table, order_ids, inverses, degree_owner):
    both = ("row", "col")
    n_row = lax.axis_size("row")
    n_col = lax.axis_size("col")
    orders, latitudes_dev = field.shape[:2]
    members = field.shape[2] * field.shape[3]
    radii_dev = field.shape[4]
    columns = members * radii_dev
    ord_dev, degrees_all, latitudes = table.shape
    deg_dev, radii, _ = inverses.shape
    devices = n_row * n_col

    weighted = (field.astype(F32) * coef[None, :, None, None, :]).astype(BF16)
    weighted = weighted.reshape(n_row, ord_dev, latitudes_dev, columns)
    arrived = lax.all_to_all(weighted, "row", split_axis=0, concat_axis=0, tiled=True)
    arrived = arrived.swapaxes(0, 1).reshape(ord_dev, latitudes, columns)

    degrees = lax.iota(jnp.int32, degrees_all)
    chosen = (degree_owner[:, None] == degrees[None, :])[None] & (
        degrees[None, None, :] >= order_ids[:, None, None]
    )
    placed_table = jnp.einsum(
        "kpl,klt->kpt", chosen.astype(BF16), table, preferred_element_type=F32
    ).astype(BF16)
    spectral = jnp.einsum(
        "kpt,ktn->kpn", placed_table, arrived, preferred_element_type=F32
    ).astype(BF16)
    spectral = spectral.reshape(ord_dev, devices, deg_dev, columns).swapaxes(0, 1)
    owned = lax.all_to_all(spectral, both, split_axis=0, concat_axis=0, tiled=True)
    owned = owned.reshape(n_row, n_col, ord_dev, deg_dev, members, radii_dev).swapaxes(1, 2)
    owned = owned.reshape(orders, n_col, deg_dev, members, radii_dev)
    solved = jnp.einsum(
        "kadms,dtas->kdmt",
        owned,
        inverses.reshape(deg_dev, radii, n_col, radii_dev),
        preferred_element_type=F32,
    ).astype(BF16)
    solved = solved.reshape(n_row, ord_dev, deg_dev, members, n_col, radii_dev)
    solved = solved.transpose(0, 4, 1, 2, 3, 5).reshape(devices, ord_dev, deg_dev, columns)
    coeffs = lax.all_to_all(solved, both, split_axis=0, concat_axis=0, tiled=True)
    coeffs = coeffs.swapaxes(0, 1).reshape(ord_dev, degrees_all, columns)
    outputs = jnp.einsum(
        "kpt,kpn->ktn", placed_table, coeffs, preferred_element_type=F32
    ).astype(BF16)
    outputs = outputs.reshape(ord_dev, n_row, latitudes_dev, columns).swapaxes(0, 1)
    outputs = lax.all_to_all(outputs, "row", split_axis=0, concat_axis=0, tiled=True)
    return outputs.reshape(field.shape)


def per_device(field, coef, table, order_ids, inverses, degree_owner):
    orders, lats, _, _, radii_dev = field.shape
    n_row = lax.axis_size("row")
    fits = (
        orders == n_row == SUBLANES
        and radii_dev == LANES
        and lats % 16 == 0
        and inverses.shape[0] % 16 == 0
        and table.shape[1] % 256 == 0
    )
    form = tiled if fits else general
    return form(field, coef, table, order_ids, inverses, degree_owner)


def solution(mesh):
    in_specs = (
        P(None, "row", None, None, "col"),
        P("row", "col"),
        P("row", None, None),
        P("row"),
        P(("row", "col"), None, None),
        P(),
    )
    out_specs = P(None, "row", None, None, "col")
    return jax.shard_map(
        per_device, mesh=mesh, in_specs=in_specs, out_specs=out_specs, check_vma=False
    )
```

time: 139 us -> 136 us (0.978)
  Pallas kernels: 11.9 us -> 32.7 us
  matrix products: 11 us -> 0 us
  local copies, waits for them, and re-layouts: 7.15 us -> 0.01 us
  other arithmetic: 4.12 us -> 0 us
    pallas_call x0 -> x5, Pallas kernels: none -> 23.2 us  [the longest x1 7.31 us: analyse(): pl.pallas_call(analyse_kernel, out_shape=jax.ShapeDtypeStruct((rows, colu...]
    dot_general x3 -> x0, matrix products: 11 us -> none  [the longest x1 5.01 us: per_device(): jnp.einsum('klt,kpl->ktp', table, chosen, preferred_element_type=jnp.floa...]
    reshape x2 -> x0, local copies, waits for them, and re-layouts: 7.14 us -> none  [the longest x1 3.65 us: per_device(): weighted = weighted.reshape(n_row, ord_dev, latitudes_dev, columns)]
    convert_element_type x1 -> x0, other arithmetic: 4.12 us -> none  [per_device(): (field.astype(jnp.float32) * coef[None, :, None, None, :]).astype(jnp.bfl...]
    pallas_call x1, Pallas kernels: 11.9 us -> 9.52 us  [solve(): pl.pallas_call(functools.partial(solve_kernel, orders, shards, members),...]
  transfers between devices with their start and end apart: 1 -> 1, of which waited for: 1 -> 1; matrix products, arithmetic and copies ran while one was open for 4% -> 0% of each run, Pallas kernels for 0% -> 5%
where the time goes in v2:
time: 136 us
  blocking collectives  83.1 us (61%)
  Pallas kernels  32.7 us (24%)
  waiting for transfers between devices  14.2 us (10%)
  starting transfers between devices  5.18 us (4%)
    all_to_all x2, blocking collectives, exchange_degrees(): lax.all_to_all(blocks, ('row', 'col'), split_axis=0, concat_axis=0, tiled...  58.2 us
    all_to_all x1, blocking collectives, exchange_rows(): lax.all_to_all(blocks, 'row', split_axis=0, concat_axis=0, tiled=True)  24.9 us
    all_to_all x1, waiting for transfers between devices, exchange_rows(): lax.all_to_all(blocks, 'row', split_axis=0, concat_axis=0, tiled=True)  14.2 us
    pallas_call x1, Pallas kernels, solve(): pl.pallas_call(functools.partial(solve_kernel, orders, shards, members),...  9.52 us
    pallas_call x1, Pallas kernels, analyse(): pl.pallas_call(analyse_kernel, out_shape=jax.ShapeDtypeStruct((rows, colu...  7.31 us
    pallas_call x1, Pallas kernels, prepare(): pl.pallas_call(prepare_kernel, out_shape=[pltpu.HBM(shape, BF16) for shap...  6.18 us
    all_to_all x1, starting transfers between devices, exchange_rows(): lax.all_to_all(blocks, 'row', split_axis=0, concat_axis=0, tiled=True)  5.18 us
    pallas_call x1, Pallas kernels, synthesise(): pl.pallas_call(synthesise_kernel, out_shape=pltpu.HBM((lats, columns), BF...  3.63 us
  transfers between devices with their start and end apart: 1, of which 1 were waited for; matrix products, arithmetic and copies ran while one was open for 0% of the time, Pallas kernels for 5%

profile of v2, /device:TPU:0, one launch (start us, length us, event | category | flops | bytes accessed | tf_op | source)
XLA Modules:
  0.0 135.9 jit_solution(3799105411955851326)
XLA Ops:
  0.0 2.8 %shard_map.65 = bf16[8,192,512]{2,1,0:T(8,128)(2,1)} custom-call(bf16[6144,128]{1,0:T(8,128)(2,1)} %bitcast.16, f32[192,128]{1,0:T(8,128)} %coef_hbm.1), custom_call_target="tpu_custom_call" | custom-call | flops 786432 | bytes 3145728 | tf_op jit(solution)/shard_map/pallas_call | solution.py:88
  2.8 0.0 copy-start
  2.8 5.2 %all-to-all-start = ((bf16[8,192,512]{2,1,0:T(8,128)(2,1)}), bf16[8,192,512]{2,1,0:T(8,128)(2,1)S(1)}, u32[]{:S(2)}, u32[]{:S(2)}) async-start(bf16[8,192,512]{2,1,0:T(8,128)(2,1)} %shard_map.65), calls=%async_computation | async-start | bytes 3145728 | tf_op jit(solution)/shard_map/all_to_all | solution.py:316
  8.6 0.0 copy-done
  8.6 6.2 %shard_map.64 = (bf16[1536,1024]{1,0:T(8,128)(2,1)}, bf16[1024,1024]{1,0:T(8,128)(2,1)}, bf16[1024,1024]{1,0:T(8,128)(2,1)}) custom-call(s32[1]{0:T(128)S(6)} %copy.7.order_ref, bf16[1024,1536]{1,0:T(8,128)(2,1)} %bitcast.18, s32[1,1024]{1,0:T(1,128)S(1)} %bitcast.15), custom_call_target="tpu_custom_call" | custom-call | flops 5000000000 | bytes 6291456 | tf_op jit(solution)/shard_map/pallas_call | solution.py:177
  14.8 14.2 %all-to-all-done = bf16[8,192,512]{2,1,0:T(8,128)(2,1)S(1)} async-done(((bf16[8,192,512]{2,1,0:T(8,128)(2,1)}), bf16[8,192,512]{2,1,0:T(8,128)(2,1)S(1)}, u32[]{:S(2)}, u32[]{:S(2)}) %all-to-all-start) | async-done | bytes 1572896 | tf_op jit(solution)/shard_map/all_to_all | solution.py:316
  29.0 7.3 %shard_map.66 = bf16[1024,512]{1,0:T(8,128)(2,1)S(1)} custom-call(bf16[1024,1536]{1,0:T(8,128)(2,1)} %bitcast.19, bf16[1024,1024]{1,0:T(8,128)(2,1)} %get-tuple-element.10.chosen_hbm, bf16[1536,512]{1,0:T(8,128)(2,1)S(1)} %bitcast.12), custom_call_target="tpu_custom_call" | custom-call | flops 2684354560 | bytes 5242880 | tf_op jit(solution)/shard_map/pallas_call | solution.py:126
  36.3 28.9 %all_to_all.20 = bf16[32,32,512]{2,1,0:T(8,128)(2,1)S(1)} all-to-all(bf16[32,32,512]{2,1,0:T(8,128)(2,1)S(1)} %bitcast.14), channel_id=1, replica_groups=mesh['row'=8,'col'=4] {'row','col'}, dimensions={0} | all-to-all | bytes 2097152 | tf_op jit(solution)/shard_map/all_to_all | solution.py:320
  65.2 0.0 copy-start.1
  65.2 9.5 %shard_map.67 = bf16[1024,512]{1,0:T(8,128)(2,1)S(1)} custom-call(bf16[1024,512]{1,0:T(8,128)(2,1)S(1)} %bitcast.10, bf16[32,512,512]{2,1,0:T(8,128)(2,1)} %inv_hbm.1), custom_call_target="tpu_custom_call" | custom-call | flops 536870912 | bytes 16777216 | tf_op jit(solution)/shard_map/pallas_call | solution.py:231
  74.7 0.0 copy-start.2
  74.7 29.3 %all_to_all.21 = bf16[32,32,512]{2,1,0:T(8,128)(2,1)S(1)} all-to-all(bf16[32,32,512]{2,1,0:T(8,128)(2,1)S(1)} %bitcast.11), channel_id=1, replica_groups=mesh['row'=8,'col'=4] {'row','col'}, dimensions={0} | all-to-all | bytes 2097152 | tf_op jit(solution)/shard_map/all_to_all | solution.py:320
  104.0 0.0 copy-done.1
  104.0 0.0 copy-done.2
  104.0 3.6 %shard_map.68 = bf16[1536,512]{1,0:T(8,128)(2,1)} custom-call(bf16[1536,1024]{1,0:T(8,128)(2,1)S(1)} %copy-done.1, bf16[1024,1024]{1,0:T(8,128)(2,1)S(1)} %copy-done.2, bf16[1024,512]{1,0:T(8,128)(2,1)S(1)} %bitcast.13), custom_call_target="tpu_custom_call" | custom-call | flops 2684354560 | bytes 5242880 | tf_op jit(solution)/shard_map/pallas_call | solution.py:257
  107.7 24.9 %all_to_all.22.x_any = bf16[8,192,512]{2,1,0:T(8,128)(2,1)S(1)} all-to-all(bf16[8,192,512]{2,1,0:T(8,128)(2,1)} %bitcast.17), channel_id=1, replica_groups=mesh['row'=8,'col'=4] {'row'}, dimensions={0} | all-to-all | bytes 3145728 | tf_op jit(solution)/shard_map/all_to_all | solution.py:316
  132.6 3.3 %shard_map.69 = bf16[6144,128]{1,0:T(8,128)(2,1)} custom-call(bf16[8,192,512]{2,1,0:T(8,128)(2,1)S(1)} %all_to_all.22.x_any), custom_call_target="tpu_custom_call" | custom-call | flops 786432 | bytes 3145728 | tf_op jit(solution)/shard_map/pallas_call | solution.py:297
Async XLA Ops:
  2.8 5.8 %copy-start = (s32[1024]{0:T(1024)S(1)}, s32[1024]{0:T(1024)}, u32[]{:S(2)}) copy-start(s32[1024]{0:T(1024)} %param.11) | copy-start | bytes 12292
  2.8 26.2 %all-to-all-start = ((bf16[8,192,512]{2,1,0:T(8,128)(2,1)}), bf16[8,192,512]{2,1,0:T(8,128)(2,1)S(1)}, u32[]{:S(2)}, u32[]{:S(2)}) async-start(bf16[8,192,512]{2,1,0:T(8,128)(2,1)} %shard_map.65), calls=%async_computation | async-start | bytes 3145728 | tf_op jit(solution)/shard_map/all_to_all | solution.py:316
  65.2 38.9 %copy-start.1 = (bf16[1536,1024]{1,0:T(8,128)(2,1)S(1)}, bf16[1536,1024]{1,0:T(8,128)(2,1)}, u32[]{:S(2)}) copy-start(bf16[1536,1024]{1,0:T(8,128)(2,1)} %get-tuple-element.8.turned_ref) | copy-start | bytes 9437188
  74.7 29.3 %copy-start.2 = (bf16[1024,1024]{1,0:T(8,128)(2,1)S(1)}, bf16[1024,1024]{1,0:T(8,128)(2,1)}, u32[]{:S(2)}) copy-start(bf16[1024,1024]{1,0:T(8,128)(2,1)} %get-tuple-element.9.back_ref) | copy-start | bytes 6291460

commit v3 on v2

v3 whole, which is shorter than its diff:
```python
import functools

import jax
import jax.numpy as jnp
from jax import lax
from jax.experimental import pallas as pl
from jax.experimental.pallas import tpu as pltpu
from jax.sharding import PartitionSpec as P

LANES = 128
SUBLANES = 8
HELD = 8
LATE = 6
PARTNERS = (0, 6, 2, 4, 7, 1, 3, 5)
MIB = 1024 * 1024
BF16 = jnp.bfloat16
F32 = jnp.float32
VMEM = pl.BlockSpec(memory_space=pltpu.VMEM)
SMEM = pl.BlockSpec(memory_space=pltpu.SMEM)
HBM = pl.BlockSpec(memory_space=pltpu.HBM)
ANY = pl.BlockSpec(memory_space=pl.ANY)


def dot(a, b):
    return jnp.dot(a, b, preferred_element_type=F32)


def params(mib):
    return pltpu.CompilerParams(vmem_limit_bytes=mib * MIB)


def in_hbm(array):
    return pltpu.with_memory_space_constraint(array, pltpu.HBM)


def cost(flops, moved):
    return pl.CostEstimate(flops=flops, bytes_accessed=moved, transcendentals=0)


def in_vmem(array):
    return pltpu.with_memory_space_constraint(array, pltpu.VMEM)


def start(*copies):
    for copy in copies:
        copy.start()


def wait(*copies):
    for copy in copies:
        copy.wait()


def tiles(rows, count):
    return [pl.ds(i * (rows // count), rows // count) for i in range(count)]


def fetches(source, target, sems):
    parts = tiles(source.shape[0], sems.shape[0])
    copies = [
        pltpu.make_async_copy(source.at[part], target.at[part], sems.at[i])
        for i, part in enumerate(parts)
    ]
    return list(zip(parts, copies))


def weigh_kernel(members, me_ref, x_hbm, coef_hbm, *rest):
    outs, (x16, x32, y16, coef, coef_sem, in_sems, out_sems) = rest[:-7], rest[-7:]
    lats = coef.shape[0]
    coef_copy = pltpu.make_async_copy(coef_hbm, coef, coef_sem)
    coef_copy.start()
    block = lats * members
    parts = []
    for j in range(len(outs)):
        rows = pl.ds(pl.multiple_of((me_ref[0] ^ PARTNERS[j]) * block, block), block)
        parts.append(pltpu.make_async_copy(x_hbm.at[rows], x16.at[j], in_sems.at[j]))
    start(*parts)
    coef_copy.wait()
    stores = []
    for j, copy in enumerate(parts):
        copy.wait()
        slot = j % 2
        x32[slot] = x16[j].astype(F32)
        for m in range(members):
            part = x32[slot, pl.ds(m, lats, stride=members), :]
            y16[j, :, m * LANES : (m + 1) * LANES] = (part * coef[...]).astype(BF16)
        stores.append(pltpu.make_async_copy(y16.at[j], outs[j], out_sems.at[j]))
        stores[-1].start()
    wait(*stores)


def weigh(me, field, coef):
    orders, lats, groups, parts, _ = field.shape
    members = groups * parts
    block = lats * members
    shape = (orders, lats, members * LANES)
    return pl.pallas_call(
        functools.partial(weigh_kernel, members),
        out_shape=[pltpu.HBM(shape[1:], BF16)] * orders,
        in_specs=[SMEM, HBM, HBM],
        out_specs=[HBM] * orders,
        scratch_shapes=[
            pltpu.VMEM((orders, block, LANES), BF16),
            pltpu.VMEM((2, block, LANES), F32),
            pltpu.VMEM(shape, BF16),
            pltpu.VMEM(coef.shape, F32),
            pltpu.SemaphoreType.DMA,
            pltpu.SemaphoreType.DMA((orders,)),
            pltpu.SemaphoreType.DMA((orders,)),
        ],
        compiler_params=params(16),
        cost_estimate=cost(field.size, field.size * 4),
    )(me, in_hbm(field.reshape(orders * block, LANES)), in_hbm(coef))


def analyse_kernel(me_ref, table_ref, inv_hbm, *rest):
    blocks, (out_ref, inv_ref, w, inv_sem) = rest[:-4], rest[-4:]
    inv_copy = pltpu.make_async_copy(inv_hbm.at[: inv_ref.shape[0]], inv_ref, inv_sem)
    inv_copy.start()
    lats = blocks[0].shape[0]
    for j, block in enumerate(blocks):
        w[pl.ds(pl.multiple_of((me_ref[0] ^ PARTNERS[j]) * lats, lats), lats), :] = block[...]
    for rows in tiles(table_ref.shape[0], 4):
        out_ref[rows, :] = dot(table_ref[rows, :], w[...]).astype(BF16)
    inv_copy.wait()


def analyse(me, table, inverses, blocks):
    rows, lats = table.shape
    columns = blocks[0].shape[1]
    held = (inverses.shape[0] // HELD, *inverses.shape[1:])
    return pl.pallas_call(
        analyse_kernel,
        out_shape=[jax.ShapeDtypeStruct((rows, columns), BF16), pltpu.VMEM(held, BF16)],
        in_specs=[SMEM, VMEM, HBM] + [VMEM] * len(blocks),
        out_specs=[VMEM, VMEM],
        scratch_shapes=[pltpu.VMEM((lats, columns), BF16), pltpu.SemaphoreType.DMA],
        compiler_params=params(14),
        cost_estimate=cost(2 * rows * lats * columns, 2 * rows * lats + inverses.size),
    )(me, table, in_hbm(inverses), *blocks)


def place_kernel(order_ref, table_hbm, owner_hbm, placed_ref, table, owner, chosen, table_sem, owner_sem):
    owner_copy = pltpu.make_async_copy(owner_hbm, owner, owner_sem)
    table_copy = pltpu.make_async_copy(table_hbm, table, table_sem)
    start(owner_copy, table_copy)
    degrees = table.shape[0]
    order = order_ref[0]
    owner_copy.wait()
    across = jnp.broadcast_to(owner[...], (LANES, degrees)).T
    for block in range(degrees // LANES):
        part = slice(block * LANES, (block + 1) * LANES)
        degree = lax.broadcasted_iota(jnp.int32, (degrees, LANES), 1) + block * LANES
        chosen[:, part] = ((across == degree) & (degree >= order)).astype(F32).astype(BF16)
    table_copy.wait()
    for rows in tiles(degrees, 4):
        placed_ref[rows, :] = dot(chosen[rows, :], table[...]).astype(BF16)


def place(order_ids, table, degree_owner):
    degrees, lats = table.shape
    return pl.pallas_call(
        place_kernel,
        out_shape=jax.ShapeDtypeStruct((degrees, lats), BF16),
        in_specs=[SMEM, HBM, HBM],
        out_specs=VMEM,
        scratch_shapes=[
            pltpu.VMEM(table.shape, BF16),
            pltpu.VMEM((1, degrees), jnp.int32),
            pltpu.VMEM((degrees, degrees), BF16),
            pltpu.SemaphoreType.DMA,
            pltpu.SemaphoreType.DMA,
        ],
        compiler_params=params(16),
        cost_estimate=cost(2 * degrees * degrees * lats, 4 * table.size),
    )(order_ids, in_hbm(table), in_hbm(degree_owner.reshape(1, degrees)))


def turn_kernel(table_ref, turned_hbm, turned, sems):
    copies = []
    for i, rows in enumerate(tiles(turned.shape[0], 4)):
        turned[rows, :] = table_ref[:, rows.start : rows.start + rows.size].T
        copies.append(pltpu.make_async_copy(turned.at[rows], turned_hbm.at[rows], sems.at[i]))
        copies[-1].start()
    wait(*copies)


def turn(table):
    turned = table.shape[::-1]
    return pl.pallas_call(
        turn_kernel,
        out_shape=pltpu.HBM(turned, BF16),
        in_specs=[VMEM],
        out_specs=HBM,
        scratch_shapes=[pltpu.VMEM(turned, BF16), pltpu.SemaphoreType.DMA((4,))],
        compiler_params=params(12),
        cost_estimate=cost(table.size, 4 * table.size),
    )(table)


def solve_kernel(orders, shards, members, x_ref, here_ref, inv_hbm, y_ref, x32, y32, inv, sems):
    degrees, held = inv_hbm.shape[0], here_ref.shape[0]
    parts = fetches(inv_hbm.at[held:], inv, sems)
    start(*[copy for _, copy in parts])
    block = shards * degrees
    stride = x32.shape[1] // orders
    half = degrees // 2

    def widen(part):
        for k in range(orders):
            for r in range(shards):
                first = r * degrees + part * half
                rows, to = pl.ds(k * block + first, half), pl.ds(k * stride + first, half)
                for m in range(members):
                    x32[m, to, :] = x_ref[rows, m * LANES : (m + 1) * LANES].astype(F32)

    def narrow(part):
        for k in range(orders):
            for r in range(shards):
                first = r * degrees + part * half
                rows, at = pl.ds(k * block + first, half), pl.ds(k * stride + first, half)
                for m in range(members):
                    y_ref[rows, m * LANES : (m + 1) * LANES] = y32[m, at, :].astype(BF16)

    def apply(matrix, degree):
        def rows(shard):
            return pl.ds(shard * degrees + degree, orders, stride=stride)

        x = jnp.concatenate(
            [
                jnp.concatenate([x32[m, rows(r), :] for r in range(shards)], axis=1)
                for m in range(members)
            ],
            axis=0,
        ).astype(BF16)
        y = lax.dot_general(x, matrix, (((1,), (1,)), ((), ())), preferred_element_type=F32)
        for m in range(members):
            for r in range(shards):
                y32[m, rows(r), :] = y[m * orders : (m + 1) * orders, r * LANES : (r + 1) * LANES]

    each = (degrees - held) // len(parts)
    widen(0)
    for degree in range(degrees):
        if degree == half:
            widen(1)
            narrow(0)
        if degree < held:
            matrix = here_ref[degree]
        else:
            if (degree - held) % each == 0:
                parts[(degree - held) // each][1].wait()
            matrix = inv[degree - held]
        apply(matrix, degree)
    narrow(1)


def solve(owned, here, inverses, orders, shards, members):
    rows, columns = owned.shape
    degrees, radii, _ = inverses.shape
    rest = degrees - here.shape[0]
    return pl.pallas_call(
        functools.partial(solve_kernel, orders, shards, members),
        out_shape=jax.ShapeDtypeStruct((rows, columns), BF16),
        in_specs=[VMEM, VMEM, HBM],
        out_specs=VMEM,
        scratch_shapes=[pltpu.VMEM((members, rows + orders, LANES), F32)] * 2
        + [pltpu.VMEM((rest, radii, radii), BF16), pltpu.SemaphoreType.DMA((rest // 4,))],
        compiler_params=params(24),
        cost_estimate=cost(2 * degrees * radii * radii * orders * members, inverses.size),
    )(owned, in_vmem(here), in_hbm(inverses))


def synthesise_kernel(me_ref, turned_ref, coeffs_ref, *outs):
    lats = outs[0].shape[0]
    for j, out in enumerate(outs):
        rows = pl.ds(pl.multiple_of((me_ref[0] ^ PARTNERS[j]) * lats, lats), lats)
        out[...] = dot(turned_ref[rows, :], coeffs_ref[...]).astype(BF16)


def synthesise(me, turned, coeffs, partners):
    lats, degrees = turned.shape
    columns = coeffs.shape[1]
    return pl.pallas_call(
        synthesise_kernel,
        out_shape=[jax.ShapeDtypeStruct((lats // partners, columns), BF16)] * partners,
        in_specs=[SMEM] + [VMEM] * 2,
        out_specs=[VMEM] * partners,
        compiler_params=params(12),
        cost_estimate=cost(2 * degrees * lats * columns, 2 * degrees * lats),
    )(me, turned, coeffs)


def assemble_kernel(members, me_ref, *rest):
    blocks, (out_hbm, y32, y16, out_sems) = rest[:-4], rest[-4:]
    lats = blocks[0].shape[0]
    block = lats * members
    copies = []
    for j, x_ref in enumerate(blocks):
        slot = j % 2
        for m in range(members):
            part = x_ref[:, m * LANES : (m + 1) * LANES].astype(F32)
            y32[slot, pl.ds(m, lats, stride=members), :] = part
        y16[j] = y32[slot].astype(BF16)
        rows = pl.ds(pl.multiple_of((me_ref[0] ^ PARTNERS[j]) * block, block), block)
        copies.append(pltpu.make_async_copy(y16.at[j], out_hbm.at[rows], out_sems.at[j]))
        copies[-1].start()
    wait(*copies)


def assemble(me, received, shape):
    orders, lats, groups, parts, _ = shape
    members = groups * parts
    block = lats * members
    out = pl.pallas_call(
        functools.partial(assemble_kernel, members),
        out_shape=pltpu.HBM((orders * block, LANES), BF16),
        in_specs=[SMEM] + [VMEM] * orders,
        out_specs=HBM,
        scratch_shapes=[
            pltpu.VMEM((2, block, LANES), F32),
            pltpu.VMEM((orders, block, LANES), BF16),
            pltpu.SemaphoreType.DMA((orders,)),
        ],
        compiler_params=params(12),
        cost_estimate=cost(orders * block * LANES, orders * block * LANES * 4),
    )(me, *received)
    return out.reshape(shape)


def exchange_rows(blocks):
    n = lax.axis_size("row")
    return [
        block if not j else lax.ppermute(block, "row", [(a, a ^ j) for a in range(n)])
        for block, j in zip(blocks, PARTNERS)
    ]


def exchange_degrees(blocks):
    return lax.all_to_all(blocks, ("row", "col"), split_axis=0, concat_axis=0, tiled=True)


def tiled(field, coef, table, order_ids, inverses, degree_owner):
    n_row = lax.axis_size("row")
    n_col = lax.axis_size("col")
    orders, lats_dev, groups, parts, radii_dev = field.shape
    degrees_all, lats = table.shape[1:]
    deg_dev = inverses.shape[0]
    members = groups * parts
    columns = members * radii_dev

    me = lax.axis_index("row").astype(jnp.int32).reshape(1)

    weighted = list(weigh(me, field, coef))
    placed = place(order_ids, table[0], degree_owner)
    placed, *weighted[LATE:] = lax.optimization_barrier((placed, *weighted[LATE:]))
    arrived = exchange_rows(weighted)
    turned = turn(placed)
    turned, arrived[0] = lax.optimization_barrier((turned, arrived[0]))
    spectral, here = analyse(me, placed, inverses, arrived)
    owned = exchange_degrees(spectral.reshape(n_row * n_col, deg_dev, columns))
    solved = solve(owned.reshape(degrees_all, columns), here, inverses, orders, n_col, members)
    coeffs = exchange_degrees(solved.reshape(n_row * n_col, deg_dev, columns))
    outputs = synthesise(me, turned, coeffs.reshape(degrees_all, columns), n_row)
    return assemble(me, exchange_rows(outputs), field.shape)


def general(field, coef, table, order_ids, inverses, degree_owner):
    both = ("row", "col")
    n_row = lax.axis_size("row")
    n_col = lax.axis_size("col")
    orders, latitudes_dev = field.shape[:2]
    members = field.shape[2] * field.shape[3]
    radii_dev = field.shape[4]
    columns = members * radii_dev
    ord_dev, degrees_all, latitudes = table.shape
    deg_dev, radii, _ = inverses.shape
    devices = n_row * n_col

    weighted = (field.astype(F32) * coef[None, :, None, None, :]).astype(BF16)
    weighted = weighted.reshape(n_row, ord_dev, latitudes_dev, columns)
    arrived = lax.all_to_all(weighted, "row", split_axis=0, concat_axis=0, tiled=True)
    arrived = arrived.swapaxes(0, 1).reshape(ord_dev, latitudes, columns)

    degrees = lax.iota(jnp.int32, degrees_all)
    chosen = (degree_owner[:, None] == degrees[None, :])[None] & (
        degrees[None, None, :] >= order_ids[:, None, None]
    )
    placed_table = jnp.einsum(
        "kpl,klt->kpt", chosen.astype(BF16), table, preferred_element_type=F32
    ).astype(BF16)
    spectral = jnp.einsum(
        "kpt,ktn->kpn", placed_table, arrived, preferred_element_type=F32
    ).astype(BF16)
    spectral = spectral.reshape(ord_dev, devices, deg_dev, columns).swapaxes(0, 1)
    owned = lax.all_to_all(spectral, both, split_axis=0, concat_axis=0, tiled=True)
    owned = owned.reshape(n_row, n_col, ord_dev, deg_dev, members, radii_dev).swapaxes(1, 2)
    owned = owned.reshape(orders, n_col, deg_dev, members, radii_dev)
    solved = jnp.einsum(
        "kadms,dtas->kdmt",
        owned,
        inverses.reshape(deg_dev, radii, n_col, radii_dev),
        preferred_element_type=F32,
    ).astype(BF16)
    solved = solved.reshape(n_row, ord_dev, deg_dev, members, n_col, radii_dev)
    solved = solved.transpose(0, 4, 1, 2, 3, 5).reshape(devices, ord_dev, deg_dev, columns)
    coeffs = lax.all_to_all(solved, both, split_axis=0, concat_axis=0, tiled=True)
    coeffs = coeffs.swapaxes(0, 1).reshape(ord_dev, degrees_all, columns)
    outputs = jnp.einsum(
        "kpt,kpn->ktn", placed_table, coeffs, preferred_element_type=F32
    ).astype(BF16)
    outputs = outputs.reshape(ord_dev, n_row, latitudes_dev, columns).swapaxes(0, 1)
    outputs = lax.all_to_all(outputs, "row", split_axis=0, concat_axis=0, tiled=True)
    return outputs.reshape(field.shape)


def per_device(field, coef, table, order_ids, inverses, degree_owner):
    orders, lats, _, _, radii_dev = field.shape
    n_row = lax.axis_size("row")
    fits = (
        orders == n_row == SUBLANES
        and radii_dev == LANES
        and lats % 16 == 0
        and inverses.shape[0] % 16 == 0
        and table.shape[1] % 256 == 0
    )
    form = tiled if fits else general
    return form(field, coef, table, order_ids, inverses, degree_owner)


def solution(mesh):
    in_specs = (
        P(None, "row", None, None, "col"),
        P("row", "col"),
        P("row", None, None),
        P("row"),
        P(("row", "col"), None, None),
        P(),
    )
    out_specs = P(None, "row", None, None, "col")
    return jax.shard_map(
        per_device, mesh=mesh, in_specs=in_specs, out_specs=out_specs, check_vma=False
    )
```

time: 136 us -> 119 us (0.88)
  blocking collectives: 83.1 us -> 59.8 us
  starting transfers between devices: 5.18 us -> 17 us
  Pallas kernels: 32.7 us -> 22.3 us
  waiting for transfers between devices: 14.2 us -> 18.5 us
    all_to_all x1 -> x0, blocking collectives: 24.9 us -> none  [exchange_rows(): lax.all_to_all(blocks, 'row', split_axis=0, concat_axis=0, tiled=True)]
    ppermute x0 -> x14, waiting for transfers between devices: none -> 18.5 us  [exchange_rows(): lax.ppermute(block, 'row', [(a, a ^ j) for a in range(n)])]
    ppermute x0 -> x14, starting transfers between devices: none -> 17 us  [exchange_rows(): lax.ppermute(block, 'row', [(a, a ^ j) for a in range(n)])]
    all_to_all x1 -> x0, waiting for transfers between devices: 14.2 us -> none  [exchange_rows(): lax.all_to_all(blocks, 'row', split_axis=0, concat_axis=0, tiled=True)]
    pallas_call x4 -> x5, Pallas kernels: 19.9 us -> 14 us  [the longest x1 5.39 us: place(): pl.pallas_call(place_kernel, out_shape=jax.ShapeDtypeStruct((degrees, lat...]
    all_to_all x1 -> x0, starting transfers between devices: 5.18 us -> none  [exchange_rows(): lax.all_to_all(blocks, 'row', split_axis=0, concat_axis=0, tiled=True)]
    pallas_call x1, Pallas kernels: 9.52 us -> 7.08 us  [solve(): pl.pallas_call(functools.partial(solve_kernel, orders, shards, members),...]
    pallas_call x1, Pallas kernels: 3.33 us -> 1.29 us  [assemble(): pl.pallas_call(functools.partial(assemble_kernel, members), out_shape=plt...]
  transfers between devices with their start and end apart: 1 -> 14, of which waited for: 1 -> 8; matrix products, arithmetic and copies ran while one was open for 0% -> 0% of each run, Pallas kernels for 5% -> 6%
where the time goes in v3:
time: 119 us; the launch traced here: 118 us
  blocking collectives  59.8 us (50%)
  Pallas kernels  22.3 us (19%)
  waiting for transfers between devices  18.5 us (16%)
  starting transfers between devices  17 us (14%)
    all_to_all x2, blocking collectives, exchange_degrees(): lax.all_to_all(blocks, ('row', 'col'), split_axis=0, concat_axis=0, tiled...  59.8 us
    ppermute x14, waiting for transfers between devices, exchange_rows(): lax.ppermute(block, 'row', [(a, a ^ j) for a in range(n)])  18.5 us
    ppermute x14, starting transfers between devices, exchange_rows(): lax.ppermute(block, 'row', [(a, a ^ j) for a in range(n)])  17 us
    pallas_call x1, Pallas kernels, solve(): pl.pallas_call(functools.partial(solve_kernel, orders, shards, members),...  7.08 us
    pallas_call x1, Pallas kernels, place(): pl.pallas_call(place_kernel, out_shape=jax.ShapeDtypeStruct((degrees, lat...  5.39 us
    pallas_call x1, Pallas kernels, weigh(): pl.pallas_call(functools.partial(weigh_kernel, members), out_shape=[pltpu...  2.77 us
  transfers between devices with their start and end apart: 14, of which 8 were waited for; matrix products, arithmetic and copies ran while one was open for 0% of the time, Pallas kernels for 6%

profile of v3, /device:TPU:0, one launch (start us, length us, event | category | flops | bytes accessed | tf_op | source)
XLA Modules:
  0.0 118.4 jit_solution(6558622232910844102)
XLA Ops:
  0.0 2.8 %shard_map.65 = (bf16[192,512]{1,0:T(8,128)(2,1)}, bf16[192,512]{1,0:T(8,128)(2,1)}, bf16[192,512]{1,0:T(8,128)(2,1)}, bf16[192,512]{1,0:T(8,128)(2,1)}, bf16[19...) custom-call(s32[1]{0:T(128)} %bitcast.me_ref, ...), custom_call_target="tpu_custom_call" | custom-call | flops 786432 | bytes 3145728 | tf_op jit(solution)/shard_map/pallas_call | solution.py:97
  2.8 4.0 %collective-permute-start = (bf16[192,512]{1,0:T(8,128)(2,1)}, bf16[192,512]{1,0:T(8,128)(2,1)S(1)}, u32[]{:S(2)}, u32[]{:S(2)}) collective-permute-start(bf16[192,512]{1,0:T(8,128)(2,1)} %get-tuple-element.34), channel_id=1, source_target_pairs={{0,24},{4,28},{8,16},{12,20},{16,8},{20,12},{24,0},{28,4},{1,25},{... | collective-permute-start | bytes 589832 | tf_op jit(solution)/shard_map/ppermute | solution.py:333
  6.7 0.5 collective-permute-start.1
  7.3 0.1 collective-permute-start.2
  7.4 1.4 %collective-permute-start.3 = (bf16[192,512]{1,0:T(8,128)(2,1)}, bf16[192,512]{1,0:T(8,128)(2,1)S(1)}, u32[]{:S(2)}, u32[]{:S(2)}) collective-permute-start(bf16[192,512]{1,0:T(8,128)(2,1)} %get-tuple-element.37), channel_id=1, source_target_pairs={{0,28},{4,24},{8,20},{12,16},{16,12},{20,8},{24,4},{28,0},{1,29},{... | collective-permute-start | bytes 589832 | tf_op jit(solution)/shard_map/ppermute | solution.py:333
  8.8 1.5 %collective-permute-start.4 = (bf16[192,512]{1,0:T(8,128)(2,1)}, bf16[192,512]{1,0:T(8,128)(2,1)S(1)}, u32[]{:S(2)}, u32[]{:S(2)}) collective-permute-start(bf16[192,512]{1,0:T(8,128)(2,1)} %get-tuple-element.38), channel_id=1, source_target_pairs={{0,4},{4,0},{8,12},{12,8},{16,20},{20,16},{24,28},{28,24},{1,5},{5... | collective-permute-start | bytes 589832 | tf_op jit(solution)/shard_map/ppermute | solution.py:333
  11.0 5.4 %shard_map.64.table_ref = bf16[1024,1536]{1,0:T(8,128)(2,1)S(1)} custom-call(s32[1]{0:T(128)S(6)} %copy.7.order_ref, bf16[1024,1536]{1,0:T(8,128)(2,1)} %bitcast.14, s32[1,1024]{1,0:T(1,128)} %bitcast.15), custom_call_target="tpu_custom_call" | custom-call | flops 3221225472 | bytes 6291456 | tf_op jit(solution)/shard_map/pallas_call | solution.py:162
  16.4 0.0 copy-start.1
  16.4 0.2 collective-permute-start.5
  16.7 0.8 collective-permute-done.1.rest_2_
  17.5 0.0 collective-permute-start.6
  17.5 2.0 %shard_map.66.turned_ref = bf16[1536,1024]{1,0:T(8,128)(2,1)} custom-call(bf16[1024,1536]{1,0:T(8,128)(2,1)S(1)} %shard_map.64.table_ref), custom_call_target="tpu_custom_call" | custom-call | flops 1572864 | bytes 6291456 | tf_op jit(solution)/shard_map/pallas_call | solution.py:190
  19.5 1.3 %collective-permute-done.3.rest_4_ = bf16[192,512]{1,0:T(8,128)(2,1)S(1)} collective-permute-done((bf16[192,512]{1,0:T(8,128)(2,1)}, bf16[192,512]{1,0:T(8,128)(2,1)S(1)}, u32[]{:S(2)}, u32[]{:S(2)}) %collective-permute-start.3) | collective-permute-done | bytes 196640 | tf_op jit(solution)/shard_map/ppermute | solution.py:333
  20.8 3.0 %collective-permute-done.5.rest_6_ = bf16[192,512]{1,0:T(8,128)(2,1)S(1)} collective-permute-done((bf16[192,512]{1,0:T(8,128)(2,1)S(1)}, bf16[192,512]{1,0:T(8,128)(2,1)S(1)}, u32[]{:S(2)}, u32[]{:S(2)}) %collective-permute-start.5) | collective-permute-done | bytes 196640 | tf_op jit(solution)/shard_map/ppermute | solution.py:333
  23.8 1.2 collective-permute-done.6.rest_7_
  24.9 1.9 %shard_map.67 = (bf16[1024,512]{1,0:T(8,128)(2,1)S(1)}, bf16[4,512,512]{2,1,0:T(8,128)(2,1)S(1)}) custom-call(s32[1]{0:T(128)} %bitcast.me_ref, bf16[1024,1536]{1,0:T(8,128)(2,1)S(1)} %shard_map.64.table_ref, bf16[32,512,512]{2,1,0:T(8,128)(2,1)} %inv_hbm.3, bf16[192,512]{1,0:T(8,128)(2,1)S(1)} %copy-done.1, ...), custom_call_target="tpu_custom_call" | custom-call | flops 1610612736 | bytes 11534336 | tf_op jit(solution)/shard_map/pallas_call | solution.py:132
  26.9 30.5 %all_to_all.10 = bf16[32,32,512]{2,1,0:T(8,128)(2,1)S(1)} all-to-all(bf16[32,32,512]{2,1,0:T(8,128)(2,1)S(1)} %bitcast.11), channel_id=1, replica_groups=mesh['row'=8,'col'=4] {'row','col'}, dimensions={0} | all-to-all | bytes 2097152 | tf_op jit(solution)/shard_map/all_to_all | solution.py:339
  57.3 7.1 %shard_map.68 = bf16[1024,512]{1,0:T(8,128)(2,1)S(1)} custom-call(bf16[1024,512]{1,0:T(8,128)(2,1)S(1)} %bitcast.9, bf16[4,512,512]{2,1,0:T(8,128)(2,1)S(1)} %get-tuple-element.42.here_ref, bf16[32,512,512]{2,1,0:T(8,128)(2,1)} %inv_hbm.3), custom_call_target="tpu_custom_call" | custom-call | flops 536870912 | bytes 8388608 | tf_op jit(solution)/shard_map/pallas_call | solution.py:261
  64.4 29.3 %all_to_all.11 = bf16[32,32,512]{2,1,0:T(8,128)(2,1)S(1)} all-to-all(bf16[32,32,512]{2,1,0:T(8,128)(2,1)S(1)} %bitcast.10), channel_id=1, replica_groups=mesh['row'=8,'col'=4] {'row','col'}, dimensions={0} | all-to-all | bytes 2097152 | tf_op jit(solution)/shard_map/all_to_all | solution.py:339
  93.7 1.9 %shard_map.69 = (bf16[192,512]{1,0:T(8,128)(2,1)S(1)}, bf16[192,512]{1,0:T(8,128)(2,1)S(1)}, bf16[192,512]{1,0:T(8,128)(2,1)S(1)}, bf16[192,512]{1,0:T(8,128)(2,...) custom-call(s32[1]{0:T(128)} %bitcast.me_ref, ...), custom_call_target="tpu_custom_call" | custom-call | flops 1610612736 | bytes 3145728 | tf_op jit(solution)/shard_map/pallas_call | solution.py:283
  95.7 2.4 %collective-permute-start.7 = (bf16[192,512]{1,0:T(8,128)(2,1)S(1)}, bf16[192,512]{1,0:T(8,128)(2,1)S(1)}, u32[]{:S(2)}, u32[]{:S(2)}) collective-permute-start(bf16[192,512]{1,0:T(8,128)(2,1)S(1)} %get-tuple-element.44), channel_id=1, source_target_pairs={{0,24},{4,28},{8,16},{12,20},{16,8},{20,12},{24,0},{28,4},{1,25},{... | collective-permute-start | bytes 589832 | tf_op jit(solution)/shard_map/ppermute | solution.py:333
  98.1 0.5 collective-permute-start.8
  98.7 0.6 collective-permute-start.9
  99.2 1.8 %collective-permute-start.10 = (bf16[192,512]{1,0:T(8,128)(2,1)S(1)}, bf16[192,512]{1,0:T(8,128)(2,1)S(1)}, u32[]{:S(2)}, u32[]{:S(2)}) collective-permute-start(bf16[192,512]{1,0:T(8,128)(2,1)S(1)} %get-tuple-element.47), channel_id=1, source_target_pairs={{0,28},{4,24},{8,20},{12,16},{16,12},{20,8},{24,4},{28,0},{1,29},{... | collective-permute-start | bytes 589832 | tf_op jit(solution)/shard_map/ppermute | solution.py:333
  101.0 0.7 collective-permute-start.11
  101.7 2.3 %collective-permute-done.7.rest_1_ = bf16[192,512]{1,0:T(8,128)(2,1)S(1)} collective-permute-done((bf16[192,512]{1,0:T(8,128)(2,1)S(1)}, bf16[192,512]{1,0:T(8,128)(2,1)S(1)}, u32[]{:S(2)}, u32[]{:S(2)}) %collective-permute-start.7) | collective-permute-done | bytes 196640 | tf_op jit(solution)/shard_map/ppermute | solution.py:333
  104.0 1.9 %collective-permute-start.12 = (bf16[192,512]{1,0:T(8,128)(2,1)S(1)}, bf16[192,512]{1,0:T(8,128)(2,1)S(1)}, u32[]{:S(2)}, u32[]{:S(2)}) collective-permute-start(bf16[192,512]{1,0:T(8,128)(2,1)S(1)} %get-tuple-element.49), channel_id=1, source_target_pairs={{0,12},{4,8},{8,4},{12,0},{16,28},{20,24},{24,20},{28,16},{1,13},{... | collective-permute-start | bytes 589832 | tf_op jit(solution)/shard_map/ppermute | solution.py:333
  105.9 2.3 %collective-permute-done.8.rest_2_ = bf16[192,512]{1,0:T(8,128)(2,1)S(1)} collective-permute-done((bf16[192,512]{1,0:T(8,128)(2,1)S(1)}, bf16[192,512]{1,0:T(8,128)(2,1)S(1)}, u32[]{:S(2)}, u32[]{:S(2)}) %collective-permute-start.8) | collective-permute-done | bytes 196640 | tf_op jit(solution)/shard_map/ppermute | solution.py:333
  108.1 1.3 %collective-permute-start.13 = (bf16[192,512]{1,0:T(8,128)(2,1)S(1)}, bf16[192,512]{1,0:T(8,128)(2,1)S(1)}, u32[]{:S(2)}, u32[]{:S(2)}) collective-permute-start(bf16[192,512]{1,0:T(8,128)(2,1)S(1)} %get-tuple-element.50), channel_id=1, source_target_pairs={{0,20},{4,16},{8,28},{12,24},{16,4},{20,0},{24,12},{28,8},{1,21},{... | collective-permute-start | bytes 589832 | tf_op jit(solution)/shard_map/ppermute | solution.py:333
  109.5 3.9 %collective-permute-done.10.rest_4_ = bf16[192,512]{1,0:T(8,128)(2,1)S(1)} collective-permute-done((bf16[192,512]{1,0:T(8,128)(2,1)S(1)}, bf16[192,512]{1,0:T(8,128)(2,1)S(1)}, u32[]{:S(2)}, u32[]{:S(2)}) %collective-permute-start.10) | collective-permute-done | bytes 196640 | tf_op jit(solution)/shard_map/ppermute | solution.py:333
  113.4 3.7 %collective-permute-done.12.rest_6_ = bf16[192,512]{1,0:T(8,128)(2,1)S(1)} collective-permute-done((bf16[192,512]{1,0:T(8,128)(2,1)S(1)}, bf16[192,512]{1,0:T(8,128)(2,1)S(1)}, u32[]{:S(2)}, u32[]{:S(2)}) %collective-permute-start.12) | collective-permute-done | bytes 196640 | tf_op jit(solution)/shard_map/ppermute | solution.py:333
  117.1 1.3 %shard_map.70 = bf16[6144,128]{1,0:T(8,128)(2,1)} custom-call(s32[1]{0:T(128)} %bitcast.me_ref, bf16[192,512]{1,0:T(8,128)(2,1)S(1)} %get-tuple-element.43.rest_0_, bf16[192,512]{1,0:T(8,128)(2,1)S(1)} %collective-permute-done.7.rest_1_, bf16[192,512]{1,0:T(8,128)(2,1)S(1)} %collective-permute-done.8.rest_2_, ...), custom_call_target="tpu_custom_call" | custom-call | flops 786432 | bytes 3145728 | tf_op jit(solution)/shard_map/pallas_call | solution.py:314
  (13 shorter events, 0.0 us)
Async XLA Ops:
  2.8 13.7 %collective-permute-start = (bf16[192,512]{1,0:T(8,128)(2,1)}, bf16[192,512]{1,0:T(8,128)(2,1)S(1)}, u32[]{:S(2)}, u32[]{:S(2)}) collective-permute-start(bf16[192,512]{1,0:T(8,128)(2,1)} %get-tuple-element.34), channel_id=1, source_target_pairs={{0,24},{4,28},{8,16},{12,20},{16,8},{20,12},{24,0},{28,4},{1,25},{... | collective-permute-start | bytes 589832 | tf_op jit(solution)/shard_map/ppermute | solution.py:333
  6.7 10.8 %collective-permute-start.1 = (bf16[192,512]{1,0:T(8,128)(2,1)}, bf16[192,512]{1,0:T(8,128)(2,1)S(1)}, u32[]{:S(2)}, u32[]{:S(2)}) collective-permute-start(bf16[192,512]{1,0:T(8,128)(2,1)} %get-tuple-element.35), channel_id=1, source_target_pairs={{0,8},{4,12},{8,0},{12,4},{16,24},{20,28},{24,16},{28,20},{1,9},{5... | collective-permute-start | bytes 589832 | tf_op jit(solution)/shard_map/ppermute | solution.py:333
  7.3 12.2 %collective-permute-start.2 = (bf16[192,512]{1,0:T(8,128)(2,1)}, bf16[192,512]{1,0:T(8,128)(2,1)S(1)}, u32[]{:S(2)}, u32[]{:S(2)}) collective-permute-start(bf16[192,512]{1,0:T(8,128)(2,1)} %get-tuple-element.36), channel_id=1, source_target_pairs={{0,16},{4,20},{8,24},{12,28},{16,0},{20,4},{24,8},{28,12},{1,17},{... | collective-permute-start | bytes 589832 | tf_op jit(solution)/shard_map/ppermute | solution.py:333
  7.4 13.4 %collective-permute-start.3 = (bf16[192,512]{1,0:T(8,128)(2,1)}, bf16[192,512]{1,0:T(8,128)(2,1)S(1)}, u32[]{:S(2)}, u32[]{:S(2)}) collective-permute-start(bf16[192,512]{1,0:T(8,128)(2,1)} %get-tuple-element.37), channel_id=1, source_target_pairs={{0,28},{4,24},{8,20},{12,16},{16,12},{20,8},{24,4},{28,0},{1,29},{... | collective-permute-start | bytes 589832 | tf_op jit(solution)/shard_map/ppermute | solution.py:333
  8.8 12.0 %collective-permute-start.4 = (bf16[192,512]{1,0:T(8,128)(2,1)}, bf16[192,512]{1,0:T(8,128)(2,1)S(1)}, u32[]{:S(2)}, u32[]{:S(2)}) collective-permute-start(bf16[192,512]{1,0:T(8,128)(2,1)} %get-tuple-element.38), channel_id=1, source_target_pairs={{0,4},{4,0},{8,12},{12,8},{16,20},{20,16},{24,28},{28,24},{1,5},{5... | collective-permute-start | bytes 589832 | tf_op jit(solution)/shard_map/ppermute | solution.py:333
  11.0 5.4 %copy-start.3 = (bf16[192,512]{1,0:T(8,128)(2,1)S(1)}, bf16[192,512]{1,0:T(8,128)(2,1)}, u32[]{:S(2)}) copy-start(bf16[192,512]{1,0:T(8,128)(2,1)} %get-tuple-element.39) | copy-start | bytes 589828
  11.0 6.5 %copy-start.2 = (bf16[192,512]{1,0:T(8,128)(2,1)S(1)}, bf16[192,512]{1,0:T(8,128)(2,1)}, u32[]{:S(2)}) copy-start(bf16[192,512]{1,0:T(8,128)(2,1)} %get-tuple-element.40) | copy-start | bytes 589828
  16.4 8.5 %copy-start.1 = (bf16[192,512]{1,0:T(8,128)(2,1)S(1)}, bf16[192,512]{1,0:T(8,128)(2,1)}, u32[]{:S(2)}) copy-start(bf16[192,512]{1,0:T(8,128)(2,1)} %get-tuple-element.33.rest_0_) | copy-start | bytes 589828
  16.4 7.3 %collective-permute-start.5 = (bf16[192,512]{1,0:T(8,128)(2,1)S(1)}, bf16[192,512]{1,0:T(8,128)(2,1)S(1)}, u32[]{:S(2)}, u32[]{:S(2)}) collective-permute-start(bf16[192,512]{1,0:T(8,128)(2,1)S(1)} %copy-done.3), channel_id=1, source_target_pairs={{0,12},{4,8},{8,4},{12,0},{16,28},{20,24},{24,20},{28,16},{1,13},{... | collective-permute-start | bytes 589832 | tf_op jit(solution)/shard_map/ppermute | solution.py:333
  17.5 7.4 %collective-permute-start.6 = (bf16[192,512]{1,0:T(8,128)(2,1)S(1)}, bf16[192,512]{1,0:T(8,128)(2,1)S(1)}, u32[]{:S(2)}, u32[]{:S(2)}) collective-permute-start(bf16[192,512]{1,0:T(8,128)(2,1)S(1)} %copy-done.2), channel_id=1, source_target_pairs={{0,20},{4,16},{8,28},{12,24},{16,4},{20,0},{24,12},{28,8},{1,21},{... | collective-permute-start | bytes 589832 | tf_op jit(solution)/shard_map/ppermute | solution.py:333
  57.3 36.4 %copy-start = (bf16[1536,1024]{1,0:T(8,128)(2,1)S(1)}, bf16[1536,1024]{1,0:T(8,128)(2,1)}, u32[]{:S(2)}) copy-start(bf16[1536,1024]{1,0:T(8,128)(2,1)} %shard_map.66.turned_ref) | copy-start | bytes 9437188
  95.7 8.3 %collective-permute-start.7 = (bf16[192,512]{1,0:T(8,128)(2,1)S(1)}, bf16[192,512]{1,0:T(8,128)(2,1)S(1)}, u32[]{:S(2)}, u32[]{:S(2)}) collective-permute-start(bf16[192,512]{1,0:T(8,128)(2,1)S(1)} %get-tuple-element.44), channel_id=1, source_target_pairs={{0,24},{4,28},{8,16},{12,20},{16,8},{20,12},{24,0},{28,4},{1,25},{... | collective-permute-start | bytes 589832 | tf_op jit(solution)/shard_map/ppermute | solution.py:333
  98.1 10.0 %collective-permute-start.8 = (bf16[192,512]{1,0:T(8,128)(2,1)S(1)}, bf16[192,512]{1,0:T(8,128)(2,1)S(1)}, u32[]{:S(2)}, u32[]{:S(2)}) collective-permute-start(bf16[192,512]{1,0:T(8,128)(2,1)S(1)} %get-tuple-element.45), channel_id=1, source_target_pairs={{0,8},{4,12},{8,0},{12,4},{16,24},{20,28},{24,16},{28,20},{1,9},{5... | collective-permute-start | bytes 589832 | tf_op jit(solution)/shard_map/ppermute | solution.py:333
  98.7 10.8 %collective-permute-start.9 = (bf16[192,512]{1,0:T(8,128)(2,1)S(1)}, bf16[192,512]{1,0:T(8,128)(2,1)S(1)}, u32[]{:S(2)}, u32[]{:S(2)}) collective-permute-start(bf16[192,512]{1,0:T(8,128)(2,1)S(1)} %get-tuple-element.46), channel_id=1, source_target_pairs={{0,16},{4,20},{8,24},{12,28},{16,0},{20,4},{24,8},{28,12},{1,17},{... | collective-permute-start | bytes 589832 | tf_op jit(solution)/shard_map/ppermute | solution.py:333
  99.2 14.1 %collective-permute-start.10 = (bf16[192,512]{1,0:T(8,128)(2,1)S(1)}, bf16[192,512]{1,0:T(8,128)(2,1)S(1)}, u32[]{:S(2)}, u32[]{:S(2)}) collective-permute-start(bf16[192,512]{1,0:T(8,128)(2,1)S(1)} %get-tuple-element.47), channel_id=1, source_target_pairs={{0,28},{4,24},{8,20},{12,16},{16,12},{20,8},{24,4},{28,0},{1,29},{... | collective-permute-start | bytes 589832 | tf_op jit(solution)/shard_map/ppermute | solution.py:333
  101.0 12.4 %collective-permute-start.11 = (bf16[192,512]{1,0:T(8,128)(2,1)S(1)}, bf16[192,512]{1,0:T(8,128)(2,1)S(1)}, u32[]{:S(2)}, u32[]{:S(2)}) collective-permute-start(bf16[192,512]{1,0:T(8,128)(2,1)S(1)} %get-tuple-element.48), channel_id=1, source_target_pairs={{0,4},{4,0},{8,12},{12,8},{16,20},{20,16},{24,28},{28,24},{1,5},{5... | collective-permute-start | bytes 589832 | tf_op jit(solution)/shard_map/ppermute | solution.py:333
  104.0 13.1 %collective-permute-start.12 = (bf16[192,512]{1,0:T(8,128)(2,1)S(1)}, bf16[192,512]{1,0:T(8,128)(2,1)S(1)}, u32[]{:S(2)}, u32[]{:S(2)}) collective-permute-start(bf16[192,512]{1,0:T(8,128)(2,1)S(1)} %get-tuple-element.49), channel_id=1, source_target_pairs={{0,12},{4,8},{8,4},{12,0},{16,28},{20,24},{24,20},{28,16},{1,13},{... | collective-permute-start | bytes 589832 | tf_op jit(solution)/shard_map/ppermute | solution.py:333
  108.1 9.0 %collective-permute-start.13 = (bf16[192,512]{1,0:T(8,128)(2,1)S(1)}, bf16[192,512]{1,0:T(8,128)(2,1)S(1)}, u32[]{:S(2)}, u32[]{:S(2)}) collective-permute-start(bf16[192,512]{1,0:T(8,128)(2,1)S(1)} %get-tuple-element.50), channel_id=1, source_target_pairs={{0,20},{4,16},{8,28},{12,24},{16,4},{20,0},{24,12},{28,8},{1,21},{... | collective-permute-start | bytes 589832 | tf_op jit(solution)/shard_map/ppermute | solution.py:333

commit v4 on v3

--- a/solution.py
+++ b/solution.py
@@ -9,7 +9,9 @@
 
 LANES = 128
 SUBLANES = 8
-HELD = 8
+HELD = 24
+RING = 12
+FIRST = 5
 LATE = 6
 PARTNERS = (0, 6, 2, 4, 7, 1, 3, 5)
 MIB = 1024 * 1024
@@ -65,7 +67,7 @@
 
 
 def weigh_kernel(members, me_ref, x_hbm, coef_hbm, *rest):
-    outs, (x16, x32, y16, coef, coef_sem, in_sems, out_sems) = rest[:-7], rest[-7:]
+    outs, (x16, x32, coef, coef_sem, in_sems) = rest[:-5], rest[-5:]
     lats = coef.shape[0]
     coef_copy = pltpu.make_async_copy(coef_hbm, coef, coef_sem)
     coef_copy.start()
@@ -76,68 +78,57 @@
         parts.append(pltpu.make_async_copy(x_hbm.at[rows], x16.at[j], in_sems.at[j]))
     start(*parts)
     coef_copy.wait()
-    stores = []
     for j, copy in enumerate(parts):
         copy.wait()
         slot = j % 2
-        x32[slot] = x16[j].astype(F32)
+        x32[slot, :block] = x16[j].astype(F32)
         for m in range(members):
             part = x32[slot, pl.ds(m, lats, stride=members), :]
-            y16[j, :, m * LANES : (m + 1) * LANES] = (part * coef[...]).astype(BF16)
-        stores.append(pltpu.make_async_copy(y16.at[j], outs[j], out_sems.at[j]))
-        stores[-1].start()
-    wait(*stores)
+            outs[j][:, m * LANES : (m + 1) * LANES] = (part * coef[...]).astype(BF16)
 
 
 def weigh(me, field, coef):
     orders, lats, groups, parts, _ = field.shape
     members = groups * parts
     block = lats * members
-    shape = (orders, lats, members * LANES)
     return pl.pallas_call(
         functools.partial(weigh_kernel, members),
-        out_shape=[pltpu.HBM(shape[1:], BF16)] * orders,
+        out_shape=[jax.ShapeDtypeStruct((lats, members * LANES), BF16)] * orders,
         in_specs=[SMEM, HBM, HBM],
-        out_specs=[HBM] * orders,
+        out_specs=[VMEM] * orders,
         scratch_shapes=[
             pltpu.VMEM((orders, block, LANES), BF16),
-            pltpu.VMEM((2, block, LANES), F32),
-            pltpu.VMEM(shape, BF16),
+            pltpu.VMEM((2, block + SUBLANES, LANES), F32),
             pltpu.VMEM(coef.shape, F32),
             pltpu.SemaphoreType.DMA,
             pltpu.SemaphoreType.DMA((orders,)),
-            pltpu.SemaphoreType.DMA((orders,)),
         ],
-        compiler_params=params(16),
+        compiler_params=params(12),
         cost_estimate=cost(field.size, field.size * 4),
     )(me, in_hbm(field.reshape(orders * block, LANES)), in_hbm(coef))
 
 
-def analyse_kernel(me_ref, table_ref, inv_hbm, *rest):
-    blocks, (out_ref, inv_ref, w, inv_sem) = rest[:-4], rest[-4:]
-    inv_copy = pltpu.make_async_copy(inv_hbm.at[: inv_ref.shape[0]], inv_ref, inv_sem)
-    inv_copy.start()
+def analyse_kernel(me_ref, table_ref, *rest):
+    blocks, (out_ref, w) = rest[:-2], rest[-2:]
     lats = blocks[0].shape[0]
     for j, block in enumerate(blocks):
         w[pl.ds(pl.multiple_of((me_ref[0] ^ PARTNERS[j]) * lats, lats), lats), :] = block[...]
     for rows in tiles(table_ref.shape[0], 4):
         out_ref[rows, :] = dot(table_ref[rows, :], w[...]).astype(BF16)
-    inv_copy.wait()
-
-
-def analyse(me, table, inverses, blocks):
+
+
+def analyse(me, table, blocks):
     rows, lats = table.shape
     columns = blocks[0].shape[1]
-    held = (inverses.shape[0] // HELD, *inverses.shape[1:])
     return pl.pallas_call(
         analyse_kernel,
-        out_shape=[jax.ShapeDtypeStruct((rows, columns), BF16), pltpu.VMEM(held, BF16)],
-        in_specs=[SMEM, VMEM, HBM] + [VMEM] * len(blocks),
-        out_specs=[VMEM, VMEM],
-        scratch_shapes=[pltpu.VMEM((lats, columns), BF16), pltpu.SemaphoreType.DMA],
+        out_shape=jax.ShapeDtypeStruct((rows, columns), BF16),
+        in_specs=[SMEM] + [VMEM] * (1 + len(blocks)),
+        out_specs=VMEM,
+        scratch_shapes=[pltpu.VMEM((lats, columns), BF16)],
         compiler_params=params(14),
-        cost_estimate=cost(2 * rows * lats * columns, 2 * rows * lats + inverses.size),
-    )(me, table, in_hbm(inverses), *blocks)
+        cost_estimate=cost(2 * rows * lats * columns, 2 * rows * lats),
+    )(me, table, *blocks)
 
 
 def place_kernel(order_ref, table_hbm, owner_hbm, placed_ref, table, owner, chosen, table_sem, owner_sem):
@@ -176,34 +167,54 @@
     )(order_ids, in_hbm(table), in_hbm(degree_owner.reshape(1, degrees)))
 
 
-def turn_kernel(table_ref, turned_hbm, turned, sems):
+def turn_kernel(table_ref, inv_hbm, turned_hbm, here_ref, turned, ring, sems, ring_sems):
+    degrees, slots = here_ref.shape[0], ring.shape[0]
+
+    def fetch(degree):
+        slot = degree % slots
+        return pltpu.make_async_copy(inv_hbm.at[degree], ring.at[slot], ring_sems.at[slot])
+
+    for degree in range(slots):
+        fetch(degree).start()
     copies = []
     for i, rows in enumerate(tiles(turned.shape[0], 4)):
         turned[rows, :] = table_ref[:, rows.start : rows.start + rows.size].T
         copies.append(pltpu.make_async_copy(turned.at[rows], turned_hbm.at[rows], sems.at[i]))
         copies[-1].start()
+    for degree in range(degrees):
+        fetch(degree).wait()
+        here_ref[degree] = ring[degree % slots].T
+        if degree + slots < degrees:
+            fetch(degree + slots).start()
     wait(*copies)
 
 
-def turn(table):
+def turn(table, inverses, count):
     turned = table.shape[::-1]
+    radii = inverses.shape[1:]
     return pl.pallas_call(
         turn_kernel,
-        out_shape=pltpu.HBM(turned, BF16),
-        in_specs=[VMEM],
-        out_specs=HBM,
-        scratch_shapes=[pltpu.VMEM(turned, BF16), pltpu.SemaphoreType.DMA((4,))],
-        compiler_params=params(12),
-        cost_estimate=cost(table.size, 4 * table.size),
-    )(table)
+        out_shape=[pltpu.HBM(turned, BF16), pltpu.VMEM((count, *radii), BF16)],
+        in_specs=[VMEM, HBM],
+        out_specs=[HBM, VMEM],
+        scratch_shapes=[
+            pltpu.VMEM(turned, BF16),
+            pltpu.VMEM((RING, *radii), BF16),
+            pltpu.SemaphoreType.DMA((4,)),
+            pltpu.SemaphoreType.DMA((RING,)),
+        ],
+        compiler_params=params(16),
+        cost_estimate=cost(table.size, 4 * table.size + 4 * inverses.size),
+    )(table, in_hbm(inverses))
 
 
 def solve_kernel(orders, shards, members, x_ref, here_ref, inv_hbm, y_ref, x32, y32, inv, sems):
     degrees, held = inv_hbm.shape[0], here_ref.shape[0]
     parts = fetches(inv_hbm.at[held:], inv, sems)
     start(*[copy for _, copy in parts])
+    each = (degrees - held) // len(parts)
     block = shards * degrees
-    stride = x32.shape[1] // orders
+    stride = block + 1
     half = degrees // 2
 
     def widen(part):
@@ -222,7 +233,7 @@
                 for m in range(members):
                     y_ref[rows, m * LANES : (m + 1) * LANES] = y32[m, at, :].astype(BF16)
 
-    def apply(matrix, degree):
+    def apply(degree):
         def rows(shard):
             return pl.ds(shard * degrees + degree, orders, stride=stride)
 
@@ -233,25 +244,23 @@
             ],
             axis=0,
         ).astype(BF16)
-        y = lax.dot_general(x, matrix, (((1,), (1,)), ((), ())), preferred_element_type=F32)
+        if degree < held:
+            y = dot(x, here_ref[degree])
+        else:
+            if (degree - held) % each == 0:
+                parts[(degree - held) // each][1].wait()
+            y = lax.dot_general(
+                x, inv[degree - held], (((1,), (1,)), ((), ())), preferred_element_type=F32
+            )
         for m in range(members):
             for r in range(shards):
                 y32[m, rows(r), :] = y[m * orders : (m + 1) * orders, r * LANES : (r + 1) * LANES]
 
-    each = (degrees - held) // len(parts)
-    widen(0)
-    for degree in range(degrees):
-        if degree == half:
-            widen(1)
-            narrow(0)
-        if degree < held:
-            matrix = here_ref[degree]
-        else:
-            if (degree - held) % each == 0:
-                parts[(degree - held) // each][1].wait()
-            matrix = inv[degree - held]
-        apply(matrix, degree)
-    narrow(1)
+    for part in range(2):
+        widen(part)
+        for degree in range(part * half, (part + 1) * half):
+            apply(degree)
+        narrow(part)
 
 
 def solve(owned, here, inverses, orders, shards, members):
@@ -263,30 +272,31 @@
         out_shape=jax.ShapeDtypeStruct((rows, columns), BF16),
         in_specs=[VMEM, VMEM, HBM],
         out_specs=VMEM,
-        scratch_shapes=[pltpu.VMEM((members, rows + orders, LANES), F32)] * 2
+        scratch_shapes=[pltpu.VMEM((members, rows + 2 * orders + rows // orders, LANES), F32)] * 2
         + [pltpu.VMEM((rest, radii, radii), BF16), pltpu.SemaphoreType.DMA((rest // 4,))],
         compiler_params=params(24),
         cost_estimate=cost(2 * degrees * radii * radii * orders * members, inverses.size),
     )(owned, in_vmem(here), in_hbm(inverses))
 
 
-def synthesise_kernel(me_ref, turned_ref, coeffs_ref, *outs):
+def synthesise_kernel(partners, me_ref, turned_ref, coeffs_ref, *outs):
     lats = outs[0].shape[0]
-    for j, out in enumerate(outs):
-        rows = pl.ds(pl.multiple_of((me_ref[0] ^ PARTNERS[j]) * lats, lats), lats)
+    for j, out in zip(partners, outs):
+        rows = pl.ds(pl.multiple_of((me_ref[0] ^ j) * lats, lats), lats)
         out[...] = dot(turned_ref[rows, :], coeffs_ref[...]).astype(BF16)
 
 
 def synthesise(me, turned, coeffs, partners):
     lats, degrees = turned.shape
     columns = coeffs.shape[1]
-    return pl.pallas_call(
-        synthesise_kernel,
-        out_shape=[jax.ShapeDtypeStruct((lats // partners, columns), BF16)] * partners,
+    count = len(partners)
+    return pl.pallas_call(
+        functools.partial(synthesise_kernel, partners),
+        out_shape=[jax.ShapeDtypeStruct((lats // len(PARTNERS), columns), BF16)] * count,
         in_specs=[SMEM] + [VMEM] * 2,
-        out_specs=[VMEM] * partners,
+        out_specs=[VMEM] * count,
         compiler_params=params(12),
-        cost_estimate=cost(2 * degrees * lats * columns, 2 * degrees * lats),
+        cost_estimate=cost(2 * degrees * lats * columns // 2, 2 * degrees * lats),
     )(me, turned, coeffs)
 
 
@@ -300,7 +310,7 @@
         for m in range(members):
             part = x_ref[:, m * LANES : (m + 1) * LANES].astype(F32)
             y32[slot, pl.ds(m, lats, stride=members), :] = part
-        y16[j] = y32[slot].astype(BF16)
+        y16[j] = y32[slot, :block].astype(BF16)
         rows = pl.ds(pl.multiple_of((me_ref[0] ^ PARTNERS[j]) * block, block), block)
         copies.append(pltpu.make_async_copy(y16.at[j], out_hbm.at[rows], out_sems.at[j]))
         copies[-1].start()
@@ -317,7 +327,7 @@
         in_specs=[SMEM] + [VMEM] * orders,
         out_specs=HBM,
         scratch_shapes=[
-            pltpu.VMEM((2, block, LANES), F32),
+            pltpu.VMEM((2, block + SUBLANES, LANES), F32),
             pltpu.VMEM((orders, block, LANES), BF16),
             pltpu.SemaphoreType.DMA((orders,)),
         ],
@@ -327,11 +337,11 @@
     return out.reshape(shape)
 
 
-def exchange_rows(blocks):
+def exchange_rows(blocks, partners):
     n = lax.axis_size("row")
     return [
         block if not j else lax.ppermute(block, "row", [(a, a ^ j) for a in range(n)])
-        for block, j in zip(blocks, PARTNERS)
+        for block, j in zip(blocks, partners)
     ]
 
 
@@ -353,15 +363,22 @@
     weighted = list(weigh(me, field, coef))
     placed = place(order_ids, table[0], degree_owner)
     placed, *weighted[LATE:] = lax.optimization_barrier((placed, *weighted[LATE:]))
-    arrived = exchange_rows(weighted)
-    turned = turn(placed)
-    turned, arrived[0] = lax.optimization_barrier((turned, arrived[0]))
-    spectral, here = analyse(me, placed, inverses, arrived)
+    arrived = exchange_rows(weighted, PARTNERS)
+    turned, here = turn(placed, inverses, HELD)
+    here, turned, arrived[0] = lax.optimization_barrier((here, turned, arrived[0]))
+    spectral = analyse(me, placed, arrived)
     owned = exchange_degrees(spectral.reshape(n_row * n_col, deg_dev, columns))
     solved = solve(owned.reshape(degrees_all, columns), here, inverses, orders, n_col, members)
     coeffs = exchange_degrees(solved.reshape(n_row * n_col, deg_dev, columns))
-    outputs = synthesise(me, turned, coeffs.reshape(degrees_all, columns), n_row)
-    return assemble(me, exchange_rows(outputs), field.shape)
+    coeffs = coeffs.reshape(degrees_all, columns)
+    outputs = synthesise(me, turned, coeffs, PARTNERS[:FIRST])
+    received = exchange_rows(outputs, PARTNERS[:FIRST])
+    if FIRST < len(PARTNERS):
+        quick = 1
+        received[quick], coeffs = lax.optimization_barrier((received[quick], coeffs))
+        outputs = synthesise(me, turned, coeffs, PARTNERS[FIRST:])
+        received += exchange_rows(outputs, PARTNERS[FIRST:])
+    return assemble(me, received, field.shape)
 
 
 def general(field, coef, table, order_ids, inverses, degree_owner):

time: 119 us -> 114 us (0.958)
  waiting for transfers between devices: 18.5 us -> 13.1 us
    ppermute x14, waiting for transfers between devices: 18.5 us -> 13.1 us  [exchange_rows(): lax.ppermute(block, 'row', [(a, a ^ j) for a in range(n)])]
    pallas_call x4 -> x5, Pallas kernels: 8.56 us -> 12.8 us  [the longest x1 6.96 us: turn(): pl.pallas_call(turn_kernel, out_shape=[pltpu.HBM(turned, BF16), pltpu.VME...]
    pallas_call x1, Pallas kernels: 7.08 us -> 3.85 us  [solve(): pl.pallas_call(functools.partial(solve_kernel, orders, shards, members),...]
  transfers between devices with their start and end apart: 14 -> 14, of which waited for: 8 -> 6; matrix products, arithmetic and copies ran while one was open for 0% -> 0% of each run, Pallas kernels for 6% -> 12%
where the time goes in v4:
time: 114 us
  blocking collectives  59.9 us (53%)
  Pallas kernels  23.3 us (20%)
  starting transfers between devices  16.4 us (14%)
  waiting for transfers between devices  13.1 us (11%)
    all_to_all x2, blocking collectives, exchange_degrees(): lax.all_to_all(blocks, ('row', 'col'), split_axis=0, concat_axis=0, tiled...  59.9 us
    ppermute x14, starting transfers between devices, exchange_rows(): lax.ppermute(block, 'row', [(a, a ^ j) for a in range(n)])  16.4 us
    ppermute x14, waiting for transfers between devices, exchange_rows(): lax.ppermute(block, 'row', [(a, a ^ j) for a in range(n)])  13.1 us
    pallas_call x1, Pallas kernels, turn(): pl.pallas_call(turn_kernel, out_shape=[pltpu.HBM(turned, BF16), pltpu.VME...  6.96 us
    pallas_call x1, Pallas kernels, place(): pl.pallas_call(place_kernel, out_shape=jax.ShapeDtypeStruct((degrees, lat...  5.34 us
    pallas_call x1, Pallas kernels, solve(): pl.pallas_call(functools.partial(solve_kernel, orders, shards, members),...  3.85 us
  transfers between devices with their start and end apart: 14, of which 6 were waited for; matrix products, arithmetic and copies ran while one was open for 0% of the time, Pallas kernels for 12%

profile of v4, /device:TPU:0, one launch (start us, length us, event | category | flops | bytes accessed | tf_op | source)
XLA Modules:
  0.0 113.5 jit_solution(5021341232128332855)
XLA Ops:
  0.0 2.0 %shard_map.65 = (bf16[192,512]{1,0:T(8,128)(2,1)S(1)}, bf16[192,512]{1,0:T(8,128)(2,1)S(1)}, bf16[192,512]{1,0:T(8,128)(2,1)S(1)}, bf16[192,512]{1,0:T(8,128)(2,...) custom-call(s32[1]{0:T(128)} %bitcast.me_ref, ...), custom_call_target="tpu_custom_call" | custom-call | flops 786432 | bytes 3145728 | tf_op jit(solution)/shard_map/pallas_call | solution.py:94
  2.0 4.0 %collective-permute-start = (bf16[192,512]{1,0:T(8,128)(2,1)S(1)}, bf16[192,512]{1,0:T(8,128)(2,1)S(1)}, u32[]{:S(2)}, u32[]{:S(2)}) collective-permute-start(bf16[192,512]{1,0:T(8,128)(2,1)S(1)} %get-tuple-element.39), channel_id=1, source_target_pairs={{0,24},{4,28},{8,16},{12,20},{16,8},{20,12},{24,0},{28,4},{1,25},{... | collective-permute-start | bytes 589832 | tf_op jit(solution)/shard_map/ppermute | solution.py:343
  6.0 0.5 collective-permute-start.1
  6.5 0.1 collective-permute-start.2
  6.6 1.4 %collective-permute-start.3 = (bf16[192,512]{1,0:T(8,128)(2,1)S(1)}, bf16[192,512]{1,0:T(8,128)(2,1)S(1)}, u32[]{:S(2)}, u32[]{:S(2)}) collective-permute-start(bf16[192,512]{1,0:T(8,128)(2,1)S(1)} %get-tuple-element.42), channel_id=1, source_target_pairs={{0,28},{4,24},{8,20},{12,16},{16,12},{20,8},{24,4},{28,0},{1,29},{... | collective-permute-start | bytes 589832 | tf_op jit(solution)/shard_map/ppermute | solution.py:343
  8.1 1.5 %collective-permute-start.4 = (bf16[192,512]{1,0:T(8,128)(2,1)S(1)}, bf16[192,512]{1,0:T(8,128)(2,1)S(1)}, u32[]{:S(2)}, u32[]{:S(2)}) collective-permute-start(bf16[192,512]{1,0:T(8,128)(2,1)S(1)} %get-tuple-element.43), channel_id=1, source_target_pairs={{0,4},{4,0},{8,12},{12,8},{16,20},{20,16},{24,28},{28,24},{1,5},{5... | collective-permute-start | bytes 589832 | tf_op jit(solution)/shard_map/ppermute | solution.py:343
  10.2 5.3 %shard_map.64.table_ref = bf16[1024,1536]{1,0:T(8,128)(2,1)S(1)} custom-call(s32[1]{0:T(128)S(6)} %copy.7.order_ref, bf16[1024,1536]{1,0:T(8,128)(2,1)} %bitcast.15, s32[1,1024]{1,0:T(1,128)} %bitcast.16), custom_call_target="tpu_custom_call" | custom-call | flops 3221225472 | bytes 6291456 | tf_op jit(solution)/shard_map/pallas_call | solution.py:153
  15.6 0.2 collective-permute-start.5
  15.8 0.7 collective-permute-done.1.rest_2_
  16.5 7.0 %shard_map.66 = (bf16[1536,1024]{1,0:T(8,128)(2,1)}, bf16[24,512,512]{2,1,0:T(8,128)(2,1)S(1)}) custom-call(bf16[1024,1536]{1,0:T(8,128)(2,1)S(1)} %shard_map.64.table_ref, bf16[32,512,512]{2,1,0:T(8,128)(2,1)} %inv_hbm.3), custom_call_target="tpu_custom_call" | custom-call | flops 1572864 | bytes 39845888 | tf_op jit(solution)/shard_map/pallas_call | solution.py:195
  23.5 0.0 collective-permute-done.4.rest_5_
  23.5 0.0 collective-permute-done.5.rest_6_
  23.6 0.4 collective-permute-done.6.rest_7_
  24.0 1.9 %shard_map.67 = bf16[1024,512]{1,0:T(8,128)(2,1)S(1)} custom-call(s32[1]{0:T(128)} %bitcast.me_ref, bf16[1024,1536]{1,0:T(8,128)(2,1)S(1)} %shard_map.64.table_ref, bf16[192,512]{1,0:T(8,128)(2,1)S(1)} %get-tuple-element.38.rest_0_, bf16[192,512]{1,0:T(8,128)(2,1)S(1)} %collective-permute-done.rest_1_, bf16[192,512]{1,0:T(8,128)(2,1)S(1)} %collective-permute-done.1.rest_2_, ...), custom_call_target="tpu_custom_call" | custom-call | flops 1610612736 | bytes 3145728 | tf_op jit(solution)/shard_map/pallas_call | solution.py:123
  25.9 30.6 %all_to_all.10 = bf16[32,32,512]{2,1,0:T(8,128)(2,1)S(1)} all-to-all(bf16[32,32,512]{2,1,0:T(8,128)(2,1)S(1)} %bitcast.13), channel_id=1, replica_groups=mesh['row'=8,'col'=4] {'row','col'}, dimensions={0} | all-to-all | bytes 2097152 | tf_op jit(solution)/shard_map/all_to_all | solution.py:349
  56.4 3.9 %shard_map.68 = bf16[1024,512]{1,0:T(8,128)(2,1)S(1)} custom-call(bf16[1024,512]{1,0:T(8,128)(2,1)S(1)} %bitcast.11, bf16[24,512,512]{2,1,0:T(8,128)(2,1)S(1)} %get-tuple-element.46.here_ref, bf16[32,512,512]{2,1,0:T(8,128)(2,1)} %inv_hbm.3), custom_call_target="tpu_custom_call" | custom-call | flops 536870912 | bytes 8388608 | tf_op jit(solution)/shard_map/pallas_call | solution.py:270
  60.3 29.3 %all_to_all.11 = bf16[32,32,512]{2,1,0:T(8,128)(2,1)S(1)} all-to-all(bf16[32,32,512]{2,1,0:T(8,128)(2,1)S(1)} %bitcast.12), channel_id=1, replica_groups=mesh['row'=8,'col'=4] {'row','col'}, dimensions={0} | all-to-all | bytes 2097152 | tf_op jit(solution)/shard_map/all_to_all | solution.py:349
  89.6 1.2 %shard_map.69 = (bf16[192,512]{1,0:T(8,128)(2,1)S(1)}, bf16[192,512]{1,0:T(8,128)(2,1)S(1)}, bf16[192,512]{1,0:T(8,128)(2,1)S(1)}, bf16[192,512]{1,0:T(8,128)(2,1)S(1)}, bf16[192,512]{1,0:T(8,128)(2,1)S(1)}) custom-call(s32[1]{0:T(128)} %bitcast.me_ref, bf16[1536,1024]{1,0:T(8,128)(2,1)S(1)} %copy-done, bf16[1024,512]{1,0:T(8,128)(2,1)S(1)} %bitcast.9), custom_call_target="tpu_custom_call" | custom-call | flops 805306368 | bytes 3145728 | tf_op jit(solution)/shard_map/pallas_call | solution.py:293
  90.8 2.5 %collective-permute-start.7 = (bf16[192,512]{1,0:T(8,128)(2,1)S(1)}, bf16[192,512]{1,0:T(8,128)(2,1)S(1)}, u32[]{:S(2)}, u32[]{:S(2)}) collective-permute-start(bf16[192,512]{1,0:T(8,128)(2,1)S(1)} %get-tuple-element.48), channel_id=1, source_target_pairs={{0,24},{4,28},{8,16},{12,20},{16,8},{20,12},{24,0},{28,4},{1,25},{... | collective-permute-start | bytes 589832 | tf_op jit(solution)/shard_map/ppermute | solution.py:343
  93.2 0.5 collective-permute-start.8
  93.8 0.6 collective-permute-start.9
  94.3 1.8 %collective-permute-start.10 = (bf16[192,512]{1,0:T(8,128)(2,1)S(1)}, bf16[192,512]{1,0:T(8,128)(2,1)S(1)}, u32[]{:S(2)}, u32[]{:S(2)}) collective-permute-start(bf16[192,512]{1,0:T(8,128)(2,1)S(1)} %get-tuple-element.52), channel_id=1, source_target_pairs={{0,28},{4,24},{8,20},{12,16},{16,12},{20,8},{24,4},{28,0},{1,29},{... | collective-permute-start | bytes 589832 | tf_op jit(solution)/shard_map/ppermute | solution.py:343
  96.1 3.0 %collective-permute-done.7.rest_1_ = bf16[192,512]{1,0:T(8,128)(2,1)S(1)} collective-permute-done((bf16[192,512]{1,0:T(8,128)(2,1)S(1)}, bf16[192,512]{1,0:T(8,128)(2,1)S(1)}, u32[]{:S(2)}, u32[]{:S(2)}) %collective-permute-start.7) | collective-permute-done | bytes 196640 | tf_op jit(solution)/shard_map/ppermute | solution.py:343
  99.1 0.8 shard_map.70
  99.9 0.8 collective-permute-start.11
  100.7 1.2 %collective-permute-start.12 = (bf16[192,512]{1,0:T(8,128)(2,1)S(1)}, bf16[192,512]{1,0:T(8,128)(2,1)S(1)}, u32[]{:S(2)}, u32[]{:S(2)}) collective-permute-start(bf16[192,512]{1,0:T(8,128)(2,1)S(1)} %get-tuple-element.55), channel_id=1, source_target_pairs={{0,12},{4,8},{8,4},{12,0},{16,28},{20,24},{24,20},{28,16},{1,13},{... | collective-permute-start | bytes 589832 | tf_op jit(solution)/shard_map/ppermute | solution.py:343
  101.9 1.3 %collective-permute-done.8.rest_2_ = bf16[192,512]{1,0:T(8,128)(2,1)S(1)} collective-permute-done((bf16[192,512]{1,0:T(8,128)(2,1)S(1)}, bf16[192,512]{1,0:T(8,128)(2,1)S(1)}, u32[]{:S(2)}, u32[]{:S(2)}) %collective-permute-start.8) | collective-permute-done | bytes 196640 | tf_op jit(solution)/shard_map/ppermute | solution.py:343
  103.2 1.3 %collective-permute-start.13 = (bf16[192,512]{1,0:T(8,128)(2,1)S(1)}, bf16[192,512]{1,0:T(8,128)(2,1)S(1)}, u32[]{:S(2)}, u32[]{:S(2)}) collective-permute-start(bf16[192,512]{1,0:T(8,128)(2,1)S(1)} %get-tuple-element.56), channel_id=1, source_target_pairs={{0,20},{4,16},{8,28},{12,24},{16,4},{20,0},{24,12},{28,8},{1,21},{... | collective-permute-start | bytes 589832 | tf_op jit(solution)/shard_map/ppermute | solution.py:343
  104.6 0.0 collective-permute-done.9.rest_3_
  104.6 3.9 %collective-permute-done.10.rest_4_ = bf16[192,512]{1,0:T(8,128)(2,1)S(1)} collective-permute-done((bf16[192,512]{1,0:T(8,128)(2,1)S(1)}, bf16[192,512]{1,0:T(8,128)(2,1)S(1)}, u32[]{:S(2)}, u32[]{:S(2)}) %collective-permute-start.10) | collective-permute-done | bytes 196640 | tf_op jit(solution)/shard_map/ppermute | solution.py:343
  108.5 3.7 %collective-permute-done.12.rest_6_ = bf16[192,512]{1,0:T(8,128)(2,1)S(1)} collective-permute-done((bf16[192,512]{1,0:T(8,128)(2,1)S(1)}, bf16[192,512]{1,0:T(8,128)(2,1)S(1)}, u32[]{:S(2)}, u32[]{:S(2)}) %collective-permute-start.12) | collective-permute-done | bytes 196640 | tf_op jit(solution)/shard_map/ppermute | solution.py:343
  112.2 1.3 %shard_map.71 = bf16[6144,128]{1,0:T(8,128)(2,1)} custom-call(s32[1]{0:T(128)} %bitcast.me_ref, bf16[192,512]{1,0:T(8,128)(2,1)S(1)} %get-tuple-element.47.rest_0_, bf16[192,512]{1,0:T(8,128)(2,1)S(1)} %collective-permute-done.7.rest_1_, bf16[192,512]{1,0:T(8,128)(2,1)S(1)} %collective-permute-done.8.rest_2_, ...), custom_call_target="tpu_custom_call" | custom-call | flops 786432 | bytes 3145728 | tf_op jit(solution)/shard_map/pallas_call | solution.py:324
  (8 shorter events, 0.0 us)
Async XLA Ops:
  2.0 13.6 %collective-permute-start = (bf16[192,512]{1,0:T(8,128)(2,1)S(1)}, bf16[192,512]{1,0:T(8,128)(2,1)S(1)}, u32[]{:S(2)}, u32[]{:S(2)}) collective-permute-start(bf16[192,512]{1,0:T(8,128)(2,1)S(1)} %get-tuple-element.39), channel_id=1, source_target_pairs={{0,24},{4,28},{8,16},{12,20},{16,8},{20,12},{24,0},{28,4},{1,25},{... | collective-permute-start | bytes 589832 | tf_op jit(solution)/shard_map/ppermute | solution.py:343
  6.0 10.6 %collective-permute-start.1 = (bf16[192,512]{1,0:T(8,128)(2,1)S(1)}, bf16[192,512]{1,0:T(8,128)(2,1)S(1)}, u32[]{:S(2)}, u32[]{:S(2)}) collective-permute-start(bf16[192,512]{1,0:T(8,128)(2,1)S(1)} %get-tuple-element.40), channel_id=1, source_target_pairs={{0,8},{4,12},{8,0},{12,4},{16,24},{20,28},{24,16},{28,20},{1,9},{5... | collective-permute-start | bytes 589832 | tf_op jit(solution)/shard_map/ppermute | solution.py:343
  6.5 17.0 %collective-permute-start.2 = (bf16[192,512]{1,0:T(8,128)(2,1)S(1)}, bf16[192,512]{1,0:T(8,128)(2,1)S(1)}, u32[]{:S(2)}, u32[]{:S(2)}) collective-permute-start(bf16[192,512]{1,0:T(8,128)(2,1)S(1)} %get-tuple-element.41), channel_id=1, source_target_pairs={{0,16},{4,20},{8,24},{12,28},{16,0},{20,4},{24,8},{28,12},{1,17},{... | collective-permute-start | bytes 589832 | tf_op jit(solution)/shard_map/ppermute | solution.py:343
  6.6 16.9 %collective-permute-start.3 = (bf16[192,512]{1,0:T(8,128)(2,1)S(1)}, bf16[192,512]{1,0:T(8,128)(2,1)S(1)}, u32[]{:S(2)}, u32[]{:S(2)}) collective-permute-start(bf16[192,512]{1,0:T(8,128)(2,1)S(1)} %get-tuple-element.42), channel_id=1, source_target_pairs={{0,28},{4,24},{8,20},{12,16},{16,12},{20,8},{24,4},{28,0},{1,29},{... | collective-permute-start | bytes 589832 | tf_op jit(solution)/shard_map/ppermute | solution.py:343
  8.1 15.5 %collective-permute-start.4 = (bf16[192,512]{1,0:T(8,128)(2,1)S(1)}, bf16[192,512]{1,0:T(8,128)(2,1)S(1)}, u32[]{:S(2)}, u32[]{:S(2)}) collective-permute-start(bf16[192,512]{1,0:T(8,128)(2,1)S(1)} %get-tuple-element.43), channel_id=1, source_target_pairs={{0,4},{4,0},{8,12},{12,8},{16,20},{20,16},{24,28},{28,24},{1,5},{5... | collective-permute-start | bytes 589832 | tf_op jit(solution)/shard_map/ppermute | solution.py:343
  15.6 7.9 %collective-permute-start.5 = (bf16[192,512]{1,0:T(8,128)(2,1)S(1)}, bf16[192,512]{1,0:T(8,128)(2,1)S(1)}, u32[]{:S(2)}, u32[]{:S(2)}) collective-permute-start(bf16[192,512]{1,0:T(8,128)(2,1)S(1)} %get-tuple-element.44), channel_id=1, source_target_pairs={{0,12},{4,8},{8,4},{12,0},{16,28},{20,24},{24,20},{28,16},{1,13},{... | collective-permute-start | bytes 589832 | tf_op jit(solution)/shard_map/ppermute | solution.py:343
  16.5 7.4 %collective-permute-start.6 = (bf16[192,512]{1,0:T(8,128)(2,1)S(1)}, bf16[192,512]{1,0:T(8,128)(2,1)S(1)}, u32[]{:S(2)}, u32[]{:S(2)}) collective-permute-start(bf16[192,512]{1,0:T(8,128)(2,1)S(1)} %get-tuple-element.45), channel_id=1, source_target_pairs={{0,20},{4,16},{8,28},{12,24},{16,4},{20,0},{24,12},{28,8},{1,21},{... | collective-permute-start | bytes 589832 | tf_op jit(solution)/shard_map/ppermute | solution.py:343
  56.4 33.2 %copy-start = (bf16[1536,1024]{1,0:T(8,128)(2,1)S(1)}, bf16[1536,1024]{1,0:T(8,128)(2,1)}, u32[]{:S(2)}) copy-start(bf16[1536,1024]{1,0:T(8,128)(2,1)} %get-tuple-element.37.turned_ref) | copy-start | bytes 9437188
  90.8 8.3 %collective-permute-start.7 = (bf16[192,512]{1,0:T(8,128)(2,1)S(1)}, bf16[192,512]{1,0:T(8,128)(2,1)S(1)}, u32[]{:S(2)}, u32[]{:S(2)}) collective-permute-start(bf16[192,512]{1,0:T(8,128)(2,1)S(1)} %get-tuple-element.48), channel_id=1, source_target_pairs={{0,24},{4,28},{8,16},{12,20},{16,8},{20,12},{24,0},{28,4},{1,25},{... | collective-permute-start | bytes 589832 | tf_op jit(solution)/shard_map/ppermute | solution.py:343
  93.2 10.0 %collective-permute-start.8 = (bf16[192,512]{1,0:T(8,128)(2,1)S(1)}, bf16[192,512]{1,0:T(8,128)(2,1)S(1)}, u32[]{:S(2)}, u32[]{:S(2)}) collective-permute-start(bf16[192,512]{1,0:T(8,128)(2,1)S(1)} %get-tuple-element.50), channel_id=1, source_target_pairs={{0,8},{4,12},{8,0},{12,4},{16,24},{20,28},{24,16},{28,20},{1,9},{5... | collective-permute-start | bytes 589832 | tf_op jit(solution)/shard_map/ppermute | solution.py:343
  93.8 10.8 %collective-permute-start.9 = (bf16[192,512]{1,0:T(8,128)(2,1)S(1)}, bf16[192,512]{1,0:T(8,128)(2,1)S(1)}, u32[]{:S(2)}, u32[]{:S(2)}) collective-permute-start(bf16[192,512]{1,0:T(8,128)(2,1)S(1)} %get-tuple-element.51), channel_id=1, source_target_pairs={{0,16},{4,20},{8,24},{12,28},{16,0},{20,4},{24,8},{28,12},{1,17},{... | collective-permute-start | bytes 589832 | tf_op jit(solution)/shard_map/ppermute | solution.py:343
  94.3 14.1 %collective-permute-start.10 = (bf16[192,512]{1,0:T(8,128)(2,1)S(1)}, bf16[192,512]{1,0:T(8,128)(2,1)S(1)}, u32[]{:S(2)}, u32[]{:S(2)}) collective-permute-start(bf16[192,512]{1,0:T(8,128)(2,1)S(1)} %get-tuple-element.52), channel_id=1, source_target_pairs={{0,28},{4,24},{8,20},{12,16},{16,12},{20,8},{24,4},{28,0},{1,29},{... | collective-permute-start | bytes 589832 | tf_op jit(solution)/shard_map/ppermute | solution.py:343
  99.9 8.6 %collective-permute-start.11 = (bf16[192,512]{1,0:T(8,128)(2,1)S(1)}, bf16[192,512]{1,0:T(8,128)(2,1)S(1)}, u32[]{:S(2)}, u32[]{:S(2)}) collective-permute-start(bf16[192,512]{1,0:T(8,128)(2,1)S(1)} %get-tuple-element.54), channel_id=1, source_target_pairs={{0,4},{4,0},{8,12},{12,8},{16,20},{20,16},{24,28},{28,24},{1,5},{5... | collective-permute-start | bytes 589832 | tf_op jit(solution)/shard_map/ppermute | solution.py:343
  100.7 11.5 %collective-permute-start.12 = (bf16[192,512]{1,0:T(8,128)(2,1)S(1)}, bf16[192,512]{1,0:T(8,128)(2,1)S(1)}, u32[]{:S(2)}, u32[]{:S(2)}) collective-permute-start(bf16[192,512]{1,0:T(8,128)(2,1)S(1)} %get-tuple-element.55), channel_id=1, source_target_pairs={{0,12},{4,8},{8,4},{12,0},{16,28},{20,24},{24,20},{28,16},{1,13},{... | collective-permute-start | bytes 589832 | tf_op jit(solution)/shard_map/ppermute | solution.py:343
  103.2 9.0 %collective-permute-start.13 = (bf16[192,512]{1,0:T(8,128)(2,1)S(1)}, bf16[192,512]{1,0:T(8,128)(2,1)S(1)}, u32[]{:S(2)}, u32[]{:S(2)}) collective-permute-start(bf16[192,512]{1,0:T(8,128)(2,1)S(1)} %get-tuple-element.56), channel_id=1, source_target_pairs={{0,20},{4,16},{8,28},{12,24},{16,4},{20,0},{24,12},{28,8},{1,21},{... | collective-permute-start | bytes 589832 | tf_op jit(solution)/shard_map/ppermute | solution.py:343

commit v5 on v4

--- a/solution.py
+++ b/solution.py
@@ -9,8 +9,10 @@
 
 LANES = 128
 SUBLANES = 8
-HELD = 24
-RING = 12
+HELD = 32
+GROUP = 4
+FETCHED = 14
+BESIDE = 0
 FIRST = 5
 LATE = 6
 PARTNERS = (0, 6, 2, 4, 7, 1, 3, 5)
@@ -131,10 +133,12 @@
     )(me, table, *blocks)
 
 
-def place_kernel(order_ref, table_hbm, owner_hbm, placed_ref, table, owner, chosen, table_sem, owner_sem):
+def place_kernel(order_ref, table_hbm, owner_hbm, inv_hbm, placed_ref, raw_ref, *scratch):
+    table, owner, chosen, table_sem, owner_sem, raw_sem = scratch
     owner_copy = pltpu.make_async_copy(owner_hbm, owner, owner_sem)
     table_copy = pltpu.make_async_copy(table_hbm, table, table_sem)
-    start(owner_copy, table_copy)
+    raw_copy = pltpu.make_async_copy(inv_hbm.at[: raw_ref.shape[0]], raw_ref, raw_sem)
+    start(owner_copy, table_copy, raw_copy)
     degrees = table.shape[0]
     order = order_ref[0]
     owner_copy.wait()
@@ -146,73 +150,100 @@
     table_copy.wait()
     for rows in tiles(degrees, 4):
         placed_ref[rows, :] = dot(chosen[rows, :], table[...]).astype(BF16)
-
-
-def place(order_ids, table, degree_owner):
+    raw_copy.wait()
+
+
+def place(order_ids, table, degree_owner, inverses, count):
     degrees, lats = table.shape
     return pl.pallas_call(
         place_kernel,
-        out_shape=jax.ShapeDtypeStruct((degrees, lats), BF16),
-        in_specs=[SMEM, HBM, HBM],
-        out_specs=VMEM,
+        out_shape=[
+            jax.ShapeDtypeStruct((degrees, lats), BF16),
+            pltpu.VMEM((count, *inverses.shape[1:]), BF16),
+        ],
+        in_specs=[SMEM, HBM, HBM, HBM],
+        out_specs=[VMEM, VMEM],
         scratch_shapes=[
             pltpu.VMEM(table.shape, BF16),
             pltpu.VMEM((1, degrees), jnp.int32),
             pltpu.VMEM((degrees, degrees), BF16),
             pltpu.SemaphoreType.DMA,
             pltpu.SemaphoreType.DMA,
+            pltpu.SemaphoreType.DMA,
         ],
         compiler_params=params(16),
         cost_estimate=cost(2 * degrees * degrees * lats, 4 * table.size),
-    )(order_ids, in_hbm(table), in_hbm(degree_owner.reshape(1, degrees)))
-
-
-def turn_kernel(table_ref, inv_hbm, turned_hbm, here_ref, turned, ring, sems, ring_sems):
-    degrees, slots = here_ref.shape[0], ring.shape[0]
-
-    def fetch(degree):
-        slot = degree % slots
-        return pltpu.make_async_copy(inv_hbm.at[degree], ring.at[slot], ring_sems.at[slot])
-
-    for degree in range(slots):
-        fetch(degree).start()
+    )(order_ids, in_hbm(table), in_hbm(degree_owner.reshape(1, degrees)), in_hbm(inverses))
+
+
+def transpose_by_product(target, source, unit):
+    size = unit.shape[0]
+    for i in range(0, source.shape[1], size):
+        for j in range(0, source.shape[0], size):
+            target[i : i + size, j : j + size] = lax.dot_general(
+                unit,
+                source[j : j + size, i : i + size],
+                (((1,), (1,)), ((), ())),
+                preferred_element_type=F32,
+            ).astype(BF16)
+
+
+def turn_kernel(table_ref, raw_ref, inv_hbm, turned_hbm, here_ref, turned, ring, sems, ring_sems):
+    ready, degrees = raw_ref.shape[0], here_ref.shape[0]
+    fetched = [
+        pltpu.make_async_copy(inv_hbm.at[ready + i], ring.at[i], ring_sems.at[i])
+        for i in range(degrees - ready)
+    ]
+    start(*fetched)
+    size = 2 * LANES
+    place = lax.broadcasted_iota(jnp.int32, (size, size), 0)
+    unit = (place == lax.broadcasted_iota(jnp.int32, (size, size), 1)).astype(F32).astype(BF16)
     copies = []
-    for i, rows in enumerate(tiles(turned.shape[0], 4)):
+    table_parts = tiles(turned.shape[0], 4)
+    each = BESIDE // len(table_parts)
+    for i, rows in enumerate(table_parts):
+        for degree in range(i * each, (i + 1) * each):
+            transpose_by_product(here_ref.at[degree], raw_ref.at[degree], unit)
         turned[rows, :] = table_ref[:, rows.start : rows.start + rows.size].T
         copies.append(pltpu.make_async_copy(turned.at[rows], turned_hbm.at[rows], sems.at[i]))
         copies[-1].start()
-    for degree in range(degrees):
-        fetch(degree).wait()
-        here_ref[degree] = ring[degree % slots].T
-        if degree + slots < degrees:
-            fetch(degree + slots).start()
+    for first in range(BESIDE, degrees, GROUP):
+        group = range(first, min(first + GROUP, degrees))
+        wait(*[fetched[degree - ready] for degree in group if degree >= ready])
+        for degree in group:
+            source = raw_ref.at[degree] if degree < ready else ring.at[degree - ready]
+            if degree % 2:
+                transpose_by_product(here_ref.at[degree], source, unit)
+            else:
+                here_ref[degree] = source[...].T
     wait(*copies)
 
 
-def turn(table, inverses, count):
+def turn(table, raw, inverses, count):
     turned = table.shape[::-1]
     radii = inverses.shape[1:]
+    ring = count - raw.shape[0]
     return pl.pallas_call(
         turn_kernel,
         out_shape=[pltpu.HBM(turned, BF16), pltpu.VMEM((count, *radii), BF16)],
-        in_specs=[VMEM, HBM],
+        in_specs=[VMEM, VMEM, HBM],
         out_specs=[HBM, VMEM],
         scratch_shapes=[
             pltpu.VMEM(turned, BF16),
-            pltpu.VMEM((RING, *radii), BF16),
+            pltpu.VMEM((ring, *radii), BF16),
             pltpu.SemaphoreType.DMA((4,)),
-            pltpu.SemaphoreType.DMA((RING,)),
+            pltpu.SemaphoreType.DMA((ring,)),
         ],
         compiler_params=params(16),
         cost_estimate=cost(table.size, 4 * table.size + 4 * inverses.size),
-    )(table, in_hbm(inverses))
+    )(table, in_vmem(raw), in_hbm(inverses))
 
 
 def solve_kernel(orders, shards, members, x_ref, here_ref, inv_hbm, y_ref, x32, y32, inv, sems):
     degrees, held = inv_hbm.shape[0], here_ref.shape[0]
-    parts = fetches(inv_hbm.at[held:], inv, sems)
+    parts = fetches(inv_hbm.at[held:], inv, sems) if held < degrees else []
     start(*[copy for _, copy in parts])
-    each = (degrees - held) // len(parts)
+    each = (degrees - held) // max(len(parts), 1)
     block = shards * degrees
     stride = block + 1
     half = degrees // 2
@@ -266,7 +297,7 @@
 def solve(owned, here, inverses, orders, shards, members):
     rows, columns = owned.shape
     degrees, radii, _ = inverses.shape
-    rest = degrees - here.shape[0]
+    rest = max(degrees - here.shape[0], 4)
     return pl.pallas_call(
         functools.partial(solve_kernel, orders, shards, members),
         out_shape=jax.ShapeDtypeStruct((rows, columns), BF16),
@@ -361,24 +392,21 @@
     me = lax.axis_index("row").astype(jnp.int32).reshape(1)
 
     weighted = list(weigh(me, field, coef))
-    placed = place(order_ids, table[0], degree_owner)
+    placed, raw = place(order_ids, table[0], degree_owner, inverses, FETCHED)
     placed, *weighted[LATE:] = lax.optimization_barrier((placed, *weighted[LATE:]))
     arrived = exchange_rows(weighted, PARTNERS)
-    turned, here = turn(placed, inverses, HELD)
+    turned, here = turn(placed, raw, inverses, HELD)
     here, turned, arrived[0] = lax.optimization_barrier((here, turned, arrived[0]))
     spectral = analyse(me, placed, arrived)
     owned = exchange_degrees(spectral.reshape(n_row * n_col, deg_dev, columns))
     solved = solve(owned.reshape(degrees_all, columns), here, inverses, orders, n_col, members)
     coeffs = exchange_degrees(solved.reshape(n_row * n_col, deg_dev, columns))
     coeffs = coeffs.reshape(degrees_all, columns)
-    outputs = synthesise(me, turned, coeffs, PARTNERS[:FIRST])
-    received = exchange_rows(outputs, PARTNERS[:FIRST])
-    if FIRST < len(PARTNERS):
-        quick = 1
-        received[quick], coeffs = lax.optimization_barrier((received[quick], coeffs))
-        outputs = synthesise(me, turned, coeffs, PARTNERS[FIRST:])
-        received += exchange_rows(outputs, PARTNERS[FIRST:])
-    return assemble(me, received, field.shape)
+    early, late = PARTNERS[1:FIRST], PARTNERS[:1] + PARTNERS[FIRST:]
+    received = exchange_rows(synthesise(me, turned, coeffs, early), early)
+    received[0], coeffs = lax.optimization_barrier((received[0], coeffs))
+    own, *rest = exchange_rows(synthesise(me, turned, coeffs, late), late)
+    return assemble(me, [own, *received, *rest], field.shape)
 
 
 def general(field, coef, table, order_ids, inverses, degree_owner):
@@ -434,7 +462,9 @@
     orders, lats, _, _, radii_dev = field.shape
     n_row = lax.axis_size("row")
     fits = (
-        orders == n_row == SUBLANES
+        orders == n_row == len(PARTNERS) == SUBLANES
+        and inverses.shape[0] >= HELD
+        and inverses.shape[1] % (2 * LANES) == 0
         and radii_dev == LANES
         and lats % 16 == 0
         and inverses.shape[0] % 16 == 0

time: 114 us -> 113 us (level)
  Pallas kernels: 23.3 us -> 21.2 us
  waiting for transfers between devices: 13.1 us -> 14.3 us
    pallas_call x1, Pallas kernels: 6.96 us -> 5.64 us  [turn(): pl.pallas_call(turn_kernel, out_shape=[pltpu.HBM(turned, BF16), pltpu.VME...]
  transfers between devices with their start and end apart: 14 -> 14, of which waited for: 6 -> 7; matrix products, arithmetic and copies ran while one was open for 0% -> 0% of each run, Pallas kernels for 12% -> 11%
where the time goes in v5:
time: 113 us
  blocking collectives  59.8 us (53%)
  Pallas kernels  21.2 us (19%)
  starting transfers between devices  16.4 us (15%)
  waiting for transfers between devices  14.3 us (13%)
    all_to_all x2, blocking collectives, exchange_degrees(): lax.all_to_all(blocks, ('row', 'col'), split_axis=0, concat_axis=0, tiled...  59.8 us
    ppermute x14, starting transfers between devices, exchange_rows(): lax.ppermute(block, 'row', [(a, a ^ j) for a in range(n)])  16.4 us
    ppermute x14, waiting for transfers between devices, exchange_rows(): lax.ppermute(block, 'row', [(a, a ^ j) for a in range(n)])  14.3 us
    pallas_call x1, Pallas kernels, turn(): pl.pallas_call(turn_kernel, out_shape=[pltpu.HBM(turned, BF16), pltpu.VME...  5.64 us
    pallas_call x1, Pallas kernels, place(): pl.pallas_call(place_kernel, out_shape=[jax.ShapeDtypeStruct((degrees, la...  5.36 us
    pallas_call x1, Pallas kernels, solve(): pl.pallas_call(functools.partial(solve_kernel, orders, shards, members),...  3.1 us
  transfers between devices with their start and end apart: 14, of which 7 were waited for; matrix products, arithmetic and copies ran while one was open for 0% of the time, Pallas kernels for 11%

profile of v5, /device:TPU:0, one launch (start us, length us, event | category | flops | bytes accessed | tf_op | source)
XLA Modules:
  0.0 112.5 jit_solution(14013992245512435299)
XLA Ops:
  0.0 2.0 %shard_map.65 = (bf16[192,512]{1,0:T(8,128)(2,1)S(1)}, bf16[192,512]{1,0:T(8,128)(2,1)S(1)}, bf16[192,512]{1,0:T(8,128)(2,1)S(1)}, bf16[192,512]{1,0:T(8,128)(2,...) custom-call(s32[1]{0:T(128)} %bitcast.me_ref, ...), custom_call_target="tpu_custom_call" | custom-call | flops 786432 | bytes 3145728 | tf_op jit(solution)/shard_map/pallas_call | solution.py:96
  2.0 4.0 %collective-permute-start = (bf16[192,512]{1,0:T(8,128)(2,1)S(1)}, bf16[192,512]{1,0:T(8,128)(2,1)S(1)}, u32[]{:S(2)}, u32[]{:S(2)}) collective-permute-start(bf16[192,512]{1,0:T(8,128)(2,1)S(1)} %get-tuple-element.43), channel_id=1, source_target_pairs={{0,24},{4,28},{8,16},{12,20},{16,8},{20,12},{24,0},{28,4},{1,25},{... | collective-permute-start | bytes 589832 | tf_op jit(solution)/shard_map/ppermute | solution.py:374
  6.0 0.5 collective-permute-start.1
  6.5 0.1 collective-permute-start.2
  6.6 1.4 %collective-permute-start.3 = (bf16[192,512]{1,0:T(8,128)(2,1)S(1)}, bf16[192,512]{1,0:T(8,128)(2,1)S(1)}, u32[]{:S(2)}, u32[]{:S(2)}) collective-permute-start(bf16[192,512]{1,0:T(8,128)(2,1)S(1)} %get-tuple-element.46), channel_id=1, source_target_pairs={{0,28},{4,24},{8,20},{12,16},{16,12},{20,8},{24,4},{28,0},{1,29},{... | collective-permute-start | bytes 589832 | tf_op jit(solution)/shard_map/ppermute | solution.py:374
  8.1 1.5 %collective-permute-start.4 = (bf16[192,512]{1,0:T(8,128)(2,1)S(1)}, bf16[192,512]{1,0:T(8,128)(2,1)S(1)}, u32[]{:S(2)}, u32[]{:S(2)}) collective-permute-start(bf16[192,512]{1,0:T(8,128)(2,1)S(1)} %get-tuple-element.47), channel_id=1, source_target_pairs={{0,4},{4,0},{8,12},{12,8},{16,20},{20,16},{24,28},{28,24},{1,5},{5... | collective-permute-start | bytes 589832 | tf_op jit(solution)/shard_map/ppermute | solution.py:374
  10.2 5.4 %shard_map.64 = (bf16[1024,1536]{1,0:T(8,128)(2,1)S(1)}, bf16[14,512,512]{2,1,0:T(8,128)(2,1)S(1)}) custom-call(s32[1]{0:T(128)S(6)} %copy.7.order_ref, bf16[1024,1536]{1,0:T(8,128)(2,1)} %bitcast.14, s32[1,1024]{1,0:T(1,128)} %bitcast.16, bf16[32,512,512]{2,1,0:T(8,128)(2,1)} %inv_hbm.5), custom_call_target="tpu_custom_call" | custom-call | flops 3221225472 | bytes 6291456 | tf_op jit(solution)/shard_map/pallas_call | solution.py:158
  15.6 0.0 collective-permute-done.rest_1_
  15.6 0.2 collective-permute-start.5
  15.8 0.7 collective-permute-done.1.rest_2_
  16.5 0.0 collective-permute-start.6
  16.5 5.6 %shard_map.66 = (bf16[1536,1024]{1,0:T(8,128)(2,1)}, bf16[32,512,512]{2,1,0:T(8,128)(2,1)S(1)}) custom-call(bf16[1024,1536]{1,0:T(8,128)(2,1)S(1)} %get-tuple-element.36.table_ref, bf16[14,512,512]{2,1,0:T(8,128)(2,1)S(1)} %get-tuple-element.37.raw_ref, bf16[32,512,512]{2,1,0:T(8,128)(2,1)} %inv_hbm.5), custom_call_target="tpu_custom_call" | custom-call | flops 1572864 | bytes 39845888 | tf_op jit(solution)/shard_map/pallas_call | solution.py:226
  22.2 0.7 collective-permute-done.5.rest_6_
  22.9 1.0 collective-permute-done.6.rest_7_
  24.0 1.9 %shard_map.67 = bf16[1024,512]{1,0:T(8,128)(2,1)S(1)} custom-call(s32[1]{0:T(128)} %bitcast.me_ref, bf16[1024,1536]{1,0:T(8,128)(2,1)S(1)} %get-tuple-element.36.table_ref, bf16[192,512]{1,0:T(8,128)(2,1)S(1)} %get-tuple-element.42.rest_0_, bf16[192,512]{1,0:T(8,128)(2,1)S(1)} %collective-permute-done.rest_1_, ...), custom_call_target="tpu_custom_call" | custom-call | flops 1610612736 | bytes 3145728 | tf_op jit(solution)/shard_map/pallas_call | solution.py:125
  25.9 30.5 %all_to_all.10 = bf16[32,32,512]{2,1,0:T(8,128)(2,1)S(1)} all-to-all(bf16[32,32,512]{2,1,0:T(8,128)(2,1)S(1)} %bitcast.13), channel_id=1, replica_groups=mesh['row'=8,'col'=4] {'row','col'}, dimensions={0} | all-to-all | bytes 2097152 | tf_op jit(solution)/shard_map/all_to_all | solution.py:380
  56.4 3.1 %shard_map.68 = bf16[1024,512]{1,0:T(8,128)(2,1)S(1)} custom-call(bf16[1024,512]{1,0:T(8,128)(2,1)S(1)} %bitcast.11, bf16[32,512,512]{2,1,0:T(8,128)(2,1)S(1)} %get-tuple-element.50.here_ref, bf16[32,512,512]{2,1,0:T(8,128)(2,1)} %inv_hbm.5), custom_call_target="tpu_custom_call" | custom-call | flops 536870912 | bytes 8388608 | tf_op jit(solution)/shard_map/pallas_call | solution.py:301
  59.5 29.3 %all_to_all.11 = bf16[32,32,512]{2,1,0:T(8,128)(2,1)S(1)} all-to-all(bf16[32,32,512]{2,1,0:T(8,128)(2,1)S(1)} %bitcast.12), channel_id=1, replica_groups=mesh['row'=8,'col'=4] {'row','col'}, dimensions={0} | all-to-all | bytes 2097152 | tf_op jit(solution)/shard_map/all_to_all | solution.py:380
  88.8 1.0 shard_map.69
  89.8 2.5 %collective-permute-start.7 = (bf16[192,512]{1,0:T(8,128)(2,1)S(1)}, bf16[192,512]{1,0:T(8,128)(2,1)S(1)}, u32[]{:S(2)}, u32[]{:S(2)}) collective-permute-start(bf16[192,512]{1,0:T(8,128)(2,1)S(1)} %get-tuple-element.51), channel_id=1, source_target_pairs={{0,24},{4,28},{8,16},{12,20},{16,8},{20,12},{24,0},{28,4},{1,25},{... | collective-permute-start | bytes 589832 | tf_op jit(solution)/shard_map/ppermute | solution.py:374
  92.2 0.5 collective-permute-start.8
  92.8 0.6 collective-permute-start.9
  93.3 1.8 %collective-permute-start.10 = (bf16[192,512]{1,0:T(8,128)(2,1)S(1)}, bf16[192,512]{1,0:T(8,128)(2,1)S(1)}, u32[]{:S(2)}, u32[]{:S(2)}) collective-permute-start(bf16[192,512]{1,0:T(8,128)(2,1)S(1)} %get-tuple-element.57), channel_id=1, source_target_pairs={{0,28},{4,24},{8,20},{12,16},{16,12},{20,8},{24,4},{28,0},{1,29},{... | collective-permute-start | bytes 589832 | tf_op jit(solution)/shard_map/ppermute | solution.py:374
  95.1 3.0 %collective-permute-done.7.rest_1_ = bf16[192,512]{1,0:T(8,128)(2,1)S(1)} collective-permute-done((bf16[192,512]{1,0:T(8,128)(2,1)S(1)}, bf16[192,512]{1,0:T(8,128)(2,1)S(1)}, u32[]{:S(2)}, u32[]{:S(2)}) %collective-permute-start.7) | collective-permute-done | bytes 196640 | tf_op jit(solution)/shard_map/ppermute | solution.py:374
  98.1 1.0 shard_map.70
  99.1 0.8 collective-permute-start.11
  99.9 1.2 %collective-permute-start.12 = (bf16[192,512]{1,0:T(8,128)(2,1)S(1)}, bf16[192,512]{1,0:T(8,128)(2,1)S(1)}, u32[]{:S(2)}, u32[]{:S(2)}) collective-permute-start(bf16[192,512]{1,0:T(8,128)(2,1)S(1)} %get-tuple-element.59), channel_id=1, source_target_pairs={{0,12},{4,8},{8,4},{12,0},{16,28},{20,24},{24,20},{28,16},{1,13},{... | collective-permute-start | bytes 589832 | tf_op jit(solution)/shard_map/ppermute | solution.py:374
  101.1 1.1 %collective-permute-done.8.rest_2_ = bf16[192,512]{1,0:T(8,128)(2,1)S(1)} collective-permute-done((bf16[192,512]{1,0:T(8,128)(2,1)S(1)}, bf16[192,512]{1,0:T(8,128)(2,1)S(1)}, u32[]{:S(2)}, u32[]{:S(2)}) %collective-permute-start.8) | collective-permute-done | bytes 196640 | tf_op jit(solution)/shard_map/ppermute | solution.py:374
  102.2 1.3 %collective-permute-start.13 = (bf16[192,512]{1,0:T(8,128)(2,1)S(1)}, bf16[192,512]{1,0:T(8,128)(2,1)S(1)}, u32[]{:S(2)}, u32[]{:S(2)}) collective-permute-start(bf16[192,512]{1,0:T(8,128)(2,1)S(1)} %get-tuple-element.60), channel_id=1, source_target_pairs={{0,20},{4,16},{8,28},{12,24},{16,4},{20,0},{24,12},{28,8},{1,21},{... | collective-permute-start | bytes 589832 | tf_op jit(solution)/shard_map/ppermute | solution.py:374
  103.5 3.9 %collective-permute-done.10.rest_4_ = bf16[192,512]{1,0:T(8,128)(2,1)S(1)} collective-permute-done((bf16[192,512]{1,0:T(8,128)(2,1)S(1)}, bf16[192,512]{1,0:T(8,128)(2,1)S(1)}, u32[]{:S(2)}, u32[]{:S(2)}) %collective-permute-start.10) | collective-permute-done | bytes 196640 | tf_op jit(solution)/shard_map/ppermute | solution.py:374
  107.5 3.7 %collective-permute-done.12.rest_6_ = bf16[192,512]{1,0:T(8,128)(2,1)S(1)} collective-permute-done((bf16[192,512]{1,0:T(8,128)(2,1)S(1)}, bf16[192,512]{1,0:T(8,128)(2,1)S(1)}, u32[]{:S(2)}, u32[]{:S(2)}) %collective-permute-start.12) | collective-permute-done | bytes 196640 | tf_op jit(solution)/shard_map/ppermute | solution.py:374
  111.2 1.3 %shard_map.71 = bf16[6144,128]{1,0:T(8,128)(2,1)} custom-call(s32[1]{0:T(128)} %bitcast.me_ref, bf16[192,512]{1,0:T(8,128)(2,1)S(1)} %get-tuple-element.53.rest_0_, bf16[192,512]{1,0:T(8,128)(2,1)S(1)} %collective-permute-done.7.rest_1_, bf16[192,512]{1,0:T(8,128)(2,1)S(1)} %collective-permute-done.8.rest_2_, ...), custom_call_target="tpu_custom_call" | custom-call | flops 786432 | bytes 3145728 | tf_op jit(solution)/shard_map/pallas_call | solution.py:355
  (8 shorter events, 0.0 us)
Async XLA Ops:
  2.0 13.6 %collective-permute-start = (bf16[192,512]{1,0:T(8,128)(2,1)S(1)}, bf16[192,512]{1,0:T(8,128)(2,1)S(1)}, u32[]{:S(2)}, u32[]{:S(2)}) collective-permute-start(bf16[192,512]{1,0:T(8,128)(2,1)S(1)} %get-tuple-element.43), channel_id=1, source_target_pairs={{0,24},{4,28},{8,16},{12,20},{16,8},{20,12},{24,0},{28,4},{1,25},{... | collective-permute-start | bytes 589832 | tf_op jit(solution)/shard_map/ppermute | solution.py:374
  6.0 10.6 %collective-permute-start.1 = (bf16[192,512]{1,0:T(8,128)(2,1)S(1)}, bf16[192,512]{1,0:T(8,128)(2,1)S(1)}, u32[]{:S(2)}, u32[]{:S(2)}) collective-permute-start(bf16[192,512]{1,0:T(8,128)(2,1)S(1)} %get-tuple-element.44), channel_id=1, source_target_pairs={{0,8},{4,12},{8,0},{12,4},{16,24},{20,28},{24,16},{28,20},{1,9},{5... | collective-permute-start | bytes 589832 | tf_op jit(solution)/shard_map/ppermute | solution.py:374
  6.5 15.7 %collective-permute-start.2 = (bf16[192,512]{1,0:T(8,128)(2,1)S(1)}, bf16[192,512]{1,0:T(8,128)(2,1)S(1)}, u32[]{:S(2)}, u32[]{:S(2)}) collective-permute-start(bf16[192,512]{1,0:T(8,128)(2,1)S(1)} %get-tuple-element.45), channel_id=1, source_target_pairs={{0,16},{4,20},{8,24},{12,28},{16,0},{20,4},{24,8},{28,12},{1,17},{... | collective-permute-start | bytes 589832 | tf_op jit(solution)/shard_map/ppermute | solution.py:374
  6.6 15.6 %collective-permute-start.3 = (bf16[192,512]{1,0:T(8,128)(2,1)S(1)}, bf16[192,512]{1,0:T(8,128)(2,1)S(1)}, u32[]{:S(2)}, u32[]{:S(2)}) collective-permute-start(bf16[192,512]{1,0:T(8,128)(2,1)S(1)} %get-tuple-element.46), channel_id=1, source_target_pairs={{0,28},{4,24},{8,20},{12,16},{16,12},{20,8},{24,4},{28,0},{1,29},{... | collective-permute-start | bytes 589832 | tf_op jit(solution)/shard_map/ppermute | solution.py:374
  8.1 14.1 %collective-permute-start.4 = (bf16[192,512]{1,0:T(8,128)(2,1)S(1)}, bf16[192,512]{1,0:T(8,128)(2,1)S(1)}, u32[]{:S(2)}, u32[]{:S(2)}) collective-permute-start(bf16[192,512]{1,0:T(8,128)(2,1)S(1)} %get-tuple-element.47), channel_id=1, source_target_pairs={{0,4},{4,0},{8,12},{12,8},{16,20},{20,16},{24,28},{28,24},{1,5},{5... | collective-permute-start | bytes 589832 | tf_op jit(solution)/shard_map/ppermute | solution.py:374
  15.6 7.3 %collective-permute-start.5 = (bf16[192,512]{1,0:T(8,128)(2,1)S(1)}, bf16[192,512]{1,0:T(8,128)(2,1)S(1)}, u32[]{:S(2)}, u32[]{:S(2)}) collective-permute-start(bf16[192,512]{1,0:T(8,128)(2,1)S(1)} %get-tuple-element.48), channel_id=1, source_target_pairs={{0,12},{4,8},{8,4},{12,0},{16,28},{20,24},{24,20},{28,16},{1,13},{... | collective-permute-start | bytes 589832 | tf_op jit(solution)/shard_map/ppermute | solution.py:374
  16.5 7.4 %collective-permute-start.6 = (bf16[192,512]{1,0:T(8,128)(2,1)S(1)}, bf16[192,512]{1,0:T(8,128)(2,1)S(1)}, u32[]{:S(2)}, u32[]{:S(2)}) collective-permute-start(bf16[192,512]{1,0:T(8,128)(2,1)S(1)} %get-tuple-element.49), channel_id=1, source_target_pairs={{0,20},{4,16},{8,28},{12,24},{16,4},{20,0},{24,12},{28,8},{1,21},{... | collective-permute-start | bytes 589832 | tf_op jit(solution)/shard_map/ppermute | solution.py:374
  56.4 32.4 %copy-start = (bf16[1536,1024]{1,0:T(8,128)(2,1)S(1)}, bf16[1536,1024]{1,0:T(8,128)(2,1)}, u32[]{:S(2)}) copy-start(bf16[1536,1024]{1,0:T(8,128)(2,1)} %get-tuple-element.41.turned_ref) | copy-start | bytes 9437188
  89.8 8.3 %collective-permute-start.7 = (bf16[192,512]{1,0:T(8,128)(2,1)S(1)}, bf16[192,512]{1,0:T(8,128)(2,1)S(1)}, u32[]{:S(2)}, u32[]{:S(2)}) collective-permute-start(bf16[192,512]{1,0:T(8,128)(2,1)S(1)} %get-tuple-element.51), channel_id=1, source_target_pairs={{0,24},{4,28},{8,16},{12,20},{16,8},{20,12},{24,0},{28,4},{1,25},{... | collective-permute-start | bytes 589832 | tf_op jit(solution)/shard_map/ppermute | solution.py:374
  92.2 10.0 %collective-permute-start.8 = (bf16[192,512]{1,0:T(8,128)(2,1)S(1)}, bf16[192,512]{1,0:T(8,128)(2,1)S(1)}, u32[]{:S(2)}, u32[]{:S(2)}) collective-permute-start(bf16[192,512]{1,0:T(8,128)(2,1)S(1)} %get-tuple-element.55), channel_id=1, source_target_pairs={{0,8},{4,12},{8,0},{12,4},{16,24},{20,28},{24,16},{28,20},{1,9},{5... | collective-permute-start | bytes 589832 | tf_op jit(solution)/shard_map/ppermute | solution.py:374
  92.8 10.8 %collective-permute-start.9 = (bf16[192,512]{1,0:T(8,128)(2,1)S(1)}, bf16[192,512]{1,0:T(8,128)(2,1)S(1)}, u32[]{:S(2)}, u32[]{:S(2)}) collective-permute-start(bf16[192,512]{1,0:T(8,128)(2,1)S(1)} %get-tuple-element.56), channel_id=1, source_target_pairs={{0,16},{4,20},{8,24},{12,28},{16,0},{20,4},{24,8},{28,12},{1,17},{... | collective-permute-start | bytes 589832 | tf_op jit(solution)/shard_map/ppermute | solution.py:374
  93.3 14.1 %collective-permute-start.10 = (bf16[192,512]{1,0:T(8,128)(2,1)S(1)}, bf16[192,512]{1,0:T(8,128)(2,1)S(1)}, u32[]{:S(2)}, u32[]{:S(2)}) collective-permute-start(bf16[192,512]{1,0:T(8,128)(2,1)S(1)} %get-tuple-element.57), channel_id=1, source_target_pairs={{0,28},{4,24},{8,20},{12,16},{16,12},{20,8},{24,4},{28,0},{1,29},{... | collective-permute-start | bytes 589832 | tf_op jit(solution)/shard_map/ppermute | solution.py:374
  99.1 8.4 %collective-permute-start.11 = (bf16[192,512]{1,0:T(8,128)(2,1)S(1)}, bf16[192,512]{1,0:T(8,128)(2,1)S(1)}, u32[]{:S(2)}, u32[]{:S(2)}) collective-permute-start(bf16[192,512]{1,0:T(8,128)(2,1)S(1)} %get-tuple-element.58), channel_id=1, source_target_pairs={{0,4},{4,0},{8,12},{12,8},{16,20},{20,16},{24,28},{28,24},{1,5},{5... | collective-permute-start | bytes 589832 | tf_op jit(solution)/shard_map/ppermute | solution.py:374
  99.9 11.3 %collective-permute-start.12 = (bf16[192,512]{1,0:T(8,128)(2,1)S(1)}, bf16[192,512]{1,0:T(8,128)(2,1)S(1)}, u32[]{:S(2)}, u32[]{:S(2)}) collective-permute-start(bf16[192,512]{1,0:T(8,128)(2,1)S(1)} %get-tuple-element.59), channel_id=1, source_target_pairs={{0,12},{4,8},{8,4},{12,0},{16,28},{20,24},{24,20},{28,16},{1,13},{... | collective-permute-start | bytes 589832 | tf_op jit(solution)/shard_map/ppermute | solution.py:374
  102.2 9.0 %collective-permute-start.13 = (bf16[192,512]{1,0:T(8,128)(2,1)S(1)}, bf16[192,512]{1,0:T(8,128)(2,1)S(1)}, u32[]{:S(2)}, u32[]{:S(2)}) collective-permute-start(bf16[192,512]{1,0:T(8,128)(2,1)S(1)} %get-tuple-element.60), channel_id=1, source_target_pairs={{0,20},{4,16},{8,28},{12,24},{16,4},{20,0},{24,12},{28,8},{1,21},{... | collective-permute-start | bytes 589832 | tf_op jit(solution)/shard_map/ppermute | solution.py:374

commit v6 on v5

--- a/solution.py
+++ b/solution.py
@@ -9,9 +9,9 @@
 
 LANES = 128
 SUBLANES = 8
-HELD = 32
+HELD = 28
 GROUP = 4
-FETCHED = 14
+FETCHED = 16
 BESIDE = 0
 FIRST = 5
 LATE = 6
@@ -113,10 +113,16 @@
 def analyse_kernel(me_ref, table_ref, *rest):
     blocks, (out_ref, w) = rest[:-2], rest[-2:]
     lats = blocks[0].shape[0]
-    for j, block in enumerate(blocks):
-        w[pl.ds(pl.multiple_of((me_ref[0] ^ PARTNERS[j]) * lats, lats), lats), :] = block[...]
-    for rows in tiles(table_ref.shape[0], 4):
-        out_ref[rows, :] = dot(table_ref[rows, :], w[...]).astype(BF16)
+
+    def rows(j):
+        return pl.ds(pl.multiple_of((me_ref[0] ^ j) * lats, lats), lats)
+
+    for j, block in zip(PARTNERS, blocks):
+        w[rows(j), :] = block[...]
+    for j in PARTNERS[len(blocks) :]:
+        w[rows(j), :] = jnp.zeros(blocks[0].shape, BF16)
+    for part in tiles(table_ref.shape[0], 4):
+        out_ref[part, :] = dot(table_ref[part, :], w[...])
 
 
 def analyse(me, table, blocks):
@@ -124,13 +130,44 @@
     columns = blocks[0].shape[1]
     return pl.pallas_call(
         analyse_kernel,
-        out_shape=jax.ShapeDtypeStruct((rows, columns), BF16),
+        out_shape=jax.ShapeDtypeStruct((rows, columns), F32),
         in_specs=[SMEM] + [VMEM] * (1 + len(blocks)),
         out_specs=VMEM,
         scratch_shapes=[pltpu.VMEM((lats, columns), BF16)],
         compiler_params=params(14),
         cost_estimate=cost(2 * rows * lats * columns, 2 * rows * lats),
     )(me, table, *blocks)
+
+
+def add_rest_kernel(partners, me_ref, table_ref, sums_ref, *refs):
+    blocks, (out_ref, w) = refs[:-2], refs[-2:]
+    lats = blocks[0].shape[0]
+    windows = []
+    for i, (j, block) in enumerate(zip(partners, blocks)):
+        at = me_ref[0] ^ j
+        w[i] = jnp.zeros(w.shape[1:], BF16)
+        w[i, pl.ds(pl.multiple_of(at % 2 * lats, lats), lats), :] = block[...]
+        windows.append(pl.ds(pl.multiple_of(at // 2 * (2 * lats), 2 * lats), 2 * lats))
+    for part in tiles(table_ref.shape[0], 4):
+        total = sums_ref[part, :]
+        for i, window in enumerate(windows):
+            total = total + dot(table_ref[part, window], w[i])
+        out_ref[part, :] = total.astype(BF16)
+
+
+def add_rest(me, table, sums, blocks):
+    rows, columns = sums.shape
+    lats = blocks[0].shape[0]
+    count = len(blocks)
+    return pl.pallas_call(
+        functools.partial(add_rest_kernel, PARTNERS[-count:]),
+        out_shape=jax.ShapeDtypeStruct((rows, columns), BF16),
+        in_specs=[SMEM] + [VMEM] * (2 + count),
+        out_specs=VMEM,
+        scratch_shapes=[pltpu.VMEM((count, 2 * lats, columns), BF16)],
+        compiler_params=params(14),
+        cost_estimate=cost(4 * rows * lats * columns * count, 4 * rows * lats * count),
+    )(me, table, sums, *blocks)
 
 
 def place_kernel(order_ref, table_hbm, owner_hbm, inv_hbm, placed_ref, raw_ref, *scratch):
@@ -331,41 +368,43 @@
     )(me, turned, coeffs)
 
 
-def assemble_kernel(members, me_ref, *rest):
-    blocks, (out_hbm, y32, y16, out_sems) = rest[:-4], rest[-4:]
+def assemble_kernel(members, partners, me_ref, *rest):
+    blocks, (out_hbm, y32, y16, out_sems) = rest[-4 - len(partners) : -4], rest[-4:]
     lats = blocks[0].shape[0]
     block = lats * members
     copies = []
-    for j, x_ref in enumerate(blocks):
-        slot = j % 2
+    for i, (j, x_ref) in enumerate(zip(partners, blocks)):
+        slot = i % 2
         for m in range(members):
             part = x_ref[:, m * LANES : (m + 1) * LANES].astype(F32)
             y32[slot, pl.ds(m, lats, stride=members), :] = part
-        y16[j] = y32[slot, :block].astype(BF16)
-        rows = pl.ds(pl.multiple_of((me_ref[0] ^ PARTNERS[j]) * block, block), block)
-        copies.append(pltpu.make_async_copy(y16.at[j], out_hbm.at[rows], out_sems.at[j]))
+        y16[i] = y32[slot, :block].astype(BF16)
+        rows = pl.ds(pl.multiple_of((me_ref[0] ^ j) * block, block), block)
+        copies.append(pltpu.make_async_copy(y16.at[i], out_hbm.at[rows], out_sems.at[i]))
         copies[-1].start()
     wait(*copies)
 
 
-def assemble(me, received, shape):
+def assemble(me, received, partners, shape, so_far=None):
     orders, lats, groups, parts, _ = shape
     members = groups * parts
     block = lats * members
-    out = pl.pallas_call(
-        functools.partial(assemble_kernel, members),
+    count = len(partners)
+    before = [] if so_far is None else [in_hbm(so_far)]
+    return pl.pallas_call(
+        functools.partial(assemble_kernel, members, partners),
         out_shape=pltpu.HBM((orders * block, LANES), BF16),
-        in_specs=[SMEM] + [VMEM] * orders,
+        in_specs=[SMEM] + [HBM] * len(before) + [VMEM] * count,
         out_specs=HBM,
+        input_output_aliases={1: 0} if before else {},
         scratch_shapes=[
             pltpu.VMEM((2, block + SUBLANES, LANES), F32),
-            pltpu.VMEM((orders, block, LANES), BF16),
-            pltpu.SemaphoreType.DMA((orders,)),
+            pltpu.VMEM((count, block, LANES), BF16),
+            pltpu.SemaphoreType.DMA((count,)),
         ],
         compiler_params=params(12),
-        cost_estimate=cost(orders * block * LANES, orders * block * LANES * 4),
-    )(me, *received)
-    return out.reshape(shape)
+        cost_estimate=cost(count * block * LANES, count * block * LANES * 4),
+    )(me, *before, *received)
 
 
 def exchange_rows(blocks, partners):
@@ -397,7 +436,8 @@
     arrived = exchange_rows(weighted, PARTNERS)
     turned, here = turn(placed, raw, inverses, HELD)
     here, turned, arrived[0] = lax.optimization_barrier((here, turned, arrived[0]))
-    spectral = analyse(me, placed, arrived)
+    sums = analyse(me, placed, arrived[:LATE])
+    spectral = add_rest(me, placed, sums, arrived[LATE:])
     owned = exchange_degrees(spectral.reshape(n_row * n_col, deg_dev, columns))
     solved = solve(owned.reshape(degrees_all, columns), here, inverses, orders, n_col, members)
     coeffs = exchange_degrees(solved.reshape(n_row * n_col, deg_dev, columns))
@@ -406,7 +446,10 @@
     received = exchange_rows(synthesise(me, turned, coeffs, early), early)
     received[0], coeffs = lax.optimization_barrier((received[0], coeffs))
     own, *rest = exchange_rows(synthesise(me, turned, coeffs, late), late)
-    return assemble(me, [own, *received, *rest], field.shape)
+    received = [own, *received, *rest]
+    out = assemble(me, received[:LATE], PARTNERS[:LATE], field.shape)
+    out = assemble(me, received[LATE:], PARTNERS[LATE:], field.shape, out)
+    return out.reshape(field.shape)
 
 
 def general(field, coef, table, order_ids, inverses, degree_owner):
@@ -466,7 +509,7 @@
         and inverses.shape[0] >= HELD
         and inverses.shape[1] % (2 * LANES) == 0
         and radii_dev == LANES
-        and lats % 16 == 0
+        and lats % LANES in (0, LANES // 2)
         and inverses.shape[0] % 16 == 0
         and table.shape[1] % 256 == 0
     )

time: 113 us -> 112 us (level)
  waiting for transfers between devices: 14.3 us -> 12.1 us
  Pallas kernels: 21.2 us -> 22.8 us
    ppermute x14, waiting for transfers between devices: 14.3 us -> 12.1 us  [exchange_rows(): lax.ppermute(block, 'row', [(a, a ^ j) for a in range(n)])]
    pallas_call x1 -> x3, Pallas kernels: 1.29 us -> 3.32 us  [the longest x2 2 us: assemble(): pl.pallas_call(functools.partial(assemble_kernel, members, partners), out...]
  transfers between devices with their start and end apart: 14 -> 14, of which waited for: 7 -> 6; matrix products, arithmetic and copies ran while one was open for 0% -> 0% of each run, Pallas kernels for 11% -> 13%
where the time goes in v6:
time: 112 us
  blocking collectives  59.8 us (53%)
  Pallas kernels  22.8 us (20%)
  starting transfers between devices  16.4 us (15%)
  waiting for transfers between devices  12.1 us (11%)
    all_to_all x2, blocking collectives, exchange_degrees(): lax.all_to_all(blocks, ('row', 'col'), split_axis=0, concat_axis=0, tiled...  59.8 us
    ppermute x14, starting transfers between devices, exchange_rows(): lax.ppermute(block, 'row', [(a, a ^ j) for a in range(n)])  16.4 us
    ppermute x14, waiting for transfers between devices, exchange_rows(): lax.ppermute(block, 'row', [(a, a ^ j) for a in range(n)])  12.1 us
    pallas_call x1, Pallas kernels, place(): pl.pallas_call(place_kernel, out_shape=[jax.ShapeDtypeStruct((degrees, la...  5.36 us
    pallas_call x1, Pallas kernels, turn(): pl.pallas_call(turn_kernel, out_shape=[pltpu.HBM(turned, BF16), pltpu.VME...  4.77 us
    pallas_call x1, Pallas kernels, solve(): pl.pallas_call(functools.partial(solve_kernel, orders, shards, members),...  3.48 us
  transfers between devices with their start and end apart: 14, of which 6 were waited for; matrix products, arithmetic and copies ran while one was open for 0% of the time, Pallas kernels for 13%

profile of v6, /device:TPU:0, one launch (start us, length us, event | category | flops | bytes accessed | tf_op | source)
XLA Modules:
  0.0 111.9 jit_solution(5316183806324959359)
XLA Ops:
  0.0 2.0 %shard_map.65 = (bf16[192,512]{1,0:T(8,128)(2,1)S(1)}, bf16[192,512]{1,0:T(8,128)(2,1)S(1)}, bf16[192,512]{1,0:T(8,128)(2,1)S(1)}, bf16[192,512]{1,0:T(8,128)(2,...) custom-call(s32[1]{0:T(128)} %bitcast.me_ref, ...), custom_call_target="tpu_custom_call" | custom-call | flops 786432 | bytes 3145728 | tf_op jit(solution)/shard_map/pallas_call | solution.py:96
  2.0 4.0 %collective-permute-start = (bf16[192,512]{1,0:T(8,128)(2,1)S(1)}, bf16[192,512]{1,0:T(8,128)(2,1)S(1)}, u32[]{:S(2)}, u32[]{:S(2)}) collective-permute-start(bf16[192,512]{1,0:T(8,128)(2,1)S(1)} %get-tuple-element.43), channel_id=1, source_target_pairs={{0,24},{4,28},{8,16},{12,20},{16,8},{20,12},{24,0},{28,4},{1,25},{... | collective-permute-start | bytes 589832 | tf_op jit(solution)/shard_map/ppermute | solution.py:413
  6.0 0.5 collective-permute-start.1
  6.5 0.1 collective-permute-start.2
  6.6 1.4 %collective-permute-start.3 = (bf16[192,512]{1,0:T(8,128)(2,1)S(1)}, bf16[192,512]{1,0:T(8,128)(2,1)S(1)}, u32[]{:S(2)}, u32[]{:S(2)}) collective-permute-start(bf16[192,512]{1,0:T(8,128)(2,1)S(1)} %get-tuple-element.46), channel_id=1, source_target_pairs={{0,28},{4,24},{8,20},{12,16},{16,12},{20,8},{24,4},{28,0},{1,29},{... | collective-permute-start | bytes 589832 | tf_op jit(solution)/shard_map/ppermute | solution.py:413
  8.1 1.5 %collective-permute-start.4 = (bf16[192,512]{1,0:T(8,128)(2,1)S(1)}, bf16[192,512]{1,0:T(8,128)(2,1)S(1)}, u32[]{:S(2)}, u32[]{:S(2)}) collective-permute-start(bf16[192,512]{1,0:T(8,128)(2,1)S(1)} %get-tuple-element.47), channel_id=1, source_target_pairs={{0,4},{4,0},{8,12},{12,8},{16,20},{20,16},{24,28},{28,24},{1,5},{5... | collective-permute-start | bytes 589832 | tf_op jit(solution)/shard_map/ppermute | solution.py:413
  10.2 5.4 %shard_map.64 = (bf16[1024,1536]{1,0:T(8,128)(2,1)S(1)}, bf16[16,512,512]{2,1,0:T(8,128)(2,1)S(1)}) custom-call(s32[1]{0:T(128)S(6)} %copy.9.order_ref, bf16[1024,1536]{1,0:T(8,128)(2,1)} %bitcast.14, s32[1,1024]{1,0:T(1,128)} %bitcast.16, bf16[32,512,512]{2,1,0:T(8,128)(2,1)} %inv_hbm.5), custom_call_target="tpu_custom_call" | custom-call | flops 3221225472 | bytes 6291456 | tf_op jit(solution)/shard_map/pallas_call | solution.py:195
  15.6 0.0 collective-permute-done.rest_1_
  15.6 0.2 collective-permute-start.5
  15.8 0.7 collective-permute-done.1.rest_2_
  16.5 4.8 %shard_map.66 = (bf16[1536,1024]{1,0:T(8,128)(2,1)}, bf16[28,512,512]{2,1,0:T(8,128)(2,1)S(1)}) custom-call(bf16[1024,1536]{1,0:T(8,128)(2,1)S(1)} %get-tuple-element.36.table_ref, bf16[16,512,512]{2,1,0:T(8,128)(2,1)S(1)} %get-tuple-element.37.raw_ref, bf16[32,512,512]{2,1,0:T(8,128)(2,1)} %inv_hbm.5), custom_call_target="tpu_custom_call" | custom-call | flops 1572864 | bytes 39845888 | tf_op jit(solution)/shard_map/pallas_call | solution.py:263
  21.4 1.9 %shard_map.67.sums_ref = f32[1024,512]{1,0:T(8,128)S(1)} custom-call(s32[1]{0:T(128)} %bitcast.me_ref, bf16[1024,1536]{1,0:T(8,128)(2,1)S(1)} %get-tuple-element.36.table_ref, bf16[192,512]{1,0:T(8,128)(2,1)S(1)} %get-tuple-element.42.rest_0_, bf16[192,512]{1,0:T(8,128)(2,1)S(1)} %collective-permute-done.rest_1_, ...), custom_call_target="tpu_custom_call" | custom-call | flops 1610612736 | bytes 3145728 | tf_op jit(solution)/shard_map/pallas_call | solution.py:131
  23.3 0.7 collective-permute-done.6.refs_1_
  24.0 1.3 %shard_map.68 = bf16[1024,512]{1,0:T(8,128)(2,1)S(1)} custom-call(s32[1]{0:T(128)} %bitcast.me_ref, bf16[1024,1536]{1,0:T(8,128)(2,1)S(1)} %get-tuple-element.36.table_ref, f32[1024,512]{1,0:T(8,128)S(1)} %shard_map.67.sums_ref, bf16[192,512]{1,0:T(8,128)(2,1)S(1)} %collective-permute-done.5.refs_0_, bf16[192,512]{1,0:T(8,128)(2,1)S(1)} %collective-permute-done.6.refs_1_), custom_call_target="tpu_custom_call" | custom-call | flops 805306368 | bytes 1572864 | tf_op jit(solution)/shard_map/pallas_call | solution.py:162
  25.3 30.5 %all_to_all.10 = bf16[32,32,512]{2,1,0:T(8,128)(2,1)S(1)} all-to-all(bf16[32,32,512]{2,1,0:T(8,128)(2,1)S(1)} %bitcast.13), channel_id=1, replica_groups=mesh['row'=8,'col'=4] {'row','col'}, dimensions={0} | all-to-all | bytes 2097152 | tf_op jit(solution)/shard_map/all_to_all | solution.py:419
  55.8 3.5 %shard_map.69 = bf16[1024,512]{1,0:T(8,128)(2,1)S(1)} custom-call(bf16[1024,512]{1,0:T(8,128)(2,1)S(1)} %bitcast.11, bf16[28,512,512]{2,1,0:T(8,128)(2,1)S(1)} %get-tuple-element.50.here_ref, bf16[32,512,512]{2,1,0:T(8,128)(2,1)} %inv_hbm.5), custom_call_target="tpu_custom_call" | custom-call | flops 536870912 | bytes 8388608 | tf_op jit(solution)/shard_map/pallas_call | solution.py:338
  59.3 29.3 %all_to_all.11 = bf16[32,32,512]{2,1,0:T(8,128)(2,1)S(1)} all-to-all(bf16[32,32,512]{2,1,0:T(8,128)(2,1)S(1)} %bitcast.12), channel_id=1, replica_groups=mesh['row'=8,'col'=4] {'row','col'}, dimensions={0} | all-to-all | bytes 2097152 | tf_op jit(solution)/shard_map/all_to_all | solution.py:419
  88.6 1.0 shard_map.70
  89.6 2.5 %collective-permute-start.7 = (bf16[192,512]{1,0:T(8,128)(2,1)S(1)}, bf16[192,512]{1,0:T(8,128)(2,1)S(1)}, u32[]{:S(2)}, u32[]{:S(2)}) collective-permute-start(bf16[192,512]{1,0:T(8,128)(2,1)S(1)} %get-tuple-element.51), channel_id=1, source_target_pairs={{0,24},{4,28},{8,16},{12,20},{16,8},{20,12},{24,0},{28,4},{1,25},{... | collective-permute-start | bytes 589832 | tf_op jit(solution)/shard_map/ppermute | solution.py:413
  92.1 0.5 collective-permute-start.8
  92.6 0.5 collective-permute-start.9
  93.2 1.8 %collective-permute-start.10 = (bf16[192,512]{1,0:T(8,128)(2,1)S(1)}, bf16[192,512]{1,0:T(8,128)(2,1)S(1)}, u32[]{:S(2)}, u32[]{:S(2)}) collective-permute-start(bf16[192,512]{1,0:T(8,128)(2,1)S(1)} %get-tuple-element.57), channel_id=1, source_target_pairs={{0,28},{4,24},{8,20},{12,16},{16,12},{20,8},{24,4},{28,0},{1,29},{... | collective-permute-start | bytes 589832 | tf_op jit(solution)/shard_map/ppermute | solution.py:413
  94.9 3.0 %collective-permute-done.7.rest_1_ = bf16[192,512]{1,0:T(8,128)(2,1)S(1)} collective-permute-done((bf16[192,512]{1,0:T(8,128)(2,1)S(1)}, bf16[192,512]{1,0:T(8,128)(2,1)S(1)}, u32[]{:S(2)}, u32[]{:S(2)}) %collective-permute-start.7) | collective-permute-done | bytes 196640 | tf_op jit(solution)/shard_map/ppermute | solution.py:413
  97.9 1.0 shard_map.71
  98.9 0.8 collective-permute-start.11
  99.7 1.2 %collective-permute-start.12 = (bf16[192,512]{1,0:T(8,128)(2,1)S(1)}, bf16[192,512]{1,0:T(8,128)(2,1)S(1)}, u32[]{:S(2)}, u32[]{:S(2)}) collective-permute-start(bf16[192,512]{1,0:T(8,128)(2,1)S(1)} %get-tuple-element.59), channel_id=1, source_target_pairs={{0,12},{4,8},{8,4},{12,0},{16,28},{20,24},{24,20},{28,16},{1,13},{... | collective-permute-start | bytes 589832 | tf_op jit(solution)/shard_map/ppermute | solution.py:413
  100.9 1.1 %collective-permute-done.8.rest_2_ = bf16[192,512]{1,0:T(8,128)(2,1)S(1)} collective-permute-done((bf16[192,512]{1,0:T(8,128)(2,1)S(1)}, bf16[192,512]{1,0:T(8,128)(2,1)S(1)}, u32[]{:S(2)}, u32[]{:S(2)}) %collective-permute-start.8) | collective-permute-done | bytes 196640 | tf_op jit(solution)/shard_map/ppermute | solution.py:413
  102.1 1.3 %collective-permute-start.13 = (bf16[192,512]{1,0:T(8,128)(2,1)S(1)}, bf16[192,512]{1,0:T(8,128)(2,1)S(1)}, u32[]{:S(2)}, u32[]{:S(2)}) collective-permute-start(bf16[192,512]{1,0:T(8,128)(2,1)S(1)} %get-tuple-element.60), channel_id=1, source_target_pairs={{0,20},{4,16},{8,28},{12,24},{16,4},{20,0},{24,12},{28,8},{1,21},{... | collective-permute-start | bytes 589832 | tf_op jit(solution)/shard_map/ppermute | solution.py:413
  103.4 3.9 %collective-permute-done.10.rest_4_ = bf16[192,512]{1,0:T(8,128)(2,1)S(1)} collective-permute-done((bf16[192,512]{1,0:T(8,128)(2,1)S(1)}, bf16[192,512]{1,0:T(8,128)(2,1)S(1)}, u32[]{:S(2)}, u32[]{:S(2)}) %collective-permute-start.10) | collective-permute-done | bytes 196640 | tf_op jit(solution)/shard_map/ppermute | solution.py:413
  107.3 1.1 %shard_map.72.rest_0_ = bf16[6144,128]{1,0:T(8,128)(2,1)} custom-call(s32[1]{0:T(128)} %bitcast.me_ref, bf16[192,512]{1,0:T(8,128)(2,1)S(1)} %get-tuple-element.53.rest_0_, bf16[192,512]{1,0:T(8,128)(2,1)S(1)} %collective-permute-done.7.rest_1_, bf16[192,512]{1,0:T(8,128)(2,1)S(1)} %collective-permute-done.8.rest_2_, ...), custom_call_target="tpu_custom_call" | custom-call | flops 589824 | bytes 2359296 | tf_op jit(solution)/shard_map/pallas_call | solution.py:394
  108.5 2.6 %collective-permute-done.12.rest_1_ = bf16[192,512]{1,0:T(8,128)(2,1)S(1)} collective-permute-done((bf16[192,512]{1,0:T(8,128)(2,1)S(1)}, bf16[192,512]{1,0:T(8,128)(2,1)S(1)}, u32[]{:S(2)}, u32[]{:S(2)}) %collective-permute-start.12) | collective-permute-done | bytes 196640 | tf_op jit(solution)/shard_map/ppermute | solution.py:413
  111.1 0.9 shard_map.73
  (10 shorter events, 0.0 us)
Async XLA Ops:
  2.0 13.6 %collective-permute-start = (bf16[192,512]{1,0:T(8,128)(2,1)S(1)}, bf16[192,512]{1,0:T(8,128)(2,1)S(1)}, u32[]{:S(2)}, u32[]{:S(2)}) collective-permute-start(bf16[192,512]{1,0:T(8,128)(2,1)S(1)} %get-tuple-element.43), channel_id=1, source_target_pairs={{0,24},{4,28},{8,16},{12,20},{16,8},{20,12},{24,0},{28,4},{1,25},{... | collective-permute-start | bytes 589832 | tf_op jit(solution)/shard_map/ppermute | solution.py:413
  6.0 10.6 %collective-permute-start.1 = (bf16[192,512]{1,0:T(8,128)(2,1)S(1)}, bf16[192,512]{1,0:T(8,128)(2,1)S(1)}, u32[]{:S(2)}, u32[]{:S(2)}) collective-permute-start(bf16[192,512]{1,0:T(8,128)(2,1)S(1)} %get-tuple-element.44), channel_id=1, source_target_pairs={{0,8},{4,12},{8,0},{12,4},{16,24},{20,28},{24,16},{28,20},{1,9},{5... | collective-permute-start | bytes 589832 | tf_op jit(solution)/shard_map/ppermute | solution.py:413
  6.5 14.8 %collective-permute-start.2 = (bf16[192,512]{1,0:T(8,128)(2,1)S(1)}, bf16[192,512]{1,0:T(8,128)(2,1)S(1)}, u32[]{:S(2)}, u32[]{:S(2)}) collective-permute-start(bf16[192,512]{1,0:T(8,128)(2,1)S(1)} %get-tuple-element.45), channel_id=1, source_target_pairs={{0,16},{4,20},{8,24},{12,28},{16,0},{20,4},{24,8},{28,12},{1,17},{... | collective-permute-start | bytes 589832 | tf_op jit(solution)/shard_map/ppermute | solution.py:413
  6.6 14.7 %collective-permute-start.3 = (bf16[192,512]{1,0:T(8,128)(2,1)S(1)}, bf16[192,512]{1,0:T(8,128)(2,1)S(1)}, u32[]{:S(2)}, u32[]{:S(2)}) collective-permute-start(bf16[192,512]{1,0:T(8,128)(2,1)S(1)} %get-tuple-element.46), channel_id=1, source_target_pairs={{0,28},{4,24},{8,20},{12,16},{16,12},{20,8},{24,4},{28,0},{1,29},{... | collective-permute-start | bytes 589832 | tf_op jit(solution)/shard_map/ppermute | solution.py:413
  8.1 13.3 %collective-permute-start.4 = (bf16[192,512]{1,0:T(8,128)(2,1)S(1)}, bf16[192,512]{1,0:T(8,128)(2,1)S(1)}, u32[]{:S(2)}, u32[]{:S(2)}) collective-permute-start(bf16[192,512]{1,0:T(8,128)(2,1)S(1)} %get-tuple-element.47), channel_id=1, source_target_pairs={{0,4},{4,0},{8,12},{12,8},{16,20},{20,16},{24,28},{28,24},{1,5},{5... | collective-permute-start | bytes 589832 | tf_op jit(solution)/shard_map/ppermute | solution.py:413
  15.6 7.6 %collective-permute-start.5 = (bf16[192,512]{1,0:T(8,128)(2,1)S(1)}, bf16[192,512]{1,0:T(8,128)(2,1)S(1)}, u32[]{:S(2)}, u32[]{:S(2)}) collective-permute-start(bf16[192,512]{1,0:T(8,128)(2,1)S(1)} %get-tuple-element.48), channel_id=1, source_target_pairs={{0,12},{4,8},{8,4},{12,0},{16,28},{20,24},{24,20},{28,16},{1,13},{... | collective-permute-start | bytes 589832 | tf_op jit(solution)/shard_map/ppermute | solution.py:413
  16.5 7.4 %collective-permute-start.6 = (bf16[192,512]{1,0:T(8,128)(2,1)S(1)}, bf16[192,512]{1,0:T(8,128)(2,1)S(1)}, u32[]{:S(2)}, u32[]{:S(2)}) collective-permute-start(bf16[192,512]{1,0:T(8,128)(2,1)S(1)} %get-tuple-element.49), channel_id=1, source_target_pairs={{0,20},{4,16},{8,28},{12,24},{16,4},{20,0},{24,12},{28,8},{1,21},{... | collective-permute-start | bytes 589832 | tf_op jit(solution)/shard_map/ppermute | solution.py:413
  55.8 32.8 %copy-start = (bf16[1536,1024]{1,0:T(8,128)(2,1)S(1)}, bf16[1536,1024]{1,0:T(8,128)(2,1)}, u32[]{:S(2)}) copy-start(bf16[1536,1024]{1,0:T(8,128)(2,1)} %get-tuple-element.41.turned_ref) | copy-start | bytes 9437188
  89.6 8.3 %collective-permute-start.7 = (bf16[192,512]{1,0:T(8,128)(2,1)S(1)}, bf16[192,512]{1,0:T(8,128)(2,1)S(1)}, u32[]{:S(2)}, u32[]{:S(2)}) collective-permute-start(bf16[192,512]{1,0:T(8,128)(2,1)S(1)} %get-tuple-element.51), channel_id=1, source_target_pairs={{0,24},{4,28},{8,16},{12,20},{16,8},{20,12},{24,0},{28,4},{1,25},{... | collective-permute-start | bytes 589832 | tf_op jit(solution)/shard_map/ppermute | solution.py:413
  92.1 10.0 %collective-permute-start.8 = (bf16[192,512]{1,0:T(8,128)(2,1)S(1)}, bf16[192,512]{1,0:T(8,128)(2,1)S(1)}, u32[]{:S(2)}, u32[]{:S(2)}) collective-permute-start(bf16[192,512]{1,0:T(8,128)(2,1)S(1)} %get-tuple-element.55), channel_id=1, source_target_pairs={{0,8},{4,12},{8,0},{12,4},{16,24},{20,28},{24,16},{28,20},{1,9},{5... | collective-permute-start | bytes 589832 | tf_op jit(solution)/shard_map/ppermute | solution.py:413
  92.6 10.8 %collective-permute-start.9 = (bf16[192,512]{1,0:T(8,128)(2,1)S(1)}, bf16[192,512]{1,0:T(8,128)(2,1)S(1)}, u32[]{:S(2)}, u32[]{:S(2)}) collective-permute-start(bf16[192,512]{1,0:T(8,128)(2,1)S(1)} %get-tuple-element.56), channel_id=1, source_target_pairs={{0,16},{4,20},{8,24},{12,28},{16,0},{20,4},{24,8},{28,12},{1,17},{... | collective-permute-start | bytes 589832 | tf_op jit(solution)/shard_map/ppermute | solution.py:413
  93.2 14.1 %collective-permute-start.10 = (bf16[192,512]{1,0:T(8,128)(2,1)S(1)}, bf16[192,512]{1,0:T(8,128)(2,1)S(1)}, u32[]{:S(2)}, u32[]{:S(2)}) collective-permute-start(bf16[192,512]{1,0:T(8,128)(2,1)S(1)} %get-tuple-element.57), channel_id=1, source_target_pairs={{0,28},{4,24},{8,20},{12,16},{16,12},{20,8},{24,4},{28,0},{1,29},{... | collective-permute-start | bytes 589832 | tf_op jit(solution)/shard_map/ppermute | solution.py:413
  98.9 8.4 %collective-permute-start.11 = (bf16[192,512]{1,0:T(8,128)(2,1)S(1)}, bf16[192,512]{1,0:T(8,128)(2,1)S(1)}, u32[]{:S(2)}, u32[]{:S(2)}) collective-permute-start(bf16[192,512]{1,0:T(8,128)(2,1)S(1)} %get-tuple-element.58), channel_id=1, source_target_pairs={{0,4},{4,0},{8,12},{12,8},{16,20},{20,16},{24,28},{28,24},{1,5},{5... | collective-permute-start | bytes 589832 | tf_op jit(solution)/shard_map/ppermute | solution.py:413
  99.7 11.3 %collective-permute-start.12 = (bf16[192,512]{1,0:T(8,128)(2,1)S(1)}, bf16[192,512]{1,0:T(8,128)(2,1)S(1)}, u32[]{:S(2)}, u32[]{:S(2)}) collective-permute-start(bf16[192,512]{1,0:T(8,128)(2,1)S(1)} %get-tuple-element.59), channel_id=1, source_target_pairs={{0,12},{4,8},{8,4},{12,0},{16,28},{20,24},{24,20},{28,16},{1,13},{... | collective-permute-start | bytes 589832 | tf_op jit(solution)/shard_map/ppermute | solution.py:413
  102.1 9.0 %collective-permute-start.13 = (bf16[192,512]{1,0:T(8,128)(2,1)S(1)}, bf16[192,512]{1,0:T(8,128)(2,1)S(1)}, u32[]{:S(2)}, u32[]{:S(2)}) collective-permute-start(bf16[192,512]{1,0:T(8,128)(2,1)S(1)} %get-tuple-element.60), channel_id=1, source_target_pairs={{0,20},{4,16},{8,28},{12,24},{16,4},{20,0},{24,12},{28,8},{1,21},{... | collective-permute-start | bytes 589832 | tf_op jit(solution)/shard_map/ppermute | solution.py:413

commit v7 on v6

--- a/solution.py
+++ b/solution.py
@@ -15,7 +15,7 @@
 BESIDE = 0
 FIRST = 5
 LATE = 6
-PARTNERS = (0, 6, 2, 4, 7, 1, 3, 5)
+PARTNERS = (0, 6, 7, 2, 4, 1, 3, 5)
 MIB = 1024 * 1024
 BF16 = jnp.bfloat16
 F32 = jnp.float32

time: 112 us -> 112 us (level)
  no operation moved by 1% of the time
where the time goes in v7:
time: 112 us
  blocking collectives  59.6 us (53%)
  Pallas kernels  22.8 us (20%)
  starting transfers between devices  17.3 us (15%)
  waiting for transfers between devices  11.4 us (10%)
    all_to_all x2, blocking collectives, exchange_degrees(): lax.all_to_all(blocks, ('row', 'col'), split_axis=0, concat_axis=0, tiled...  59.6 us
    ppermute x14, starting transfers between devices, exchange_rows(): lax.ppermute(block, 'row', [(a, a ^ j) for a in range(n)])  17.3 us
    ppermute x14, waiting for transfers between devices, exchange_rows(): lax.ppermute(block, 'row', [(a, a ^ j) for a in range(n)])  11.4 us
    pallas_call x1, Pallas kernels, place(): pl.pallas_call(place_kernel, out_shape=[jax.ShapeDtypeStruct((degrees, la...  5.36 us
    pallas_call x1, Pallas kernels, turn(): pl.pallas_call(turn_kernel, out_shape=[pltpu.HBM(turned, BF16), pltpu.VME...  4.77 us
    pallas_call x1, Pallas kernels, solve(): pl.pallas_call(functools.partial(solve_kernel, orders, shards, members),...  3.48 us
  transfers between devices with their start and end apart: 14, of which 6 were waited for; matrix products, arithmetic and copies ran while one was open for 0% of the time, Pallas kernels for 13%

profile of v7, /device:TPU:0, one launch (start us, length us, event | category | flops | bytes accessed | tf_op | source)
XLA Modules:
  0.0 111.8 jit_solution(10873117818486350453)
XLA Ops:
  0.0 2.0 %shard_map.65 = (bf16[192,512]{1,0:T(8,128)(2,1)S(1)}, bf16[192,512]{1,0:T(8,128)(2,1)S(1)}, bf16[192,512]{1,0:T(8,128)(2,1)S(1)}, bf16[192,512]{1,0:T(8,128)(2,...) custom-call(s32[1]{0:T(128)} %bitcast.me_ref, ...), custom_call_target="tpu_custom_call" | custom-call | flops 786432 | bytes 3145728 | tf_op jit(solution)/shard_map/pallas_call | solution.py:96
  2.0 4.0 %collective-permute-start = (bf16[192,512]{1,0:T(8,128)(2,1)S(1)}, bf16[192,512]{1,0:T(8,128)(2,1)S(1)}, u32[]{:S(2)}, u32[]{:S(2)}) collective-permute-start(bf16[192,512]{1,0:T(8,128)(2,1)S(1)} %get-tuple-element.43), channel_id=1, source_target_pairs={{0,24},{4,28},{8,16},{12,20},{16,8},{20,12},{24,0},{28,4},{1,25},{... | collective-permute-start | bytes 589832 | tf_op jit(solution)/shard_map/ppermute | solution.py:413
  6.0 1.1 %collective-permute-start.2 = (bf16[192,512]{1,0:T(8,128)(2,1)S(1)}, bf16[192,512]{1,0:T(8,128)(2,1)S(1)}, u32[]{:S(2)}, u32[]{:S(2)}) collective-permute-start(bf16[192,512]{1,0:T(8,128)(2,1)S(1)} %get-tuple-element.45), channel_id=1, source_target_pairs={{0,8},{4,12},{8,0},{12,4},{16,24},{20,28},{24,16},{28,20},{1,9},{5... | collective-permute-start | bytes 589832 | tf_op jit(solution)/shard_map/ppermute | solution.py:413
  7.1 1.5 %collective-permute-start.3 = (bf16[192,512]{1,0:T(8,128)(2,1)S(1)}, bf16[192,512]{1,0:T(8,128)(2,1)S(1)}, u32[]{:S(2)}, u32[]{:S(2)}) collective-permute-start(bf16[192,512]{1,0:T(8,128)(2,1)S(1)} %get-tuple-element.46), channel_id=1, source_target_pairs={{0,16},{4,20},{8,24},{12,28},{16,0},{20,4},{24,8},{28,12},{1,17},{... | collective-permute-start | bytes 589832 | tf_op jit(solution)/shard_map/ppermute | solution.py:413
  8.6 0.4 collective-permute-start.4
  9.7 5.4 %shard_map.64 = (bf16[1024,1536]{1,0:T(8,128)(2,1)S(1)}, bf16[16,512,512]{2,1,0:T(8,128)(2,1)S(1)}) custom-call(s32[1]{0:T(128)S(6)} %copy.9.order_ref, bf16[1024,1536]{1,0:T(8,128)(2,1)} %bitcast.14, s32[1,1024]{1,0:T(1,128)} %bitcast.16, bf16[32,512,512]{2,1,0:T(8,128)(2,1)} %inv_hbm.5), custom_call_target="tpu_custom_call" | custom-call | flops 3221225472 | bytes 6291456 | tf_op jit(solution)/shard_map/pallas_call | solution.py:195
  15.1 0.3 collective-permute-start.5
  15.4 0.2 collective-permute-done.1.rest_2_
  15.5 1.9 %collective-permute-start.6 = (bf16[192,512]{1,0:T(8,128)(2,1)S(1)}, bf16[192,512]{1,0:T(8,128)(2,1)S(1)}, u32[]{:S(2)}, u32[]{:S(2)}) collective-permute-start(bf16[192,512]{1,0:T(8,128)(2,1)S(1)} %get-tuple-element.49), channel_id=1, source_target_pairs={{0,20},{4,16},{8,28},{12,24},{16,4},{20,0},{24,12},{28,8},{1,21},{... | collective-permute-start | bytes 589832 | tf_op jit(solution)/shard_map/ppermute | solution.py:413
  17.4 4.8 %shard_map.66 = (bf16[1536,1024]{1,0:T(8,128)(2,1)}, bf16[28,512,512]{2,1,0:T(8,128)(2,1)S(1)}) custom-call(bf16[1024,1536]{1,0:T(8,128)(2,1)S(1)} %get-tuple-element.36.table_ref, bf16[16,512,512]{2,1,0:T(8,128)(2,1)S(1)} %get-tuple-element.37.raw_ref, bf16[32,512,512]{2,1,0:T(8,128)(2,1)} %inv_hbm.5), custom_call_target="tpu_custom_call" | custom-call | flops 1572864 | bytes 39845888 | tf_op jit(solution)/shard_map/pallas_call | solution.py:263
  22.2 0.0 collective-permute-done.3.rest_4_
  22.2 1.9 %shard_map.67.sums_ref = f32[1024,512]{1,0:T(8,128)S(1)} custom-call(s32[1]{0:T(128)} %bitcast.me_ref, bf16[1024,1536]{1,0:T(8,128)(2,1)S(1)} %get-tuple-element.36.table_ref, bf16[192,512]{1,0:T(8,128)(2,1)S(1)} %get-tuple-element.42.rest_0_, bf16[192,512]{1,0:T(8,128)(2,1)S(1)} %collective-permute-done.rest_1_, ...), custom_call_target="tpu_custom_call" | custom-call | flops 1610612736 | bytes 3145728 | tf_op jit(solution)/shard_map/pallas_call | solution.py:131
  24.2 1.3 %shard_map.68 = bf16[1024,512]{1,0:T(8,128)(2,1)S(1)} custom-call(s32[1]{0:T(128)} %bitcast.me_ref, bf16[1024,1536]{1,0:T(8,128)(2,1)S(1)} %get-tuple-element.36.table_ref, f32[1024,512]{1,0:T(8,128)S(1)} %shard_map.67.sums_ref, bf16[192,512]{1,0:T(8,128)(2,1)S(1)} %collective-permute-done.5.refs_0_, bf16[192,512]{1,0:T(8,128)(2,1)S(1)} %collective-permute-done.6.refs_1_), custom_call_target="tpu_custom_call" | custom-call | flops 805306368 | bytes 1572864 | tf_op jit(solution)/shard_map/pallas_call | solution.py:162
  25.5 30.3 %all_to_all.10 = bf16[32,32,512]{2,1,0:T(8,128)(2,1)S(1)} all-to-all(bf16[32,32,512]{2,1,0:T(8,128)(2,1)S(1)} %bitcast.13), channel_id=1, replica_groups=mesh['row'=8,'col'=4] {'row','col'}, dimensions={0} | all-to-all | bytes 2097152 | tf_op jit(solution)/shard_map/all_to_all | solution.py:419
  55.7 3.5 %shard_map.69 = bf16[1024,512]{1,0:T(8,128)(2,1)S(1)} custom-call(bf16[1024,512]{1,0:T(8,128)(2,1)S(1)} %bitcast.11, bf16[28,512,512]{2,1,0:T(8,128)(2,1)S(1)} %get-tuple-element.50.here_ref, bf16[32,512,512]{2,1,0:T(8,128)(2,1)} %inv_hbm.5), custom_call_target="tpu_custom_call" | custom-call | flops 536870912 | bytes 8388608 | tf_op jit(solution)/shard_map/pallas_call | solution.py:338
  59.2 29.3 %all_to_all.11 = bf16[32,32,512]{2,1,0:T(8,128)(2,1)S(1)} all-to-all(bf16[32,32,512]{2,1,0:T(8,128)(2,1)S(1)} %bitcast.12), channel_id=1, replica_groups=mesh['row'=8,'col'=4] {'row','col'}, dimensions={0} | all-to-all | bytes 2097152 | tf_op jit(solution)/shard_map/all_to_all | solution.py:419
  88.5 1.0 shard_map.70
  89.5 2.5 %collective-permute-start.7 = (bf16[192,512]{1,0:T(8,128)(2,1)S(1)}, bf16[192,512]{1,0:T(8,128)(2,1)S(1)}, u32[]{:S(2)}, u32[]{:S(2)}) collective-permute-start(bf16[192,512]{1,0:T(8,128)(2,1)S(1)} %get-tuple-element.51), channel_id=1, source_target_pairs={{0,24},{4,28},{8,16},{12,20},{16,8},{20,12},{24,0},{28,4},{1,25},{... | collective-permute-start | bytes 589832 | tf_op jit(solution)/shard_map/ppermute | solution.py:413
  92.0 1.4 %collective-permute-start.8 = (bf16[192,512]{1,0:T(8,128)(2,1)S(1)}, bf16[192,512]{1,0:T(8,128)(2,1)S(1)}, u32[]{:S(2)}, u32[]{:S(2)}) collective-permute-start(bf16[192,512]{1,0:T(8,128)(2,1)S(1)} %get-tuple-element.55), channel_id=1, source_target_pairs={{0,28},{4,24},{8,20},{12,16},{16,12},{20,8},{24,4},{28,0},{1,29},{... | collective-permute-start | bytes 589832 | tf_op jit(solution)/shard_map/ppermute | solution.py:413
  93.4 1.5 %collective-permute-start.9 = (bf16[192,512]{1,0:T(8,128)(2,1)S(1)}, bf16[192,512]{1,0:T(8,128)(2,1)S(1)}, u32[]{:S(2)}, u32[]{:S(2)}) collective-permute-start(bf16[192,512]{1,0:T(8,128)(2,1)S(1)} %get-tuple-element.56), channel_id=1, source_target_pairs={{0,8},{4,12},{8,0},{12,4},{16,24},{20,28},{24,16},{28,20},{1,9},{5... | collective-permute-start | bytes 589832 | tf_op jit(solution)/shard_map/ppermute | solution.py:413
  94.9 0.5 collective-permute-start.10
  95.4 2.4 %collective-permute-done.7.rest_1_ = bf16[192,512]{1,0:T(8,128)(2,1)S(1)} collective-permute-done((bf16[192,512]{1,0:T(8,128)(2,1)S(1)}, bf16[192,512]{1,0:T(8,128)(2,1)S(1)}, u32[]{:S(2)}, u32[]{:S(2)}) %collective-permute-start.7) | collective-permute-done | bytes 196640 | tf_op jit(solution)/shard_map/ppermute | solution.py:413
  97.9 1.0 shard_map.71
  98.8 0.9 collective-permute-start.11
  99.8 1.2 %collective-permute-start.12 = (bf16[192,512]{1,0:T(8,128)(2,1)S(1)}, bf16[192,512]{1,0:T(8,128)(2,1)S(1)}, u32[]{:S(2)}, u32[]{:S(2)}) collective-permute-start(bf16[192,512]{1,0:T(8,128)(2,1)S(1)} %get-tuple-element.59), channel_id=1, source_target_pairs={{0,12},{4,8},{8,4},{12,0},{16,28},{20,24},{24,20},{28,16},{1,13},{... | collective-permute-start | bytes 589832 | tf_op jit(solution)/shard_map/ppermute | solution.py:413
  100.9 2.1 %collective-permute-done.8.rest_2_ = bf16[192,512]{1,0:T(8,128)(2,1)S(1)} collective-permute-done((bf16[192,512]{1,0:T(8,128)(2,1)S(1)}, bf16[192,512]{1,0:T(8,128)(2,1)S(1)}, u32[]{:S(2)}, u32[]{:S(2)}) %collective-permute-start.8) | collective-permute-done | bytes 196640 | tf_op jit(solution)/shard_map/ppermute | solution.py:413
  103.1 0.1 collective-permute-start.13
  103.2 3.0 %collective-permute-done.9.rest_3_ = bf16[192,512]{1,0:T(8,128)(2,1)S(1)} collective-permute-done((bf16[192,512]{1,0:T(8,128)(2,1)S(1)}, bf16[192,512]{1,0:T(8,128)(2,1)S(1)}, u32[]{:S(2)}, u32[]{:S(2)}) %collective-permute-start.9) | collective-permute-done | bytes 196640 | tf_op jit(solution)/shard_map/ppermute | solution.py:413
  106.2 0.6 collective-permute-done.10.rest_4_
  106.8 1.1 %shard_map.72.rest_0_ = bf16[6144,128]{1,0:T(8,128)(2,1)} custom-call(s32[1]{0:T(128)} %bitcast.me_ref, bf16[192,512]{1,0:T(8,128)(2,1)S(1)} %get-tuple-element.53.rest_0_, bf16[192,512]{1,0:T(8,128)(2,1)S(1)} %collective-permute-done.7.rest_1_, bf16[192,512]{1,0:T(8,128)(2,1)S(1)} %collective-permute-done.8.rest_2_, ...), custom_call_target="tpu_custom_call" | custom-call | flops 589824 | bytes 2359296 | tf_op jit(solution)/shard_map/pallas_call | solution.py:394
  108.0 3.0 %collective-permute-done.12.rest_1_ = bf16[192,512]{1,0:T(8,128)(2,1)S(1)} collective-permute-done((bf16[192,512]{1,0:T(8,128)(2,1)S(1)}, bf16[192,512]{1,0:T(8,128)(2,1)S(1)}, u32[]{:S(2)}, u32[]{:S(2)}) %collective-permute-start.12) | collective-permute-done | bytes 196640 | tf_op jit(solution)/shard_map/ppermute | solution.py:413
  111.0 0.9 shard_map.73
  (10 shorter events, 0.0 us)
Async XLA Ops:
  2.0 13.0 %collective-permute-start = (bf16[192,512]{1,0:T(8,128)(2,1)S(1)}, bf16[192,512]{1,0:T(8,128)(2,1)S(1)}, u32[]{:S(2)}, u32[]{:S(2)}) collective-permute-start(bf16[192,512]{1,0:T(8,128)(2,1)S(1)} %get-tuple-element.43), channel_id=1, source_target_pairs={{0,24},{4,28},{8,16},{12,20},{16,8},{20,12},{24,0},{28,4},{1,25},{... | collective-permute-start | bytes 589832 | tf_op jit(solution)/shard_map/ppermute | solution.py:413
  6.0 9.6 %collective-permute-start.1 = (bf16[192,512]{1,0:T(8,128)(2,1)S(1)}, bf16[192,512]{1,0:T(8,128)(2,1)S(1)}, u32[]{:S(2)}, u32[]{:S(2)}) collective-permute-start(bf16[192,512]{1,0:T(8,128)(2,1)S(1)} %get-tuple-element.44), channel_id=1, source_target_pairs={{0,28},{4,24},{8,20},{12,16},{16,12},{20,8},{24,4},{28,0},{1,29},{... | collective-permute-start | bytes 589832 | tf_op jit(solution)/shard_map/ppermute | solution.py:413
  6.0 16.2 %collective-permute-start.2 = (bf16[192,512]{1,0:T(8,128)(2,1)S(1)}, bf16[192,512]{1,0:T(8,128)(2,1)S(1)}, u32[]{:S(2)}, u32[]{:S(2)}) collective-permute-start(bf16[192,512]{1,0:T(8,128)(2,1)S(1)} %get-tuple-element.45), channel_id=1, source_target_pairs={{0,8},{4,12},{8,0},{12,4},{16,24},{20,28},{24,16},{28,20},{1,9},{5... | collective-permute-start | bytes 589832 | tf_op jit(solution)/shard_map/ppermute | solution.py:413
  7.1 15.1 %collective-permute-start.3 = (bf16[192,512]{1,0:T(8,128)(2,1)S(1)}, bf16[192,512]{1,0:T(8,128)(2,1)S(1)}, u32[]{:S(2)}, u32[]{:S(2)}) collective-permute-start(bf16[192,512]{1,0:T(8,128)(2,1)S(1)} %get-tuple-element.46), channel_id=1, source_target_pairs={{0,16},{4,20},{8,24},{12,28},{16,0},{20,4},{24,8},{28,12},{1,17},{... | collective-permute-start | bytes 589832 | tf_op jit(solution)/shard_map/ppermute | solution.py:413
  8.6 13.6 %collective-permute-start.4 = (bf16[192,512]{1,0:T(8,128)(2,1)S(1)}, bf16[192,512]{1,0:T(8,128)(2,1)S(1)}, u32[]{:S(2)}, u32[]{:S(2)}) collective-permute-start(bf16[192,512]{1,0:T(8,128)(2,1)S(1)} %get-tuple-element.47), channel_id=1, source_target_pairs={{0,4},{4,0},{8,12},{12,8},{16,20},{20,16},{24,28},{28,24},{1,5},{5... | collective-permute-start | bytes 589832 | tf_op jit(solution)/shard_map/ppermute | solution.py:413
  15.1 9.1 %collective-permute-start.5 = (bf16[192,512]{1,0:T(8,128)(2,1)S(1)}, bf16[192,512]{1,0:T(8,128)(2,1)S(1)}, u32[]{:S(2)}, u32[]{:S(2)}) collective-permute-start(bf16[192,512]{1,0:T(8,128)(2,1)S(1)} %get-tuple-element.48), channel_id=1, source_target_pairs={{0,12},{4,8},{8,4},{12,0},{16,28},{20,24},{24,20},{28,16},{1,13},{... | collective-permute-start | bytes 589832 | tf_op jit(solution)/shard_map/ppermute | solution.py:413
  15.5 8.6 %collective-permute-start.6 = (bf16[192,512]{1,0:T(8,128)(2,1)S(1)}, bf16[192,512]{1,0:T(8,128)(2,1)S(1)}, u32[]{:S(2)}, u32[]{:S(2)}) collective-permute-start(bf16[192,512]{1,0:T(8,128)(2,1)S(1)} %get-tuple-element.49), channel_id=1, source_target_pairs={{0,20},{4,16},{8,28},{12,24},{16,4},{20,0},{24,12},{28,8},{1,21},{... | collective-permute-start | bytes 589832 | tf_op jit(solution)/shard_map/ppermute | solution.py:413
  55.7 32.8 %copy-start = (bf16[1536,1024]{1,0:T(8,128)(2,1)S(1)}, bf16[1536,1024]{1,0:T(8,128)(2,1)}, u32[]{:S(2)}) copy-start(bf16[1536,1024]{1,0:T(8,128)(2,1)} %get-tuple-element.41.turned_ref) | copy-start | bytes 9437188
  89.5 8.3 %collective-permute-start.7 = (bf16[192,512]{1,0:T(8,128)(2,1)S(1)}, bf16[192,512]{1,0:T(8,128)(2,1)S(1)}, u32[]{:S(2)}, u32[]{:S(2)}) collective-permute-start(bf16[192,512]{1,0:T(8,128)(2,1)S(1)} %get-tuple-element.51), channel_id=1, source_target_pairs={{0,24},{4,28},{8,16},{12,20},{16,8},{20,12},{24,0},{28,4},{1,25},{... | collective-permute-start | bytes 589832 | tf_op jit(solution)/shard_map/ppermute | solution.py:413
  92.0 11.1 %collective-permute-start.8 = (bf16[192,512]{1,0:T(8,128)(2,1)S(1)}, bf16[192,512]{1,0:T(8,128)(2,1)S(1)}, u32[]{:S(2)}, u32[]{:S(2)}) collective-permute-start(bf16[192,512]{1,0:T(8,128)(2,1)S(1)} %get-tuple-element.55), channel_id=1, source_target_pairs={{0,28},{4,24},{8,20},{12,16},{16,12},{20,8},{24,4},{28,0},{1,29},{... | collective-permute-start | bytes 589832 | tf_op jit(solution)/shard_map/ppermute | solution.py:413
  93.4 12.8 %collective-permute-start.9 = (bf16[192,512]{1,0:T(8,128)(2,1)S(1)}, bf16[192,512]{1,0:T(8,128)(2,1)S(1)}, u32[]{:S(2)}, u32[]{:S(2)}) collective-permute-start(bf16[192,512]{1,0:T(8,128)(2,1)S(1)} %get-tuple-element.56), channel_id=1, source_target_pairs={{0,8},{4,12},{8,0},{12,4},{16,24},{20,28},{24,16},{28,20},{1,9},{5... | collective-permute-start | bytes 589832 | tf_op jit(solution)/shard_map/ppermute | solution.py:413
  94.9 11.9 %collective-permute-start.10 = (bf16[192,512]{1,0:T(8,128)(2,1)S(1)}, bf16[192,512]{1,0:T(8,128)(2,1)S(1)}, u32[]{:S(2)}, u32[]{:S(2)}) collective-permute-start(bf16[192,512]{1,0:T(8,128)(2,1)S(1)} %get-tuple-element.57), channel_id=1, source_target_pairs={{0,16},{4,20},{8,24},{12,28},{16,0},{20,4},{24,8},{28,12},{1,17},{... | collective-permute-start | bytes 589832 | tf_op jit(solution)/shard_map/ppermute | solution.py:413
  98.8 8.0 %collective-permute-start.11 = (bf16[192,512]{1,0:T(8,128)(2,1)S(1)}, bf16[192,512]{1,0:T(8,128)(2,1)S(1)}, u32[]{:S(2)}, u32[]{:S(2)}) collective-permute-start(bf16[192,512]{1,0:T(8,128)(2,1)S(1)} %get-tuple-element.58), channel_id=1, source_target_pairs={{0,4},{4,0},{8,12},{12,8},{16,20},{20,16},{24,28},{28,24},{1,5},{5... | collective-permute-start | bytes 589832 | tf_op jit(solution)/shard_map/ppermute | solution.py:413
  99.8 11.2 %collective-permute-start.12 = (bf16[192,512]{1,0:T(8,128)(2,1)S(1)}, bf16[192,512]{1,0:T(8,128)(2,1)S(1)}, u32[]{:S(2)}, u32[]{:S(2)}) collective-permute-start(bf16[192,512]{1,0:T(8,128)(2,1)S(1)} %get-tuple-element.59), channel_id=1, source_target_pairs={{0,12},{4,8},{8,4},{12,0},{16,28},{20,24},{24,20},{28,16},{1,13},{... | collective-permute-start | bytes 589832 | tf_op jit(solution)/shard_map/ppermute | solution.py:413
  103.1 7.9 %collective-permute-start.13 = (bf16[192,512]{1,0:T(8,128)(2,1)S(1)}, bf16[192,512]{1,0:T(8,128)(2,1)S(1)}, u32[]{:S(2)}, u32[]{:S(2)}) collective-permute-start(bf16[192,512]{1,0:T(8,128)(2,1)S(1)} %get-tuple-element.60), channel_id=1, source_target_pairs={{0,20},{4,16},{8,28},{12,24},{16,4},{20,0},{24,12},{28,8},{1,21},{... | collective-permute-start | bytes 589832 | tf_op jit(solution)/shard_map/ppermute | solution.py:413
